TPU v7x, 32 devices: a whole 2x2x4 slice. The times are simulated.
32 devices in a mesh: pole: 2 (over x), row: 4 (over y, core), col: 4 (over z).
Axes of the slice: x: 2, y: 2, z: 4, core: 2. Of those that a mesh axis runs over, the one named last changes fastest.
Arguments:
- inverse_top: bfloat16 [4, 1, 4, 256, 1, 4, 256], P('pole', None, 'row', None, None, 'col'), parts along dimension 0, may hold values from -0.25 to 0.25
- factor: bfloat16 [4, 4, 1, 4, 128, 256], P('col', 'pole', None, 'row'), parts along dimension 1, may hold values from -1.5 to 1.5
- diag_inverse: float32 [4, 4, 256, 256], P('col', 'pole'), parts along dimension 1, may hold values from -12 to 12
- row_lists: int32 [4, 4, 128], replicated, may hold values from 0 to 255, as said below
Outputs:
- inverse_block: float32 [4, 4, 1, 4, 128, 256], P('col', 'pole', None, 'row'), parts along dimension 1
- diagonal_block: float32 [4, 4, 256, 256], P('col', 'pole'), parts along dimension 1
There are 2 independent parts, one for each index of `pole`. A program takes and returns all parts, laid end to end along the dimension named above; an argument that names none is the same for every part. Nothing has to cross between parts.
Inputs may be any that keep to these rules, and one draw needn't show every extreme that they name: `row_lists`: within each supernode and ancestor block the 128 kept positions are distinct and increasing.
All inputs are finite; a program needn't handle non-finite values.
Results may differ from a plain program's by a relative error of at most 0.0003.
Values may be sent and summed in bfloat16 or wider, within the bound.
No kernel may reach another device: no remote copies, remote signals or barrier semaphores. Data moves between devices by JAX's collectives and lax.ppermute only.
A program may use at most 64 MiB of HBM per device.

v0:
```python
import jax
import jax.numpy as jnp
from jax import lax
from jax.sharding import PartitionSpec as P


def complex_wide(first_factor, wide_factor, width):
    real_rows = jnp.dot(first_factor[0], wide_factor, preferred_element_type=jnp.float32)
    imag_rows = jnp.dot(first_factor[1], wide_factor, preferred_element_type=jnp.float32)
    real_part = real_rows[:, :width] - imag_rows[:, width:]
    imag_part = real_rows[:, width:] + imag_rows[:, :width]
    return jnp.stack([real_part, imag_part])


def take_second(matrix, picks):
    return jnp.take(matrix, picks, axis=1)


def local(inverse_top, factor, diag_inverse, row_lists):
    grid_rows = lax.axis_size("row")
    grid_cols = lax.axis_size("col")
    row_place = lax.axis_index("row")
    col_place = lax.axis_index("col")
    local_nodes = factor.shape[0]
    row_blocks = factor.shape[2]
    kept_rows = factor.shape[4]
    node_width = factor.shape[5]
    col_blocks = inverse_top.shape[4]
    total_blocks = row_blocks * grid_rows
    all_nodes = local_nodes * grid_cols
    gathered = lax.all_gather(factor, "row", axis=3, tiled=True)
    grouped = gathered.reshape(
        local_nodes, 2, total_blocks // grid_cols, grid_cols, kept_rows, node_width
    )
    turned = lax.all_to_all(grouped, "col", split_axis=3, concat_axis=0, tiled=True)
    columns_here = turned.reshape(all_nodes, 2, col_blocks, kept_rows, node_width)
    surface = inverse_top.reshape(2, row_blocks, node_width, col_blocks, node_width)
    own_rows = jnp.arange(row_blocks, dtype=jnp.int32) * grid_rows + row_place
    own_cols = jnp.arange(col_blocks, dtype=jnp.int32) * grid_cols + col_place
    positions = jnp.arange(node_width, dtype=jnp.int32)
    block_take = jax.vmap(take_second, in_axes=(1, 0), out_axes=1)

    def expand_factor(supernode):
        col_picks = jnp.take(row_lists[supernode], own_cols, axis=0)
        placing = (positions[None, :, None] == col_picks[:, None, :]).astype(jnp.bfloat16)
        spread = jnp.einsum(
            "jak,cjkb->jacb", placing, columns_here[supernode], preferred_element_type=jnp.bfloat16
        )
        return spread.reshape(col_blocks * node_width, 2 * node_width)

    def per_node(supernode):
        row_index = jnp.take(row_lists[supernode], own_rows, axis=0)
        picked = block_take(surface, row_index).reshape(
            2, row_blocks * kept_rows, col_blocks * node_width
        )
        return -complex_wide(picked, expand_factor(supernode), node_width)

    summed = lax.psum_scatter(
        lax.map(per_node, jnp.arange(local_nodes * lax.axis_size("col"), dtype=jnp.int32)),
        "col",
        scatter_dimension=0,
        tiled=True,
    )
    inverse_block = summed.reshape(local_nodes, 2, row_blocks, kept_rows, node_width)
    highest = lax.Precision.HIGHEST
    narrow = factor.reshape(local_nodes, 2, row_blocks * kept_rows, node_width).astype(jnp.float32)
    blocks = inverse_block.reshape(local_nodes, 2, row_blocks * kept_rows, node_width)
    real_part = jnp.einsum(
        "nrs,nrt->nst", narrow[:, 0], blocks[:, 0], precision=highest
    ) - jnp.einsum("nrs,nrt->nst", narrow[:, 1], blocks[:, 1], precision=highest)
    imag_part = jnp.einsum(
        "nrs,nrt->nst", narrow[:, 0], blocks[:, 1], precision=highest
    ) + jnp.einsum("nrs,nrt->nst", narrow[:, 1], blocks[:, 0], precision=highest)
    local_terms = jnp.stack([real_part, imag_part], axis=1)
    totals = lax.psum(local_terms, "row")
    diagonal_block = diag_inverse - totals
    return (
        inverse_block.reshape(local_nodes, 2, row_blocks, 1, kept_rows, node_width),
        diagonal_block,
    )


def solution(mesh):
    placed = (
        P("pole", None, "row", None, None, "col", None),
        P("col", "pole", None, "row", None, None),
        P("col", "pole", None, None),
        P(),
    )
    return jax.shard_map(
        local,
        mesh=mesh,
        in_specs=placed,
        out_specs=(P("col", "pole", None, "row", None, None), P("col", "pole", None, None)),
        check_vma=False,
    )
```

profile of v0, /device:TPU:0, one launch (start us, length us, event | category | flops | bytes accessed | tf_op | source)
XLA Modules:
  0.0 130.5 jit_solution(4726892809090520174)
XLA Ops:
  7.2 8.9 %all_gather.3 = bf16[1,2,1,4,128,256]{5,4,2,1,0,3:T(8,128)(2,1)S(1)} all-gather(bf16[1,2,1,1,128,256]{5,4,2,1,0,3:T(8,128)(2,1)} %bitcast.125), channel_id=1, replica_groups=mesh['pole'=2,'row'=4,'col'=4] {'row'}, dimensions={3}, use_global_device_ids=true | all-gather | bytes 655360 | tf_op jit(solution)/shard_map/all_gather | solution.py:31
  16.0 1.0 copy.19
  17.0 5.0 %all-to-all-start = ((bf16[1,2,1,4,128,256]{4,5,1,2,0,3:T(8,128)(2,1)}), bf16[1,2,1,4,128,256]{4,5,1,2,0,3:T(8,128)(2,1)S(1)}, u32[]{:S(2)}, u32[]{:S(2)}) async-start(bf16[1,2,1,4,128,256]{4,5,1,2,0,3:T(8,128)(2,1)} %copy.19), calls=%async_computation | async-start | bytes 1048576 | tf_op jit(solution)/shard_map/all_to_all | solution.py:35
  22.0 15.0 %all-to-all-done = bf16[1,2,1,4,128,256]{4,5,1,2,0,3:T(8,128)(2,1)S(1)} async-done(((bf16[1,2,1,4,128,256]{4,5,1,2,0,3:T(8,128)(2,1)}), bf16[1,2,1,4,128,256]{4,5,1,2,0,3:T(8,128)(2,1)S(1)}, u32[]{:S(2)}, u32[]{:S(2)}) %all-to-all-start) | async-done | bytes 524320 | tf_op jit(solution)/shard_map/all_to_all | solution.py:35
  37.0 22.5 %while.12 = (s32[]{:T(128)}, f32[4,2,128,256]{3,2,1,0:T(8,128)S(1)}, s32[4]{0:T(128)S(1)}, s32[4,4,128]{2,1,0:T(4,128)}, s32[1]{0:T(128)}, /*index=5*/bf16[2,1,2...) while((s32[]{:T(128)}, ...), condition=%wide.region_1.0_spmd.clone, body=%wide.region_0.2_spmd.clone.sunk | while | flops 100959880 | bytes 4467767 | solution.py:59
  37.0 0.6 dynamic_slice.21
  39.6 0.7 dynamic-slice_bitcast_fusion.2
  40.3 0.3 copy.38
  40.6 0.9 gather_fusion
  42.7 0.6 dynamic_slice.21
  45.2 0.7 dynamic-slice_bitcast_fusion.2
  45.9 0.3 copy.38
  46.2 0.9 gather_fusion
  48.3 0.6 dynamic_slice.21
  50.8 0.7 dynamic-slice_bitcast_fusion.2
  51.5 0.3 copy.38
  51.8 0.9 gather_fusion
  53.9 0.6 dynamic_slice.21
  56.4 0.7 dynamic-slice_bitcast_fusion.2
  57.2 0.3 copy.38
  57.5 0.9 gather_fusion
  59.5 0.9 copy-done.2
  60.6 25.9 %reduce-scatter.2.cloned.1.call-done = f32[1,2,128,256]{3,2,1,0:T(8,128)} async-done(((f32[4,2,128,256]{3,2,1,0:T(8,128)}), f32[1,2,128,256]{3,2,1,0:T(8,128)}) %reduce-scatter.2.cloned.1.call-update) | async-done | bytes 262160 | tf_op jit(solution)/shard_map/reduce_scatter | solution.py:58
  86.5 1.3 fusion.18
  87.8 0.3 fusion.19
  88.1 0.3 fusion.17
  88.4 0.3 fusion.16
  88.8 0.8 pad_maximum_fusion
  89.6 1.0 copy-done.4
  90.8 30.8 %all-reduce.2.cloned.1.call-done = f32[1,2,256,256]{2,3,1,0:T(8,128)} async-done(((f32[1,2,256,256]{2,3,1,0:T(8,128)}), f32[1,2,256,256]{2,3,1,0:T(8,128)}) %all-reduce.2.cloned.1.call-update) | async-done | bytes 524304 | tf_op jit(solution)/shard_map/psum | solution.py:75
  121.6 1.1 sub.15
  122.7 1.0 copy.22
  (63 shorter events, 4.8 us)
Async XLA Ops:
  17.0 20.0 %copy-start = (bf16[2,1,1,256,1,1,256]{6,3,5,4,2,1,0:T(8,128)(2,1)S(1)}, bf16[2,1,1,256,1,1,256]{6,3,5,4,2,1,0:T(8,128)(2,1)}, u32[]{:S(2)}) copy-start(bf16[2,1,1,256,1,1,256]{6,3,5,4,2,1,0:T(8,128)(2,1)} %param.8) | copy-start | bytes 786436
  17.0 20.0 %all-to-all-start = ((bf16[1,2,1,4,128,256]{4,5,1,2,0,3:T(8,128)(2,1)}), bf16[1,2,1,4,128,256]{4,5,1,2,0,3:T(8,128)(2,1)S(1)}, u32[]{:S(2)}, u32[]{:S(2)}) async-start(bf16[1,2,1,4,128,256]{4,5,1,2,0,3:T(8,128)(2,1)} %copy.19), calls=%async_computation | async-start | bytes 1048576 | tf_op jit(solution)/shard_map/all_to_all | solution.py:35
  22.0 64.5 %reduce-scatter.2.cloned.1.call-start = ((), (), s32[]{:S(2)}) async-start(), calls=%async_computation.2 | async-start | bytes 1310720 | tf_op jit(solution)/shard_map/reduce_scatter | solution.py:58
  59.5 1.0 copy-start.2
  59.5 27.0 %copy-start.1 = (bf16[1,2,1,1,128,256]{5,4,3,2,1,0:T(8,128)(2,1)S(1)}, bf16[1,2,1,1,128,256]{5,4,3,2,1,0:T(8,128)(2,1)}, u32[]{:S(2)}) copy-start(bf16[1,2,1,1,128,256]{5,4,3,2,1,0:T(8,128)(2,1)} %param.9) | copy-start | bytes 393220
  60.5 61.1 %all-reduce.2.cloned.1.call-start = ((), (), s32[]{:S(2)}) async-start(), calls=%async_computation.3 | async-start | bytes 1048576 | tf_op jit(solution)/shard_map/psum | solution.py:75
  86.5 1.3 copy-start.3
  89.6 1.0 copy-start.4
Sparse Core Ops, SparseCore 0:
  60.6 25.8 reduce-scatter.1
  89.7 31.8 all-reduce.1
where the time goes:
time: 131 us
  waiting for transfers between devices  71.7 us (55%)
  local copies, waits for them, and re-layouts  14.8 us (11%)
  between operations  14.1 us (11%)
  blocking collectives  8.86 us (7%)
  loops' own time  8.23 us (6%)
  starting transfers between devices  5.05 us (4%)
  matrix products  4.61 us (4%)
  other arithmetic  3.18 us (2%)
    psum x1, waiting for transfers between devices, local(): totals = lax.psum(local_terms, 'row')  30.8 us
    reduce_scatter x1, waiting for transfers between devices, local(): lax.psum_scatter(lax.map(per_node, jnp.arange(local_nodes * lax.axis_size...  25.9 us
    all_to_all x1, waiting for transfers between devices, local(): lax.all_to_all(grouped, 'col', split_axis=3, concat_axis=0, tiled=True)  15 us
    all_gather x1, blocking collectives, local(): gathered = lax.all_gather(factor, 'row', axis=3, tiled=True)  8.86 us
    another operation x1, loops' own time, local(): lax.map(per_node, jnp.arange(local_nodes * lax.axis_size('col'), dtype=jn...  8.23 us
    all_to_all x1, starting transfers between devices, local(): lax.all_to_all(grouped, 'col', split_axis=3, concat_axis=0, tiled=True)  5 us
    gather x8, local copies, waits for them, and re-layouts, take_second(): return jnp.take(matrix, picks, axis=1)  3.61 us
    unnamed x12, local copies, waits for them, and re-layouts  3.17 us
  transfers between devices with their start and end apart: 3, of which 3 were waited for; matrix products, arithmetic and copies ran while one was open for 0% of the time, Pallas kernels for 0%

commit v1 on v0

v1 whole, which is shorter than its diff:
```python
import functools

import jax
import jax.numpy as jnp
from jax import lax
from jax.experimental import pallas as pl
from jax.experimental.pallas import tpu as pltpu
from jax.sharding import PartitionSpec as P

VMEM = pl.BlockSpec(memory_space=pltpu.VMEM)
VMEM_BYTES = 48 * 1024 * 1024


def partners(size, step):
    return [(place, place ^ step) for place in range(size)]


def place_one_hot(picks, width):
    kept = picks.shape[-1]
    spots = lax.broadcasted_iota(jnp.int32, (width, kept), 0)
    return jnp.where(spots == picks, 1.0, 0.0).astype(jnp.bfloat16)


def dot(lhs, rhs, contract):
    return lax.dot_general(
        lhs, rhs, (((contract[0],), (contract[1],)), ((), ())), preferred_element_type=jnp.float32
    )


def pick_kernel(grid_rows, grid_cols, local_nodes, surface, row_lists, *pieces):
    row_place = lax.axis_index("row")
    col_place = lax.axis_index("col")
    _, row_blocks, col_blocks, width, _ = surface.shape
    for step in range(grid_cols):
        target = jnp.bitwise_xor(col_place, step)
        for node in range(local_nodes):
            which = target * local_nodes + node
            for row_block in range(row_blocks):
                row_picks = row_lists[which, pl.ds(row_block * grid_rows + row_place, 1), :]
                chosen = place_one_hot(row_picks, width)
                kept = chosen.shape[1]
                for col_block in range(col_blocks):
                    col_picks = row_lists[which, pl.ds(col_block * grid_cols + col_place, 1), :]
                    wanted = place_one_hot(col_picks, width)
                    for half in range(2):
                        rows = dot(chosen, surface[half, row_block, col_block], (0, 0))
                        block = dot(rows.astype(jnp.bfloat16), wanted, (1, 0))
                        pieces[step][
                            node,
                            half,
                            row_block * kept : (row_block + 1) * kept,
                            col_block * kept : (col_block + 1) * kept,
                        ] = block.astype(jnp.bfloat16)


def block_kernel(grid_rows, grid_cols, *refs):
    pieces = refs[:grid_cols]
    factors = refs[grid_cols : grid_cols + grid_rows]
    result, held_factor, held_surface = refs[grid_cols + grid_rows :]
    row_place = lax.axis_index("row")
    col_place = lax.axis_index("col")
    local_nodes, _, row_blocks, kept, width = factors[0].shape
    col_blocks = pieces[0].shape[3] // kept
    rows = row_blocks * kept
    for node in range(local_nodes):
        for step in range(grid_rows):
            source = jnp.bitwise_xor(row_place, step)
            for row_block in range(row_blocks):
                spot = pl.ds(pl.multiple_of((row_block * grid_rows + source) * kept, kept), kept)
                held_factor[spot, :width] = factors[step][node, 0, row_block]
                held_factor[spot, width:] = factors[step][node, 1, row_block]
        for step in range(grid_cols):
            source = jnp.bitwise_xor(col_place, step)
            for col_block in range(col_blocks):
                spot = pl.ds(pl.multiple_of((col_block * grid_cols + source) * kept, kept), kept)
                taken = slice(col_block * kept, (col_block + 1) * kept)
                held_surface[:rows, spot] = pieces[step][node, 0, :, taken]
                held_surface[rows:, spot] = pieces[step][node, 1, :, taken]
        product = dot(held_surface[...], held_factor[...], (1, 0))
        result[node, 0] = product[rows:, width:] - product[:rows, :width]
        result[node, 1] = -(product[:rows, width:] + product[rows:, :width])


def correct_kernel(terms, base, *refs):
    factors, blocks = refs[:terms], refs[terms : 2 * terms]
    result = refs[2 * terms]
    local_nodes, _, rows, width = blocks[0].shape
    for node in range(local_nodes):
        real = base[node, 0]
        imag = base[node, 1]
        for factor, block in zip(factors, blocks):
            wide = jnp.concatenate([block[node, 0], block[node, 1]], axis=1)
            high = wide.astype(jnp.bfloat16)
            low = (wide - high.astype(jnp.float32)).astype(jnp.bfloat16)
            both = jnp.concatenate([high, low], axis=0)
            real_factor = factor[node, 0].reshape(rows, width)
            imag_factor = factor[node, 1].reshape(rows, width)
            from_real = dot(jnp.concatenate([real_factor, real_factor], axis=0), both, (0, 0))
            from_imag = dot(jnp.concatenate([imag_factor, imag_factor], axis=0), both, (0, 0))
            real = real - from_real[:, :width] + from_imag[:, width:]
            imag = imag - from_real[:, width:] - from_imag[:, :width]
        result[node, 0] = real
        result[node, 1] = imag


def call(kernel, out_shape, args, scratch=(), flops=0):
    moved = sum(a.size * a.dtype.itemsize for a in args)
    return pl.pallas_call(
        kernel,
        out_shape=out_shape,
        in_specs=[VMEM] * len(args),
        out_specs=jax.tree.map(lambda _: VMEM, out_shape),
        scratch_shapes=scratch,
        compiler_params=pltpu.CompilerParams(vmem_limit_bytes=VMEM_BYTES),
        cost_estimate=pl.CostEstimate(flops=flops, bytes_accessed=moved, transcendentals=0),
    )(*args)


def local(inverse_top, factor, diag_inverse, row_lists):
    grid_rows = lax.axis_size("row")
    grid_cols = lax.axis_size("col")
    local_nodes, _, row_blocks, _, kept, width = factor.shape
    col_blocks = inverse_top.shape[4]
    rows = row_blocks * kept
    surface = inverse_top.transpose(0, 1, 2, 4, 5, 3, 6).reshape(
        2, row_blocks, col_blocks, width, width
    )
    own_factor = factor.reshape(local_nodes, 2, row_blocks, kept, width)

    piece = jax.ShapeDtypeStruct((local_nodes, 2, rows, col_blocks * kept), jnp.bfloat16)
    pieces = call(
        functools.partial(pick_kernel, grid_rows, grid_cols, local_nodes),
        [piece] * grid_cols,
        [surface, row_lists],
    )
    arrived = [pieces[0]] + [None] * (grid_cols - 1)
    for step in reversed(range(1, grid_cols)):
        arrived[step] = lax.ppermute(pieces[step], "col", partners(grid_cols, step))

    def along_rows(block):
        held = [block] + [None] * (grid_rows - 1)
        for step in range(2, grid_rows, 2):
            held[step] = lax.ppermute(block, "row", partners(grid_rows, step))
        for step in range(1, grid_rows, 2):
            held[step] = lax.ppermute(held[step - 1], "row", partners(grid_rows, 1))
        return held

    factors = along_rows(own_factor)
    total = grid_rows * row_blocks * kept
    inverse_block = call(
        functools.partial(block_kernel, grid_rows, grid_cols),
        jax.ShapeDtypeStruct((local_nodes, 2, rows, width), jnp.float32),
        arrived + factors,
        [pltpu.VMEM((total, 2 * width), jnp.bfloat16), pltpu.VMEM((2 * rows, total), jnp.bfloat16)],
    )
    blocks = along_rows(inverse_block)
    out = jax.ShapeDtypeStruct((local_nodes, 2, width, width), jnp.float32)
    near = call(
        functools.partial(correct_kernel, 2), out, [diag_inverse] + factors[:2] + blocks[:2]
    )
    far = factors[2:] + blocks[2:]
    diagonal_block = call(functools.partial(correct_kernel, grid_rows - 2), out, [near] + far)
    return (
        inverse_block.reshape(local_nodes, 2, row_blocks, 1, kept, width),
        diagonal_block,
    )


def solution(mesh):
    placed = (
        P("pole", None, "row", None, None, "col", None),
        P("col", "pole", None, "row", None, None),
        P("col", "pole", None, None),
        P(),
    )
    return jax.shard_map(
        local,
        mesh=mesh,
        in_specs=placed,
        out_specs=(P("col", "pole", None, "row", None, None), P("col", "pole", None, None)),
        check_vma=False,
    )
```

time: 131 us -> 31.7 us (0.24)
  waiting for transfers between devices: 71.7 us -> 15.7 us
  between operations: 14.1 us -> 0.68 us
  local copies, waits for them, and re-layouts: 14.8 us -> 2.6 us
  blocking collectives: 8.86 us -> 0 us
  loops' own time: 8.23 us -> 0 us
  matrix products: 4.61 us -> 0 us
  starting transfers between devices: 5.05 us -> 9.03 us
  Pallas kernels: 0 us -> 3.47 us
  other arithmetic: 3.18 us -> 0 us
    psum x1 -> x0, waiting for transfers between devices: 30.8 us -> none  [local(): totals = lax.psum(local_terms, 'row')]
    reduce_scatter x1 -> x0, waiting for transfers between devices: 25.9 us -> none  [local(): lax.psum_scatter(lax.map(per_node, jnp.arange(local_nodes * lax.axis_size...]
    ppermute x0 -> x9, waiting for transfers between devices: none -> 15.7 us  [the longest x2 9.45 us: along_rows(): held[step] = lax.ppermute(block, 'row', partners(grid_rows, step))]
    all_to_all x1 -> x0, waiting for transfers between devices: 15 us -> none  [local(): lax.all_to_all(grouped, 'col', split_axis=3, concat_axis=0, tiled=True)]
    ppermute x0 -> x9, starting transfers between devices: none -> 9.03 us  [the longest x2 4.55 us: along_rows(): held[step] = lax.ppermute(block, 'row', partners(grid_rows, step))]
    all_gather x1 -> x0, blocking collectives: 8.86 us -> none  [local(): gathered = lax.all_gather(factor, 'row', axis=3, tiled=True)]
    another operation x1 -> x0, loops' own time: 8.23 us -> none  [local(): lax.map(per_node, jnp.arange(local_nodes * lax.axis_size('col'), dtype=jn...]
    all_to_all x1 -> x0, starting transfers between devices: 5 us -> none  [local(): lax.all_to_all(grouped, 'col', split_axis=3, concat_axis=0, tiled=True)]
  transfers between devices with their start and end apart: 3 -> 9, of which waited for: 3 -> 6; matrix products, arithmetic and copies ran while one was open for 0% -> 0% of each run, Pallas kernels for 0% -> 4%
where the time goes in v1:
time: 31.7 us; the launch traced here: 31.5 us
  waiting for transfers between devices  15.7 us (50%)
  starting transfers between devices  9.03 us (28%)
  Pallas kernels  3.47 us (11%)
  local copies, waits for them, and re-layouts  2.6 us (8%)
  between operations  0.68 us (2%)
    ppermute x2, waiting for transfers between devices, along_rows(): held[step] = lax.ppermute(block, 'row', partners(grid_rows, step))  9.45 us
    ppermute x3, waiting for transfers between devices, local(): arrived[step] = lax.ppermute(pieces[step], 'col', partners(grid_cols, step))  6.1 us
    ppermute x2, starting transfers between devices, along_rows(): held[step] = lax.ppermute(block, 'row', partners(grid_rows, step))  4.55 us
    ppermute x3, starting transfers between devices, local(): arrived[step] = lax.ppermute(pieces[step], 'col', partners(grid_cols, step))  4.47 us
    pallas_call x4, Pallas kernels, call(): pl.pallas_call(kernel, out_shape=out_shape, in_specs=[VMEM] * len(args),...  3.47 us
    unnamed x10, local copies, waits for them, and re-layouts  2.6 us
  transfers between devices with their start and end apart: 9, of which 6 were waited for; matrix products, arithmetic and copies ran while one was open for 0% of the time, Pallas kernels for 4%

profile of v1, /device:TPU:0, one launch (start us, length us, event | category | flops | bytes accessed | tf_op | source)
XLA Modules:
  0.0 31.5 jit_solution(10056370737374589608)
XLA Ops:
  0.6 3.0 %collective-permute-start.4 = (bf16[1,2,1,128,256]{4,3,2,1,0:T(8,128)(2,1)}, bf16[1,2,1,128,256]{4,3,2,1,0:T(8,128)(2,1)S(1)}, u32[]{:S(2)}, u32[]{:S(2)}) collective-permute-start(bf16[1,2,1,128,256]{4,3,2,1,0:T(8,128)(2,1)} %bitcast.6), channel_id=1, source_target_pairs={{0,8},{4,12},{8,0},{12,4},{1,9},{5,13},{9,1},{13,5},{2,10},{6,14},... | collective-permute-start | bytes 393224 | tf_op jit(solution)/shard_map/ppermute | solution.py:143
  3.7 0.0 collective-permute-start.3
  3.7 3.7 %collective-permute-done.4.refs_6_.refs_0_ = bf16[1,2,1,128,256]{4,3,2,1,0:T(8,128)(2,1)S(1)} collective-permute-done((bf16[1,2,1,128,256]{4,3,2,1,0:T(8,128)(2,1)}, bf16[1,2,1,128,256]{4,3,2,1,0:T(8,128)(2,1)S(1)}, u32[]{:S(2)}, u32[]{:S(2)}) %collective-permute-start.4) | collective-permute-done | bytes 131104 | tf_op jit(solution)/shard_map/ppermute | solution.py:143
  7.4 0.0 collective-permute-start.5
  7.4 0.0 copy-start.3
  7.4 0.9 %copy-done.3 = bf16[2,1,1,256,1,1,256]{6,3,5,4,2,1,0:T(8,128)(2,1)S(1)} copy-done((bf16[2,1,1,256,1,1,256]{6,3,5,4,2,1,0:T(8,128)(2,1)S(1)}, bf16[2,1,1,256,1,1,256]{6,3,5,4,2,1,0:T(8,128)(2,1)}, u32[]{:S(2)}) %copy-start.3) | copy-done | bytes 262168
  8.3 0.0 copy-start.4
  8.3 0.7 %copy-done.4 = s32[4,4,128]{2,1,0:T(4,128)S(1)} copy-done((s32[4,4,128]{2,1,0:T(4,128)S(1)}, s32[4,4,128]{2,1,0:T(4,128)}, u32[]{:S(2)}) %copy-start.4) | copy-done | bytes 8216
  9.0 0.0 copy-start.2
  9.0 0.7 %shard_map.59 = (bf16[1,2,128,128]{3,2,1,0:T(8,128)(2,1)S(1)}, bf16[1,2,128,128]{3,2,1,0:T(8,128)(2,1)S(1)}, bf16[1,2,128,128]{3,2,1,0:T(8,128)(2,1)S(1)}, bf16[1,2,128,128]{3,2,1,0:T(8,128)(2,1)S(1)}) custom-call(bf16[2,1,1,256,256]{4,3,2,1,0:T(8,128)(2,1)S(1)} %bitcast.10, s32[4,4,128]{2,1,0:T(4,128)S(1)} %copy-done.4), custom_call_target="tpu_custom_call" | custom-call | bytes 270336 | tf_op jit(solution)/shard_map/pallas_call | solution.py:108
  9.7 1.9 %collective-permute-start = (bf16[1,2,128,128]{3,2,1,0:T(8,128)(2,1)S(1)}, bf16[1,2,128,128]{3,2,1,0:T(8,128)(2,1)S(1)}, u32[]{:S(2)}, u32[]{:S(2)}) collective-permute-start(bf16[1,2,128,128]{3,2,1,0:T(8,128)(2,1)S(1)} %get-tuple-element.7), channel_id=1, source_target_pairs={{0,1},{1,0},{2,3},{3,2},{4,5},{5,4},{6,7},{7,6},{8,9},{9,8},{10,11... | collective-permute-start | bytes 196616 | tf_op jit(solution)/shard_map/ppermute | solution.py:138
  11.6 2.6 %collective-permute-start.1 = (bf16[1,2,128,128]{3,2,1,0:T(8,128)(2,1)S(1)}, bf16[1,2,128,128]{3,2,1,0:T(8,128)(2,1)S(1)}, u32[]{:S(2)}, u32[]{:S(2)}) collective-permute-start(bf16[1,2,128,128]{3,2,1,0:T(8,128)(2,1)S(1)} %get-tuple-element.8), channel_id=1, source_target_pairs={{0,2},{1,3},{2,0},{3,1},{4,6},{5,7},{6,4},{7,5},{8,10},{9,11},{10,... | collective-permute-start | bytes 196616 | tf_op jit(solution)/shard_map/ppermute | solution.py:138
  14.2 0.0 collective-permute-start.2
  14.2 0.2 collective-permute-done.refs_1_
  14.3 4.2 %collective-permute-done.1.refs_2_ = bf16[1,2,128,128]{3,2,1,0:T(8,128)(2,1)S(1)} collective-permute-done((bf16[1,2,128,128]{3,2,1,0:T(8,128)(2,1)S(1)}, bf16[1,2,128,128]{3,2,1,0:T(8,128)(2,1)S(1)}, u32[]{:S(2)}, u32[]{:S(2)}) %collective-permute-start.1) | collective-permute-done | bytes 65568 | tf_op jit(solution)/shard_map/ppermute | solution.py:138
  18.5 1.8 %collective-permute-done.2.refs_3_ = bf16[1,2,128,128]{3,2,1,0:T(8,128)(2,1)S(1)} collective-permute-done((bf16[1,2,128,128]{3,2,1,0:T(8,128)(2,1)S(1)}, bf16[1,2,128,128]{3,2,1,0:T(8,128)(2,1)S(1)}, u32[]{:S(2)}, u32[]{:S(2)}) %collective-permute-start.2) | collective-permute-done | bytes 65568 | tf_op jit(solution)/shard_map/ppermute | solution.py:138
  20.3 0.0 collective-permute-done.3.refs_5_.refs_1_
  20.3 0.0 collective-permute-done.5.refs_7_.refs_1_
  20.3 0.0 copy-done.2
  20.3 0.0 copy-start.1
  20.3 1.1 %shard_map.60.refs_2_ = f32[1,2,128,256]{3,2,1,0:T(8,128)} custom-call(bf16[1,2,128,128]{3,2,1,0:T(8,128)(2,1)S(1)} %get-tuple-element.6.refs_0_, bf16[1,2,128,128]{3,2,1,0:T(8,128)(2,1)S(1)} %collective-permute-done.refs_1_, bf16[1,2,128,128]{3,2,1,0:T(8,128)(2,1)S(1)} %collective-permute-done.1.refs_2_, ...), custom_call_target="tpu_custom_call" | custom-call | bytes 786432 | tf_op jit(solution)/shard_map/pallas_call | solution.py:108
  21.4 1.5 %collective-permute-start.7 = (f32[1,2,128,256]{3,2,1,0:T(8,128)}, f32[1,2,128,256]{3,2,1,0:T(8,128)S(1)}, u32[]{:S(2)}, u32[]{:S(2)}) collective-permute-start(f32[1,2,128,256]{3,2,1,0:T(8,128)} %shard_map.60.refs_2_), channel_id=1, source_target_pairs={{0,8},{4,12},{8,0},{12,4},{1,9},{5,13},{9,1},{13,5},{2,10},{6,14},... | collective-permute-start | bytes 786440 | tf_op jit(solution)/shard_map/ppermute | solution.py:143
  22.9 0.0 collective-permute-start.6
  22.9 5.7 %collective-permute-done.7.refs_2_ = f32[1,2,128,256]{3,2,1,0:T(8,128)S(1)} collective-permute-done((f32[1,2,128,256]{3,2,1,0:T(8,128)}, f32[1,2,128,256]{3,2,1,0:T(8,128)S(1)}, u32[]{:S(2)}, u32[]{:S(2)}) %collective-permute-start.7) | collective-permute-done | bytes 262176 | tf_op jit(solution)/shard_map/ppermute | solution.py:143
  28.7 0.0 collective-permute-start.8
  28.7 0.0 collective-permute-done.6.refs_3_
  28.7 0.0 copy-done.1
  28.7 0.0 copy-start
  28.7 0.9 %copy-done = f32[1,2,128,256]{3,2,1,0:T(8,128)S(1)} copy-done((f32[1,2,128,256]{3,2,1,0:T(8,128)S(1)}, f32[1,2,128,256]{3,2,1,0:T(8,128)}, u32[]{:S(2)}) %copy-start) | copy-done | bytes 262168
  29.6 0.5 %shard_map.61.base = f32[1,2,256,256]{3,2,1,0:T(8,128)S(1)} custom-call(f32[1,2,256,256]{3,2,1,0:T(8,128)S(1)} %copy-done.1, bf16[1,2,1,128,256]{4,3,2,1,0:T(8,128)(2,1)S(1)} %bitcast.9, bf16[1,2,1,128,256]{4,3,2,1,0:T(8,128)(2,1)S(1)} %collective-permute-done.3.refs_5_.refs_1_, f32[1,2,128,256]{3,2,1,0:T(8,128)S(1)} %copy-done, ...), custom_call_target="tpu_custom_call" | custom-call | bytes 1310720 | tf_op jit(solution)/shard_map/pallas_call | solution.py:108
  30.1 0.1 collective-permute-done.8.refs_3_
  30.2 1.3 %shard_map.62 = f32[1,2,256,256]{3,2,1,0:T(8,128)} custom-call(f32[1,2,256,256]{3,2,1,0:T(8,128)S(1)} %shard_map.61.base, bf16[1,2,1,128,256]{4,3,2,1,0:T(8,128)(2,1)S(1)} %collective-permute-done.4.refs_6_.refs_0_, bf16[1,2,1,128,256]{4,3,2,1,0:T(8,128)(2,1)S(1)} %collective-permute-done.5.refs_7_.refs_1_, ...), custom_call_target="tpu_custom_call" | custom-call | bytes 1310720 | tf_op jit(solution)/shard_map/pallas_call | solution.py:108
Async XLA Ops:
  0.6 6.7 %collective-permute-start.4 = (bf16[1,2,1,128,256]{4,3,2,1,0:T(8,128)(2,1)}, bf16[1,2,1,128,256]{4,3,2,1,0:T(8,128)(2,1)S(1)}, u32[]{:S(2)}, u32[]{:S(2)}) collective-permute-start(bf16[1,2,1,128,256]{4,3,2,1,0:T(8,128)(2,1)} %bitcast.6), channel_id=1, source_target_pairs={{0,8},{4,12},{8,0},{12,4},{1,9},{5,13},{9,1},{13,5},{2,10},{6,14},... | collective-permute-start | bytes 393224 | tf_op jit(solution)/shard_map/ppermute | solution.py:143
  3.7 16.6 %collective-permute-start.3 = (bf16[1,2,1,128,256]{4,3,2,1,0:T(8,128)(2,1)}, bf16[1,2,1,128,256]{4,3,2,1,0:T(8,128)(2,1)S(1)}, u32[]{:S(2)}, u32[]{:S(2)}) collective-permute-start(bf16[1,2,1,128,256]{4,3,2,1,0:T(8,128)(2,1)} %bitcast.7), channel_id=1, source_target_pairs={{0,4},{4,0},{8,12},{12,8},{1,5},{5,1},{9,13},{13,9},{2,6},{6,2},{1... | collective-permute-start | bytes 393224 | tf_op jit(solution)/shard_map/ppermute | solution.py:145
  7.4 12.9 %collective-permute-start.5 = (bf16[1,2,1,128,256]{4,3,2,1,0:T(8,128)(2,1)S(1)}, bf16[1,2,1,128,256]{4,3,2,1,0:T(8,128)(2,1)S(1)}, u32[]{:S(2)}, u32[]{:S(2)}) collective-permute-start(bf16[1,2,1,128,256]{4,3,2,1,0:T(8,128)(2,1)S(1)} %collective-permute-done.4.refs_6_.refs_0_), channel_id=1, source_target_pairs={{0,4},{4,0},{8,12},{12,8},{1,5},{5,1},{9,13},{13,9},{2,6},{6,2},{1... | collective-permute-start | bytes 393224 | tf_op jit(solution)/shard_map/ppermute | solution.py:145
  7.4 1.0 %copy-start.3 = (bf16[2,1,1,256,1,1,256]{6,3,5,4,2,1,0:T(8,128)(2,1)S(1)}, bf16[2,1,1,256,1,1,256]{6,3,5,4,2,1,0:T(8,128)(2,1)}, u32[]{:S(2)}) copy-start(bf16[2,1,1,256,1,1,256]{6,3,5,4,2,1,0:T(8,128)(2,1)} %param.4) | copy-start | bytes 786436
  8.3 0.7 %copy-start.4 = (s32[4,4,128]{2,1,0:T(4,128)S(1)}, s32[4,4,128]{2,1,0:T(4,128)}, u32[]{:S(2)}) copy-start(s32[4,4,128]{2,1,0:T(4,128)} %row_lists.1) | copy-start | bytes 24580
  9.0 11.3 %copy-start.2 = (bf16[1,2,1,1,128,256]{5,4,3,2,1,0:T(8,128)(2,1)S(1)}, bf16[1,2,1,1,128,256]{5,4,3,2,1,0:T(8,128)(2,1)}, u32[]{:S(2)}) copy-start(bf16[1,2,1,1,128,256]{5,4,3,2,1,0:T(8,128)(2,1)} %param.5) | copy-start | bytes 393220
  9.7 4.6 %collective-permute-start = (bf16[1,2,128,128]{3,2,1,0:T(8,128)(2,1)S(1)}, bf16[1,2,128,128]{3,2,1,0:T(8,128)(2,1)S(1)}, u32[]{:S(2)}, u32[]{:S(2)}) collective-permute-start(bf16[1,2,128,128]{3,2,1,0:T(8,128)(2,1)S(1)} %get-tuple-element.7), channel_id=1, source_target_pairs={{0,1},{1,0},{2,3},{3,2},{4,5},{5,4},{6,7},{7,6},{8,9},{9,8},{10,11... | collective-permute-start | bytes 196616 | tf_op jit(solution)/shard_map/ppermute | solution.py:138
  11.6 6.9 %collective-permute-start.1 = (bf16[1,2,128,128]{3,2,1,0:T(8,128)(2,1)S(1)}, bf16[1,2,128,128]{3,2,1,0:T(8,128)(2,1)S(1)}, u32[]{:S(2)}, u32[]{:S(2)}) collective-permute-start(bf16[1,2,128,128]{3,2,1,0:T(8,128)(2,1)S(1)} %get-tuple-element.8), channel_id=1, source_target_pairs={{0,2},{1,3},{2,0},{3,1},{4,6},{5,7},{6,4},{7,5},{8,10},{9,11},{10,... | collective-permute-start | bytes 196616 | tf_op jit(solution)/shard_map/ppermute | solution.py:138
  14.2 6.1 %collective-permute-start.2 = (bf16[1,2,128,128]{3,2,1,0:T(8,128)(2,1)S(1)}, bf16[1,2,128,128]{3,2,1,0:T(8,128)(2,1)S(1)}, u32[]{:S(2)}, u32[]{:S(2)}) collective-permute-start(bf16[1,2,128,128]{3,2,1,0:T(8,128)(2,1)S(1)} %get-tuple-element.9), channel_id=1, source_target_pairs={{0,3},{1,2},{2,1},{3,0},{4,7},{5,6},{6,5},{7,4},{8,11},{9,10},{10,... | collective-permute-start | bytes 196616 | tf_op jit(solution)/shard_map/ppermute | solution.py:138
  20.3 8.4 %copy-start.1 = (f32[1,2,256,256]{3,2,1,0:T(8,128)S(1)}, f32[1,2,256,256]{3,2,1,0:T(8,128)}, u32[]{:S(2)}) copy-start(f32[1,2,256,256]{3,2,1,0:T(8,128)} %base.1) | copy-start | bytes 1572868
  21.4 7.3 %collective-permute-start.7 = (f32[1,2,128,256]{3,2,1,0:T(8,128)}, f32[1,2,128,256]{3,2,1,0:T(8,128)S(1)}, u32[]{:S(2)}, u32[]{:S(2)}) collective-permute-start(f32[1,2,128,256]{3,2,1,0:T(8,128)} %shard_map.60.refs_2_), channel_id=1, source_target_pairs={{0,8},{4,12},{8,0},{12,4},{1,9},{5,13},{9,1},{13,5},{2,10},{6,14},... | collective-permute-start | bytes 786440 | tf_op jit(solution)/shard_map/ppermute | solution.py:143
  22.9 5.8 %collective-permute-start.6 = (f32[1,2,128,256]{3,2,1,0:T(8,128)}, f32[1,2,128,256]{3,2,1,0:T(8,128)S(1)}, u32[]{:S(2)}, u32[]{:S(2)}) collective-permute-start(f32[1,2,128,256]{3,2,1,0:T(8,128)} %shard_map.60.refs_2_), channel_id=1, source_target_pairs={{0,4},{4,0},{8,12},{12,8},{1,5},{5,1},{9,13},{13,9},{2,6},{6,2},{1... | collective-permute-start | bytes 786440 | tf_op jit(solution)/shard_map/ppermute | solution.py:145
  28.7 1.5 %collective-permute-start.8 = (f32[1,2,128,256]{3,2,1,0:T(8,128)S(1)}, f32[1,2,128,256]{3,2,1,0:T(8,128)S(1)}, u32[]{:S(2)}, u32[]{:S(2)}) collective-permute-start(f32[1,2,128,256]{3,2,1,0:T(8,128)S(1)} %collective-permute-done.7.refs_2_), channel_id=1, source_target_pairs={{0,4},{4,0},{8,12},{12,8},{1,5},{5,1},{9,13},{13,9},{2,6},{6,2},{1... | collective-permute-start | bytes 786440 | tf_op jit(solution)/shard_map/ppermute | solution.py:145
  28.7 1.0 %copy-start = (f32[1,2,128,256]{3,2,1,0:T(8,128)S(1)}, f32[1,2,128,256]{3,2,1,0:T(8,128)}, u32[]{:S(2)}) copy-start(f32[1,2,128,256]{3,2,1,0:T(8,128)} %shard_map.60.refs_2_) | copy-start | bytes 786436

commit v2 on v1

--- a/solution.py
+++ b/solution.py
@@ -8,7 +8,7 @@
 from jax.sharding import PartitionSpec as P
 
 VMEM = pl.BlockSpec(memory_space=pltpu.VMEM)
-VMEM_BYTES = 48 * 1024 * 1024
+VMEM_BYTES = 24 * 1024 * 1024
 
 
 def partners(size, step):
@@ -27,34 +27,39 @@
     )
 
 
-def pick_kernel(grid_rows, grid_cols, local_nodes, surface, row_lists, *pieces):
+def choose_kernel(grid_rows, grid_cols, local_nodes, row_lists, row_choice, col_choice):
     row_place = lax.axis_index("row")
     col_place = lax.axis_index("col")
-    _, row_blocks, col_blocks, width, _ = surface.shape
-    for step in range(grid_cols):
-        target = jnp.bitwise_xor(col_place, step)
-        for node in range(local_nodes):
-            which = target * local_nodes + node
-            for row_block in range(row_blocks):
-                row_picks = row_lists[which, pl.ds(row_block * grid_rows + row_place, 1), :]
-                chosen = place_one_hot(row_picks, width)
-                kept = chosen.shape[1]
-                for col_block in range(col_blocks):
-                    col_picks = row_lists[which, pl.ds(col_block * grid_cols + col_place, 1), :]
-                    wanted = place_one_hot(col_picks, width)
-                    for half in range(2):
-                        rows = dot(chosen, surface[half, row_block, col_block], (0, 0))
-                        block = dot(rows.astype(jnp.bfloat16), wanted, (1, 0))
-                        pieces[step][
-                            node,
-                            half,
-                            row_block * kept : (row_block + 1) * kept,
-                            col_block * kept : (col_block + 1) * kept,
-                        ] = block.astype(jnp.bfloat16)
-
-
-def block_kernel(grid_rows, grid_cols, *refs):
-    pieces = refs[:grid_cols]
+    slots, row_blocks, width, _ = row_choice.shape
+    for slot in range(slots):
+        step, node = slot // local_nodes, slot % local_nodes
+        which = jnp.bitwise_xor(col_place, step) * local_nodes + node
+        for block in range(row_blocks):
+            picks = row_lists[which, pl.ds(block * grid_rows + row_place, 1), :]
+            row_choice[slot, block] = place_one_hot(picks, width)
+        for block in range(col_choice.shape[1]):
+            picks = row_lists[which, pl.ds(block * grid_cols + col_place, 1), :]
+            col_choice[slot, block] = place_one_hot(picks, width)
+
+
+def pick_kernel(grid_cols, local_nodes, surface, row_choice, col_choice, *pieces):
+    slots, row_blocks, width, kept = row_choice.shape
+    col_blocks = col_choice.shape[1]
+    for slot in range(slots):
+        step, node = slot // local_nodes, slot % local_nodes
+        for row_block in range(row_blocks):
+            rows = slice(row_block * kept, (row_block + 1) * kept)
+            for col_block in range(col_blocks):
+                cols = slice(col_block * kept, (col_block + 1) * kept)
+                for half in range(2):
+                    block = surface[half, row_block, col_block]
+                    taken = dot(row_choice[slot, row_block], block, (0, 0)).astype(jnp.bfloat16)
+                    taken = dot(taken, col_choice[slot, col_block], (1, 0))
+                    pieces[step][node, half, rows, cols] = taken.astype(jnp.bfloat16)
+
+
+def block_kernel(grid_rows, grid_cols, order, *refs):
+    pieces = dict(zip(order, refs[:grid_cols]))
     factors = refs[grid_cols : grid_cols + grid_rows]
     result, held_factor, held_surface = refs[grid_cols + grid_rows :]
     row_place = lax.axis_index("row")
@@ -84,6 +89,8 @@
 def correct_kernel(terms, base, *refs):
     factors, blocks = refs[:terms], refs[terms : 2 * terms]
     result = refs[2 * terms]
+    if len(refs) > 2 * terms + 1:
+        refs[2 * terms + 1][...] = blocks[0][...]
     local_nodes, _, rows, width = blocks[0].shape
     for node in range(local_nodes):
         real = base[node, 0]
@@ -128,38 +135,61 @@
     own_factor = factor.reshape(local_nodes, 2, row_blocks, kept, width)
 
     piece = jax.ShapeDtypeStruct((local_nodes, 2, rows, col_blocks * kept), jnp.bfloat16)
+    slots = grid_cols * local_nodes
+    choices = call(
+        functools.partial(choose_kernel, grid_rows, grid_cols, local_nodes),
+        [
+            jax.ShapeDtypeStruct((slots, row_blocks, width, kept), jnp.bfloat16),
+            jax.ShapeDtypeStruct((slots, col_blocks, width, kept), jnp.bfloat16),
+        ],
+        [row_lists],
+    )
     pieces = call(
-        functools.partial(pick_kernel, grid_rows, grid_cols, local_nodes),
+        functools.partial(pick_kernel, grid_cols, local_nodes),
         [piece] * grid_cols,
-        [surface, row_lists],
-    )
+        [surface, *choices],
+    )
+    def across_chips(block):
+        steps = range(2, grid_rows, 2)
+        return [block] + [lax.ppermute(block, "row", partners(grid_rows, s)) for s in steps]
+
+    def within_chips(blocks):
+        return [lax.ppermute(block, "row", partners(grid_rows, 1)) for block in blocks]
+
+    def in_order(blocks):
+        half = grid_rows // 2
+        return [blocks[step // 2 + (step % 2) * half] for step in range(grid_rows)]
+
+    mate = lax.ppermute(own_factor, "row", partners(grid_rows, 1))
+    mate, *pieces = lax.optimization_barrier((mate, *pieces))
     arrived = [pieces[0]] + [None] * (grid_cols - 1)
-    for step in reversed(range(1, grid_cols)):
+    order = [0, *range(grid_cols // 2, grid_cols), *range(grid_cols // 2 - 1, 0, -1)]
+    for step in order[1:]:
         arrived[step] = lax.ppermute(pieces[step], "col", partners(grid_cols, step))
-
-    def along_rows(block):
-        held = [block] + [None] * (grid_rows - 1)
-        for step in range(2, grid_rows, 2):
-            held[step] = lax.ppermute(block, "row", partners(grid_rows, step))
-        for step in range(1, grid_rows, 2):
-            held[step] = lax.ppermute(held[step - 1], "row", partners(grid_rows, 1))
-        return held
-
-    factors = along_rows(own_factor)
+    factors = [own_factor, mate] + [lax.ppermute(own_factor, "row", partners(grid_rows, k)) for k in range(2, grid_rows)]
+    factors = factors[0::2] + factors[1::2]
     total = grid_rows * row_blocks * kept
-    inverse_block = call(
-        functools.partial(block_kernel, grid_rows, grid_cols),
+    work = call(
+        functools.partial(block_kernel, grid_rows, grid_cols, tuple(order)),
         jax.ShapeDtypeStruct((local_nodes, 2, rows, width), jnp.float32),
-        arrived + factors,
+        [arrived[step] for step in order] + in_order(factors),
         [pltpu.VMEM((total, 2 * width), jnp.bfloat16), pltpu.VMEM((2 * rows, total), jnp.bfloat16)],
     )
-    blocks = along_rows(inverse_block)
     out = jax.ShapeDtypeStruct((local_nodes, 2, width, width), jnp.float32)
-    near = call(
-        functools.partial(correct_kernel, 2), out, [diag_inverse] + factors[:2] + blocks[:2]
-    )
-    far = factors[2:] + blocks[2:]
-    diagonal_block = call(functools.partial(correct_kernel, grid_rows - 2), out, [near] + far)
+    half = grid_rows // 2
+    across = across_chips(work)
+    mate = within_chips(across[:1])
+    near, inverse_block = call(
+        functools.partial(correct_kernel, 2),
+        [out, jax.ShapeDtypeStruct(work.shape, work.dtype)],
+        [diag_inverse, factors[0], factors[half], work] + mate,
+    )
+    near, *others = lax.optimization_barrier((near, *across[1:]))
+    far_blocks = others + within_chips(others)
+    far_factors = factors[1:half] + factors[half + 1 :]
+    diagonal_block = call(
+        functools.partial(correct_kernel, grid_rows - 2), out, [near] + far_factors + far_blocks
+    )
     return (
         inverse_block.reshape(local_nodes, 2, row_blocks, 1, kept, width),
         diagonal_block,

time: 31.7 us -> 27.9 us (0.88)
  waiting for transfers between devices: 15.7 us -> 12.3 us
  local copies, waits for them, and re-layouts: 2.6 us -> 1.65 us
  starting transfers between devices: 9.03 us -> 9.56 us
    ppermute x6, waiting for transfers between devices: 9.57 us -> 7.56 us  [the longest x1 6.02 us: across_chips(): lax.ppermute(block, 'row', partners(grid_rows, s))]
    ppermute x3, waiting for transfers between devices: 6.1 us -> 4.73 us  [local(): arrived[step] = lax.ppermute(pieces[step], 'col', partners(grid_cols, step))]
    unnamed x10 -> x8, local copies, waits for them, and re-layouts: 2.6 us -> 1.65 us
    pallas_call x4 -> x5, Pallas kernels: 3.47 us -> 3.51 us  [call(): pl.pallas_call(kernel, out_shape=out_shape, in_specs=[VMEM] * len(args),...]
  transfers between devices with their start and end apart: 9 -> 9, of which waited for: 6 -> 5; matrix products, arithmetic and copies ran while one was open for 0% -> 0% of each run, Pallas kernels for 4% -> 7%
where the time goes in v2:
time: 27.9 us; the launch traced here: 27.7 us
  waiting for transfers between devices  12.3 us (44%)
  starting transfers between devices  9.56 us (34%)
  Pallas kernels  3.51 us (13%)
  local copies, waits for them, and re-layouts  1.65 us (6%)
  between operations  0.69 us (2%)
    ppermute x1, waiting for transfers between devices, across_chips(): lax.ppermute(block, 'row', partners(grid_rows, s))  6.02 us
    ppermute x3, waiting for transfers between devices, local(): arrived[step] = lax.ppermute(pieces[step], 'col', partners(grid_cols, step))  4.73 us
    ppermute x3, starting transfers between devices, local(): arrived[step] = lax.ppermute(pieces[step], 'col', partners(grid_cols, step))  4.69 us
    pallas_call x5, Pallas kernels, call(): pl.pallas_call(kernel, out_shape=out_shape, in_specs=[VMEM] * len(args),...  3.51 us
    ppermute x2, starting transfers between devices, local(): lax.ppermute(own_factor, 'row', partners(grid_rows, k))  2.69 us
    unnamed x8, local copies, waits for them, and re-layouts  1.65 us
    ppermute x1, starting transfers between devices, across_chips(): lax.ppermute(block, 'row', partners(grid_rows, s))  1.58 us
    ppermute x2, waiting for transfers between devices, within_chips(): lax.ppermute(block, 'row', partners(grid_rows, 1))  1.54 us
  transfers between devices with their start and end apart: 9, of which 5 were waited for; matrix products, arithmetic and copies ran while one was open for 0% of the time, Pallas kernels for 7%

profile of v2, /device:TPU:0, one launch (start us, length us, event | category | flops | bytes accessed | tf_op | source)
XLA Modules:
  0.0 27.7 jit_solution(7381943323309726633)
XLA Ops:
  0.6 0.5 %collective-permute-start = (bf16[1,2,1,128,256]{4,3,2,1,0:T(8,128)(2,1)}, bf16[1,2,1,128,256]{4,3,2,1,0:T(8,128)(2,1)S(1)}, u32[]{:S(2)}, u32[]{:S(2)}) collective-permute-start(bf16[1,2,1,128,256]{4,3,2,1,0:T(8,128)(2,1)} %bitcast.5), channel_id=1, source_target_pairs={{0,4},{4,0},{8,12},{12,8},{1,5},{5,1},{9,13},{13,9},{2,6},{6,2},{1... | collective-permute-start | bytes 393224 | tf_op jit(solution)/shard_map/ppermute | solution.py:163
  1.1 2.6 %collective-permute-start.5 = (bf16[1,2,1,128,256]{4,3,2,1,0:T(8,128)(2,1)}, bf16[1,2,1,128,256]{4,3,2,1,0:T(8,128)(2,1)S(1)}, u32[]{:S(2)}, u32[]{:S(2)}) collective-permute-start(bf16[1,2,1,128,256]{4,3,2,1,0:T(8,128)(2,1)} %bitcast.6), channel_id=1, source_target_pairs={{0,12},{4,8},{8,4},{12,0},{1,13},{5,9},{9,5},{13,1},{2,14},{6,10},... | collective-permute-start | bytes 393224 | tf_op jit(solution)/shard_map/ppermute | solution.py:169
  3.8 0.0 collective-permute-start.4
  3.8 0.0 copy-start.3
  3.8 0.7 %copy-done.3 = s32[4,4,128]{2,1,0:T(4,128)S(1)} copy-done((s32[4,4,128]{2,1,0:T(4,128)S(1)}, s32[4,4,128]{2,1,0:T(4,128)}, u32[]{:S(2)}) %copy-start.3) | copy-done | bytes 8216
  4.5 0.1 shard_map.59
  4.6 0.0 copy-start.2
  4.6 0.9 %copy-done.2 = bf16[2,1,1,256,1,1,256]{6,3,5,4,2,1,0:T(8,128)(2,1)S(1)} copy-done((bf16[2,1,1,256,1,1,256]{6,3,5,4,2,1,0:T(8,128)(2,1)S(1)}, bf16[2,1,1,256,1,1,256]{6,3,5,4,2,1,0:T(8,128)(2,1)}, u32[]{:S(2)}) %copy-start.2) | copy-done | bytes 262168
  5.6 0.0 copy-start.1
  5.6 0.7 %shard_map.60 = (bf16[1,2,128,128]{3,2,1,0:T(8,128)(2,1)S(1)}, bf16[1,2,128,128]{3,2,1,0:T(8,128)(2,1)S(1)}, bf16[1,2,128,128]{3,2,1,0:T(8,128)(2,1)S(1)}, bf16[1,2,128,128]{3,2,1,0:T(8,128)(2,1)S(1)}) custom-call(bf16[2,1,1,256,256]{4,3,2,1,0:T(8,128)(2,1)S(1)} %bitcast.10, bf16[4,1,256,128]{3,2,1,0:T(8,128)(2,1)S(1)} %get-tuple-element.17.row_choice, ...), custom_call_target="tpu_custom_call" | custom-call | bytes 786432 | tf_op jit(solution)/shard_map/pallas_call | solution.py:115
  6.3 0.0 collective-permute-done.refs_5_.refs_1_
  6.3 0.0 copy-start
  6.3 3.1 %collective-permute-start.1 = (bf16[1,2,128,128]{3,2,1,0:T(8,128)(2,1)S(1)}, bf16[1,2,128,128]{3,2,1,0:T(8,128)(2,1)S(1)}, u32[]{:S(2)}, u32[]{:S(2)}) collective-permute-start(bf16[1,2,128,128]{3,2,1,0:T(8,128)(2,1)S(1)} %get-tuple-element.25), channel_id=1, source_target_pairs={{0,2},{1,3},{2,0},{3,1},{4,6},{5,7},{6,4},{7,5},{8,10},{9,11},{10,... | collective-permute-start | bytes 196616 | tf_op jit(solution)/shard_map/ppermute | solution.py:168
  9.4 1.4 %collective-permute-start.2 = (bf16[1,2,128,128]{3,2,1,0:T(8,128)(2,1)S(1)}, bf16[1,2,128,128]{3,2,1,0:T(8,128)(2,1)S(1)}, u32[]{:S(2)}, u32[]{:S(2)}) collective-permute-start(bf16[1,2,128,128]{3,2,1,0:T(8,128)(2,1)S(1)} %get-tuple-element.26), channel_id=1, source_target_pairs={{0,3},{1,2},{2,1},{3,0},{4,7},{5,6},{6,5},{7,4},{8,11},{9,10},{10,... | collective-permute-start | bytes 196616 | tf_op jit(solution)/shard_map/ppermute | solution.py:168
  10.8 0.2 collective-permute-start.3
  11.0 0.0 collective-permute-done.5.refs_7_.refs_1_
  11.0 0.0 collective-permute-done.4.refs_6_.refs_0_
  11.0 2.2 %collective-permute-done.1.refs_1_ = bf16[1,2,128,128]{3,2,1,0:T(8,128)(2,1)S(1)} collective-permute-done((bf16[1,2,128,128]{3,2,1,0:T(8,128)(2,1)S(1)}, bf16[1,2,128,128]{3,2,1,0:T(8,128)(2,1)S(1)}, u32[]{:S(2)}, u32[]{:S(2)}) %collective-permute-start.1) | collective-permute-done | bytes 65568 | tf_op jit(solution)/shard_map/ppermute | solution.py:168
  13.2 2.5 %collective-permute-done.2.refs_2_ = bf16[1,2,128,128]{3,2,1,0:T(8,128)(2,1)S(1)} collective-permute-done((bf16[1,2,128,128]{3,2,1,0:T(8,128)(2,1)S(1)}, bf16[1,2,128,128]{3,2,1,0:T(8,128)(2,1)S(1)}, u32[]{:S(2)}, u32[]{:S(2)}) %collective-permute-start.2) | collective-permute-done | bytes 65568 | tf_op jit(solution)/shard_map/ppermute | solution.py:168
  15.6 0.1 collective-permute-done.3.refs_3_
  15.7 0.0 copy-done.1
  15.7 0.4 %shard_map.61.refs_2_ = f32[1,2,128,256]{3,2,1,0:T(8,128)S(1)} custom-call(bf16[1,2,128,128]{3,2,1,0:T(8,128)(2,1)S(1)} %get-tuple-element.24.refs_0_, bf16[1,2,128,128]{3,2,1,0:T(8,128)(2,1)S(1)} %collective-permute-done.1.refs_1_, bf16[1,2,128,128]{3,2,1,0:T(8,128)(2,1)S(1)} %collective-permute-done.2.refs_2_, ...), custom_call_target="tpu_custom_call" | custom-call | bytes 786432 | tf_op jit(solution)/shard_map/pallas_call | solution.py:115
  16.1 0.1 collective-permute-start.6
  16.2 1.6 %collective-permute-start.7 = (f32[1,2,128,256]{3,2,1,0:T(8,128)S(1)}, f32[1,2,128,256]{3,2,1,0:T(8,128)S(1)}, u32[]{:S(2)}, u32[]{:S(2)}) collective-permute-start(f32[1,2,128,256]{3,2,1,0:T(8,128)S(1)} %shard_map.61.refs_2_), channel_id=1, source_target_pairs={{0,8},{4,12},{8,0},{12,4},{1,9},{5,13},{9,1},{13,5},{2,10},{6,14},... | collective-permute-start | bytes 786440 | tf_op jit(solution)/shard_map/ppermute | solution.py:154
  17.8 0.0 collective-permute-done.6.refs_3_
  17.8 0.0 copy-done
  17.8 1.1 %shard_map.62 = (f32[1,2,256,256]{3,2,1,0:T(8,128)S(1)}, f32[1,2,128,256]{3,2,1,0:T(8,128)}) custom-call(f32[1,2,256,256]{3,2,1,0:T(8,128)S(1)} %copy-done, bf16[1,2,1,128,256]{4,3,2,1,0:T(8,128)(2,1)S(1)} %bitcast.9, bf16[1,2,1,128,256]{4,3,2,1,0:T(8,128)(2,1)S(1)} %collective-permute-done.refs_5_.refs_1_, f32[1,2,128,256]{3,2,1,0:T(8,128)S(1)} %shard_map.61.refs_2_, ...), custom_call_target="tpu_custom_call" | custom-call | bytes 1310720 | tf_op jit(solution)/shard_map/pallas_call | solution.py:115
  18.9 6.0 %collective-permute-done.7.refs_2_ = f32[1,2,128,256]{3,2,1,0:T(8,128)S(1)} collective-permute-done((f32[1,2,128,256]{3,2,1,0:T(8,128)S(1)}, f32[1,2,128,256]{3,2,1,0:T(8,128)S(1)}, u32[]{:S(2)}, u32[]{:S(2)}) %collective-permute-start.7) | collective-permute-done | bytes 262176 | tf_op jit(solution)/shard_map/ppermute | solution.py:154
  24.9 0.0 collective-permute-start.8
  24.9 1.5 %collective-permute-done.8.refs_3_ = f32[1,2,128,256]{3,2,1,0:T(8,128)S(1)} collective-permute-done((f32[1,2,128,256]{3,2,1,0:T(8,128)S(1)}, f32[1,2,128,256]{3,2,1,0:T(8,128)S(1)}, u32[]{:S(2)}, u32[]{:S(2)}) %collective-permute-start.8) | collective-permute-done | bytes 262176 | tf_op jit(solution)/shard_map/ppermute | solution.py:157
  26.5 1.3 %shard_map.63 = f32[1,2,256,256]{3,2,1,0:T(8,128)} custom-call(f32[1,2,256,256]{3,2,1,0:T(8,128)S(1)} %get-tuple-element.30.base, bf16[1,2,1,128,256]{4,3,2,1,0:T(8,128)(2,1)S(1)} %collective-permute-done.4.refs_6_.refs_0_, bf16[1,2,1,128,256]{4,3,2,1,0:T(8,128)(2,1)S(1)} %collective-permute-done.5.refs_7_.refs_1_, ...), custom_call_target="tpu_custom_call" | custom-call | bytes 1310720 | tf_op jit(solution)/shard_map/pallas_call | solution.py:115
Async XLA Ops:
  0.6 5.7 %collective-permute-start = (bf16[1,2,1,128,256]{4,3,2,1,0:T(8,128)(2,1)}, bf16[1,2,1,128,256]{4,3,2,1,0:T(8,128)(2,1)S(1)}, u32[]{:S(2)}, u32[]{:S(2)}) collective-permute-start(bf16[1,2,1,128,256]{4,3,2,1,0:T(8,128)(2,1)} %bitcast.5), channel_id=1, source_target_pairs={{0,4},{4,0},{8,12},{12,8},{1,5},{5,1},{9,13},{13,9},{2,6},{6,2},{1... | collective-permute-start | bytes 393224 | tf_op jit(solution)/shard_map/ppermute | solution.py:163
  1.1 9.9 %collective-permute-start.5 = (bf16[1,2,1,128,256]{4,3,2,1,0:T(8,128)(2,1)}, bf16[1,2,1,128,256]{4,3,2,1,0:T(8,128)(2,1)S(1)}, u32[]{:S(2)}, u32[]{:S(2)}) collective-permute-start(bf16[1,2,1,128,256]{4,3,2,1,0:T(8,128)(2,1)} %bitcast.6), channel_id=1, source_target_pairs={{0,12},{4,8},{8,4},{12,0},{1,13},{5,9},{9,5},{13,1},{2,14},{6,10},... | collective-permute-start | bytes 393224 | tf_op jit(solution)/shard_map/ppermute | solution.py:169
  3.8 7.2 %collective-permute-start.4 = (bf16[1,2,1,128,256]{4,3,2,1,0:T(8,128)(2,1)}, bf16[1,2,1,128,256]{4,3,2,1,0:T(8,128)(2,1)S(1)}, u32[]{:S(2)}, u32[]{:S(2)}) collective-permute-start(bf16[1,2,1,128,256]{4,3,2,1,0:T(8,128)(2,1)} %bitcast.7), channel_id=1, source_target_pairs={{0,8},{4,12},{8,0},{12,4},{1,9},{5,13},{9,1},{13,5},{2,10},{6,14},... | collective-permute-start | bytes 393224 | tf_op jit(solution)/shard_map/ppermute | solution.py:169
  3.8 0.7 %copy-start.3 = (s32[4,4,128]{2,1,0:T(4,128)S(1)}, s32[4,4,128]{2,1,0:T(4,128)}, u32[]{:S(2)}) copy-start(s32[4,4,128]{2,1,0:T(4,128)} %row_lists.1) | copy-start | bytes 24580
  4.6 1.0 %copy-start.2 = (bf16[2,1,1,256,1,1,256]{6,3,5,4,2,1,0:T(8,128)(2,1)S(1)}, bf16[2,1,1,256,1,1,256]{6,3,5,4,2,1,0:T(8,128)(2,1)}, u32[]{:S(2)}) copy-start(bf16[2,1,1,256,1,1,256]{6,3,5,4,2,1,0:T(8,128)(2,1)} %param.4) | copy-start | bytes 786436
  5.6 10.2 %copy-start.1 = (bf16[1,2,1,1,128,256]{5,4,3,2,1,0:T(8,128)(2,1)S(1)}, bf16[1,2,1,1,128,256]{5,4,3,2,1,0:T(8,128)(2,1)}, u32[]{:S(2)}) copy-start(bf16[1,2,1,1,128,256]{5,4,3,2,1,0:T(8,128)(2,1)} %param.5) | copy-start | bytes 393220
  6.3 11.5 %copy-start = (f32[1,2,256,256]{3,2,1,0:T(8,128)S(1)}, f32[1,2,256,256]{3,2,1,0:T(8,128)}, u32[]{:S(2)}) copy-start(f32[1,2,256,256]{3,2,1,0:T(8,128)} %base.1) | copy-start | bytes 1572868
  6.3 6.9 %collective-permute-start.1 = (bf16[1,2,128,128]{3,2,1,0:T(8,128)(2,1)S(1)}, bf16[1,2,128,128]{3,2,1,0:T(8,128)(2,1)S(1)}, u32[]{:S(2)}, u32[]{:S(2)}) collective-permute-start(bf16[1,2,128,128]{3,2,1,0:T(8,128)(2,1)S(1)} %get-tuple-element.25), channel_id=1, source_target_pairs={{0,2},{1,3},{2,0},{3,1},{4,6},{5,7},{6,4},{7,5},{8,10},{9,11},{10,... | collective-permute-start | bytes 196616 | tf_op jit(solution)/shard_map/ppermute | solution.py:168
  9.4 6.2 %collective-permute-start.2 = (bf16[1,2,128,128]{3,2,1,0:T(8,128)(2,1)S(1)}, bf16[1,2,128,128]{3,2,1,0:T(8,128)(2,1)S(1)}, u32[]{:S(2)}, u32[]{:S(2)}) collective-permute-start(bf16[1,2,128,128]{3,2,1,0:T(8,128)(2,1)S(1)} %get-tuple-element.26), channel_id=1, source_target_pairs={{0,3},{1,2},{2,1},{3,0},{4,7},{5,6},{6,5},{7,4},{8,11},{9,10},{10,... | collective-permute-start | bytes 196616 | tf_op jit(solution)/shard_map/ppermute | solution.py:168
  10.8 5.0 %collective-permute-start.3 = (bf16[1,2,128,128]{3,2,1,0:T(8,128)(2,1)S(1)}, bf16[1,2,128,128]{3,2,1,0:T(8,128)(2,1)S(1)}, u32[]{:S(2)}, u32[]{:S(2)}) collective-permute-start(bf16[1,2,128,128]{3,2,1,0:T(8,128)(2,1)S(1)} %get-tuple-element.27), channel_id=1, source_target_pairs={{0,1},{1,0},{2,3},{3,2},{4,5},{5,4},{6,7},{7,6},{8,9},{9,8},{10,11... | collective-permute-start | bytes 196616 | tf_op jit(solution)/shard_map/ppermute | solution.py:168
  16.1 1.7 %collective-permute-start.6 = (f32[1,2,128,256]{3,2,1,0:T(8,128)S(1)}, f32[1,2,128,256]{3,2,1,0:T(8,128)S(1)}, u32[]{:S(2)}, u32[]{:S(2)}) collective-permute-start(f32[1,2,128,256]{3,2,1,0:T(8,128)S(1)} %shard_map.61.refs_2_), channel_id=1, source_target_pairs={{0,4},{4,0},{8,12},{12,8},{1,5},{5,1},{9,13},{13,9},{2,6},{6,2},{1... | collective-permute-start | bytes 786440 | tf_op jit(solution)/shard_map/ppermute | solution.py:157
  16.2 8.7 %collective-permute-start.7 = (f32[1,2,128,256]{3,2,1,0:T(8,128)S(1)}, f32[1,2,128,256]{3,2,1,0:T(8,128)S(1)}, u32[]{:S(2)}, u32[]{:S(2)}) collective-permute-start(f32[1,2,128,256]{3,2,1,0:T(8,128)S(1)} %shard_map.61.refs_2_), channel_id=1, source_target_pairs={{0,8},{4,12},{8,0},{12,4},{1,9},{5,13},{9,1},{13,5},{2,10},{6,14},... | collective-permute-start | bytes 786440 | tf_op jit(solution)/shard_map/ppermute | solution.py:154
  24.9 1.5 %collective-permute-start.8 = (f32[1,2,128,256]{3,2,1,0:T(8,128)S(1)}, f32[1,2,128,256]{3,2,1,0:T(8,128)S(1)}, u32[]{:S(2)}, u32[]{:S(2)}) collective-permute-start(f32[1,2,128,256]{3,2,1,0:T(8,128)S(1)} %collective-permute-done.7.refs_2_), channel_id=1, source_target_pairs={{0,4},{4,0},{8,12},{12,8},{1,5},{5,1},{9,13},{13,9},{2,6},{6,2},{1... | collective-permute-start | bytes 786440 | tf_op jit(solution)/shard_map/ppermute | solution.py:157

commit v3 on v0

v3 whole, which is shorter than its diff:
```python
import collections
import functools
import typing

import jax
import jax.numpy as jnp
from jax import lax
from jax.experimental import pallas as pl
from jax.experimental.pallas import tpu as pltpu
from jax.sharding import PartitionSpec as P

VMEM = pl.BlockSpec(memory_space=pltpu.VMEM)
HBM = pl.BlockSpec(memory_space=pltpu.HBM)
VMEM_BYTES = 24 * 1024 * 1024
STEPS_PER_OCTAVE = 64


class Sizes(typing.NamedTuple):
    grid_rows: int
    grid_cols: int
    nodes: int
    row_blocks: int
    col_blocks: int
    kept: int
    width: int

    @property
    def rows(self):
        return self.row_blocks * self.kept

    @property
    def total(self):
        return self.row_blocks * self.grid_rows * self.kept


def partners(size, step):
    return [(place, place ^ step) for place in range(size)]


def dot(lhs, rhs, contract):
    return lax.dot_general(
        lhs, rhs, (((contract[0],), (contract[1],)), ((), ())), preferred_element_type=jnp.float32
    )


def place_one_hot(picks, width):
    kept = picks.shape[-1]
    spots = lax.broadcasted_iota(jnp.int32, (width, kept), 0)
    return jnp.where(spots == picks, 1.0, 0.0).astype(jnp.bfloat16)


def first_kernel(result):
    result[...] = jnp.zeros_like(result)


def pick_kernel(sizes, surface, row_lists, token, *pieces):
    del token
    row_place = lax.axis_index("row")
    col_place = lax.axis_index("col")
    kept = sizes.kept
    for slot in range(sizes.grid_cols * sizes.nodes):
        step, node = slot // sizes.nodes, slot % sizes.nodes
        which = jnp.bitwise_xor(col_place, step) * sizes.nodes + node

        def choice(block):
            return place_one_hot(row_lists[which, pl.ds(block, 1), :], sizes.width)

        for row_block in range(sizes.row_blocks):
            row_choice = choice(row_block * sizes.grid_rows + row_place)
            for col_block in range(sizes.col_blocks):
                col_choice = choice(col_block * sizes.grid_cols + col_place)
                for half in range(2):
                    block = surface[half, row_block, col_block]
                    taken = dot(row_choice, block, (0, 0)).astype(jnp.bfloat16)
                    taken = dot(taken, col_choice, (1, 0))
                    pieces[step][
                        node,
                        half,
                        row_block * kept : (row_block + 1) * kept,
                        col_block * kept : (col_block + 1) * kept,
                    ] = taken.astype(jnp.bfloat16)


def block_at(sizes, block):
    return pl.ds(pl.multiple_of(block * sizes.kept, sizes.kept), sizes.kept)


def gather_factor(sizes, factors, whole_factor):
    row_place = lax.axis_index("row")
    for node in range(sizes.nodes):
        for step in range(sizes.grid_rows):
            source = jnp.bitwise_xor(row_place, step)
            for block in range(sizes.row_blocks):
                spot = block_at(sizes, block * sizes.grid_rows + source)
                whole_factor[node, spot, : sizes.width] = factors[step][node, 0, block]
                whole_factor[node, spot, sizes.width :] = factors[step][node, 1, block]


def minus_product(sizes, node, steps, pieces, whole_factor):
    width, rows = sizes.width, sizes.rows
    col_place = lax.axis_index("col")
    surfaces, factors = [], []
    for step in steps:
        source = jnp.bitwise_xor(col_place, step)
        surfaces.append(jnp.concatenate([pieces[step][node, 0], pieces[step][node, 1]], axis=0))
        for block in range(sizes.col_blocks):
            factors.append(whole_factor[node, block_at(sizes, block * sizes.grid_cols + source), :])
    product = dot(jnp.concatenate(surfaces, axis=1), jnp.concatenate(factors, axis=0), (1, 0))
    real = product[rows:, width:] - product[:rows, :width]
    imag = -(product[:rows, width:] + product[rows:, :width])
    return real, imag


def encode(real, imag, coded):
    rows = real.shape[0]
    most = jnp.max(jnp.maximum(jnp.abs(real), jnp.abs(imag)), axis=0, keepdims=True)
    level = jnp.ceil(jnp.log2(jnp.maximum(most, 1e-30)) * STEPS_PER_OCTAVE + 0.1)
    scale = jnp.exp2(15.0 - level / STEPS_PER_OCTAVE)
    coded[:rows, :] = jnp.round(real * scale).astype(jnp.int32).astype(jnp.int16)
    coded[rows : 2 * rows, :] = jnp.round(imag * scale).astype(jnp.int32).astype(jnp.int16)
    levels = jnp.broadcast_to(level, (16, level.shape[1]))
    coded[2 * rows :, :] = levels.astype(jnp.int32).astype(jnp.int16)


def decode(coded):
    rows = coded.shape[0] // 2 - 8
    level = coded[2 * rows :, :].astype(jnp.int32).astype(jnp.float32)[:1]
    scale = jnp.exp2(level / STEPS_PER_OCTAVE - 15.0)
    values = coded[: 2 * rows, :].astype(jnp.int32).astype(jnp.float32) * scale
    return jnp.concatenate([values[:rows], values[rows:]], axis=1)


def factor_times(sizes, node, steps, blocks, whole_factor):
    width = sizes.width
    row_place = lax.axis_index("row")
    lefts, rights = [], []
    for step, wide in zip(steps, blocks):
        source = jnp.bitwise_xor(row_place, step)
        spots = [block_at(sizes, b * sizes.grid_rows + source) for b in range(sizes.row_blocks)]
        factor = jnp.concatenate([whole_factor[node, spot, :] for spot in spots], axis=0)
        high = wide.astype(jnp.bfloat16)
        low = (wide - high.astype(jnp.float32)).astype(jnp.bfloat16)
        lefts += [factor, factor]
        rights += [high, low]
    product = dot(jnp.concatenate(lefts, axis=0), jnp.concatenate(rights, axis=0), (0, 0))
    real = product[:width, :width] - product[width:, width:]
    imag = product[:width, width:] + product[width:, :width]
    return real, imag


def block_kernel(sizes, pieces, factors, block, coded, whole_factor):
    gather_factor(sizes, factors, whole_factor)
    for node in range(sizes.nodes):
        real, imag = minus_product(sizes, node, sorted(pieces), pieces, whole_factor)
        block[node, 0] = real
        block[node, 1] = imag
        encode(real, imag, coded.at[node])


def near_kernel(sizes, base, whole_factor, own, mate, result, kept_block):
    kept_block[...] = own[...]
    for node in range(sizes.nodes):
        blocks = [jnp.concatenate([b[node, 0], b[node, 1]], axis=1) for b in (own, mate)]
        real, imag = factor_times(sizes, node, (0, 1), blocks, whole_factor)
        result[node, 0] = base[node, 0] - real
        result[node, 1] = base[node, 1] - imag


def far_kernel(sizes, before, whole_factor, coded, result):
    for node in range(sizes.nodes):
        blocks = [decode(coded[step].at[node]) for step in coded]
        real, imag = factor_times(sizes, node, list(coded), blocks, whole_factor)
        result[node, 0] = before[node, 0] - real
        result[node, 1] = before[node, 1] - imag


def call(kernel, out_shape, *args):
    flat, tree = jax.tree.flatten(args)
    out_flat, out_tree = jax.tree.flatten(out_shape)

    def flat_kernel(*refs):
        ins = jax.tree.unflatten(tree, refs[: len(flat)])
        kernel(*ins, *refs[len(flat) :])

    outs = pl.pallas_call(
        flat_kernel,
        out_shape=out_flat,
        in_specs=[VMEM] * len(flat),
        out_specs=[VMEM] * len(out_flat),
        compiler_params=pltpu.CompilerParams(vmem_limit_bytes=VMEM_BYTES),
    )(*flat)
    return jax.tree.unflatten(out_tree, outs)


def local(inverse_top, factor, diag_inverse, row_lists):
    grid_rows = lax.axis_size("row")
    grid_cols = lax.axis_size("col")
    nodes, _, row_blocks, _, kept, width = factor.shape
    col_blocks = inverse_top.shape[4]
    sizes = Sizes(grid_rows, grid_cols, nodes, row_blocks, col_blocks, kept, width)
    rows = sizes.rows
    surface = inverse_top.transpose(0, 1, 2, 4, 5, 3, 6).reshape(
        2, row_blocks, col_blocks, width, width
    )
    own_factor = factor.reshape(nodes, 2, row_blocks, kept, width)
    narrow, wide = jnp.bfloat16, jnp.float32
    work = jax.ShapeDtypeStruct((nodes, 2, rows, width), wide)
    coded = jax.ShapeDtypeStruct((nodes, 2 * rows + 16, width), jnp.int16)
    square = jax.ShapeDtypeStruct((nodes, 2, width, width), wide)
    across = range(2, grid_rows, 2)

    def over_rows(block, step):
        return lax.ppermute(block, "row", partners(grid_rows, step))

    whole = jax.ShapeDtypeStruct((nodes, sizes.total, 2 * width), narrow)
    piece = jax.ShapeDtypeStruct((nodes, 2, rows, col_blocks * kept), narrow)
    token = pl.pallas_call(
        first_kernel,
        out_shape=pltpu.VMEM((8, 128), wide),
        out_specs=VMEM,
        cost_estimate=pl.CostEstimate(flops=10**10, bytes_accessed=10**8, transcendentals=0),
    )()
    token, far_factor = lax.optimization_barrier((token, own_factor))
    pieces = pl.pallas_call(
        functools.partial(pick_kernel, sizes),
        out_shape=[piece] * grid_cols,
        in_specs=[VMEM, VMEM, pl.BlockSpec(memory_space=pl.ANY)],
        out_specs=[VMEM] * grid_cols,
        compiler_params=pltpu.CompilerParams(vmem_limit_bytes=VMEM_BYTES),
    )(surface, row_lists, token)
    factors = collections.OrderedDict({0: own_factor})
    factors.update({step: over_rows(far_factor, step) for step in range(1, grid_rows)})
    factors[1], pieces = lax.optimization_barrier((factors[1], pieces))
    steps = [*range(grid_cols // 2, grid_cols), *range(grid_cols // 2 - 1, 0, -1)]
    arrived = collections.OrderedDict({0: pieces[0]})
    for step in steps:
        arrived[step] = lax.ppermute(pieces[step], "col", partners(grid_cols, step))
    block, coded, whole_factor = call(
        functools.partial(block_kernel, sizes),
        [work, coded, whole],
        arrived, factors,
    )
    sent = collections.OrderedDict((step, over_rows(coded, step)) for step in across)
    near, inverse_block = call(
        functools.partial(near_kernel, sizes),
        [square, work],
        diag_inverse,
        whole_factor,
        block,
        over_rows(block, 1),
    )
    near, sent = lax.optimization_barrier((near, sent))
    forwarded = collections.OrderedDict((step + 1, over_rows(sent[step], 1)) for step in across)
    (middle,) = call(functools.partial(far_kernel, sizes), [square], near, whole_factor, sent)
    (diagonal_block,) = call(
        functools.partial(far_kernel, sizes), [square], middle, whole_factor, forwarded
    )
    return (
        inverse_block.reshape(nodes, 2, row_blocks, 1, kept, width),
        diagonal_block,
    )


def solution(mesh):
    placed = (
        P("pole", None, "row", None, None, "col", None),
        P("col", "pole", None, "row", None, None),
        P("col", "pole", None, None),
        P(),
    )
    return jax.shard_map(
        local,
        mesh=mesh,
        in_specs=placed,
        out_specs=(P("col", "pole", None, "row", None, None), P("col", "pole", None, None)),
        check_vma=False,
    )
```

time: 131 us -> 24 us (0.18)
  waiting for transfers between devices: 71.7 us -> 9.12 us
  local copies, waits for them, and re-layouts: 14.8 us -> 0.88 us
  between operations: 14.1 us -> 0.72 us
  blocking collectives: 8.86 us -> 0 us
  loops' own time: 8.23 us -> 0 us
  matrix products: 4.61 us -> 0 us
  starting transfers between devices: 5.05 us -> 9.46 us
  Pallas kernels: 0 us -> 3.68 us
  other arithmetic: 3.18 us -> 0 us
    psum x1 -> x0, waiting for transfers between devices: 30.8 us -> none  [local(): totals = lax.psum(local_terms, 'row')]
    reduce_scatter x1 -> x0, waiting for transfers between devices: 25.9 us -> none  [local(): lax.psum_scatter(lax.map(per_node, jnp.arange(local_nodes * lax.axis_size...]
    all_to_all x1 -> x0, waiting for transfers between devices: 15 us -> none  [local(): lax.all_to_all(grouped, 'col', split_axis=3, concat_axis=0, tiled=True)]
    ppermute x0 -> x9, starting transfers between devices: none -> 9.46 us  [the longest x6 4.74 us: over_rows(): return lax.ppermute(block, 'row', partners(grid_rows, step))]
    ppermute x0 -> x9, waiting for transfers between devices: none -> 9.12 us  [the longest x6 5.79 us: over_rows(): return lax.ppermute(block, 'row', partners(grid_rows, step))]
    all_gather x1 -> x0, blocking collectives: 8.86 us -> none  [local(): gathered = lax.all_gather(factor, 'row', axis=3, tiled=True)]
    another operation x1 -> x0, loops' own time: 8.23 us -> none  [local(): lax.map(per_node, jnp.arange(local_nodes * lax.axis_size('col'), dtype=jn...]
    all_to_all x1 -> x0, starting transfers between devices: 5 us -> none  [local(): lax.all_to_all(grouped, 'col', split_axis=3, concat_axis=0, tiled=True)]
  transfers between devices with their start and end apart: 3 -> 9, of which waited for: 3 -> 6; matrix products, arithmetic and copies ran while one was open for 0% -> 0% of each run, Pallas kernels for 0% -> 9%
where the time goes in v3:
time: 24 us; the launch traced here: 23.9 us
  starting transfers between devices  9.46 us (39%)
  waiting for transfers between devices  9.12 us (38%)
  Pallas kernels  3.68 us (15%)
  local copies, waits for them, and re-layouts  0.88 us (4%)
  between operations  0.72 us (3%)
    ppermute x6, waiting for transfers between devices, over_rows(): return lax.ppermute(block, 'row', partners(grid_rows, step))  5.79 us
    ppermute x6, starting transfers between devices, over_rows(): return lax.ppermute(block, 'row', partners(grid_rows, step))  4.74 us
    ppermute x3, starting transfers between devices, local(): arrived[step] = lax.ppermute(pieces[step], 'col', partners(grid_cols, step))  4.72 us
    ppermute x3, waiting for transfers between devices, local(): arrived[step] = lax.ppermute(pieces[step], 'col', partners(grid_cols, step))  3.33 us
    pallas_call x4, Pallas kernels, call(): pl.pallas_call(flat_kernel, out_shape=out_flat, in_specs=[VMEM] * len(fla...  2.99 us
    unnamed x8, local copies, waits for them, and re-layouts  0.88 us
    pallas_call x1, Pallas kernels, local(): pl.pallas_call(functools.partial(pick_kernel, sizes), out_shape=[piece] *...  0.69 us
  transfers between devices with their start and end apart: 9, of which 6 were waited for; matrix products, arithmetic and copies ran while one was open for 0% of the time, Pallas kernels for 9%

profile of v3, /device:TPU:0, one launch (start us, length us, event | category | flops | bytes accessed | tf_op | source)
XLA Modules:
  0.0 23.9 jit_solution(11608304457352797544)
XLA Ops:
  0.6 0.0 copy-start.2
  0.6 0.0 copy-start.1
  0.6 0.0 copy-start.3
  0.7 0.9 %copy-done.2 = bf16[1,2,1,1,128,256]{5,4,3,2,1,0:T(8,128)(2,1)S(1)} copy-done((bf16[1,2,1,1,128,256]{5,4,3,2,1,0:T(8,128)(2,1)S(1)}, bf16[1,2,1,1,128,256]{5,4,3,2,1,0:T(8,128)(2,1)}, u32[]{:S(2)}) %copy-start.2) | copy-done | bytes 131096
  1.5 0.5 %collective-permute-start = (bf16[1,2,1,128,256]{4,3,2,1,0:T(8,128)(2,1)S(1)}, bf16[1,2,1,128,256]{4,3,2,1,0:T(8,128)(2,1)S(1)}, u32[]{:S(2)}, u32[]{:S(2)}) collective-permute-start(bf16[1,2,1,128,256]{4,3,2,1,0:T(8,128)(2,1)S(1)} %bitcast.6), channel_id=1, source_target_pairs={{0,4},{4,0},{8,12},{12,8},{1,5},{5,1},{9,13},{13,9},{2,6},{6,2},{1... | collective-permute-start | bytes 393224 | tf_op jit(solution)/shard_map/ppermute | solution.py:213
  2.0 2.6 %collective-permute-start.5 = (bf16[1,2,1,128,256]{4,3,2,1,0:T(8,128)(2,1)S(1)}, bf16[1,2,1,128,256]{4,3,2,1,0:T(8,128)(2,1)S(1)}, u32[]{:S(2)}, u32[]{:S(2)}) collective-permute-start(bf16[1,2,1,128,256]{4,3,2,1,0:T(8,128)(2,1)S(1)} %bitcast.7), channel_id=1, source_target_pairs={{0,12},{4,8},{8,4},{12,0},{1,13},{5,9},{9,5},{13,1},{2,14},{6,10},... | collective-permute-start | bytes 393224 | tf_op jit(solution)/shard_map/ppermute | solution.py:213
  4.6 0.0 collective-permute-start.4
  4.6 0.0 copy-done.1
  4.6 0.0 copy-done.3
  4.6 0.0 copy-start
  4.6 0.7 %shard_map.60 = (bf16[1,2,128,128]{3,2,1,0:T(8,128)(2,1)S(1)}, bf16[1,2,128,128]{3,2,1,0:T(8,128)(2,1)S(1)}, bf16[1,2,128,128]{3,2,1,0:T(8,128)(2,1)S(1)}, bf16[1,2,128,128]{3,2,1,0:T(8,128)(2,1)S(1)}) custom-call(bf16[2,1,1,256,256]{4,3,2,1,0:T(8,128)(2,1)S(1)} %bitcast.5, s32[4,4,128]{2,1,0:T(4,128)S(1)} %copy-done.3, f32[8,128]{1,0:T(8,128)S(1)} %shard_map.59.token), custom_call_target="tpu_custom_call" | custom-call | tf_op jit(solution)/shard_map/pallas_call | solution.py:224
  5.3 0.0 collective-permute-done.refs_5_
  5.4 3.1 %collective-permute-start.1 = (bf16[1,2,128,128]{3,2,1,0:T(8,128)(2,1)S(1)}, bf16[1,2,128,128]{3,2,1,0:T(8,128)(2,1)S(1)}, u32[]{:S(2)}, u32[]{:S(2)}) collective-permute-start(bf16[1,2,128,128]{3,2,1,0:T(8,128)(2,1)S(1)} %get-tuple-element.27), channel_id=1, source_target_pairs={{0,2},{1,3},{2,0},{3,1},{4,6},{5,7},{6,4},{7,5},{8,10},{9,11},{10,... | collective-permute-start | bytes 196616 | tf_op jit(solution)/shard_map/ppermute | solution.py:237
  8.5 1.3 %collective-permute-start.2 = (bf16[1,2,128,128]{3,2,1,0:T(8,128)(2,1)S(1)}, bf16[1,2,128,128]{3,2,1,0:T(8,128)(2,1)S(1)}, u32[]{:S(2)}, u32[]{:S(2)}) collective-permute-start(bf16[1,2,128,128]{3,2,1,0:T(8,128)(2,1)S(1)} %get-tuple-element.28), channel_id=1, source_target_pairs={{0,3},{1,2},{2,1},{3,0},{4,7},{5,6},{6,5},{7,4},{8,11},{9,10},{10,... | collective-permute-start | bytes 196616 | tf_op jit(solution)/shard_map/ppermute | solution.py:237
  9.8 0.2 collective-permute-start.3
  10.1 0.0 collective-permute-done.5.refs_7_
  10.1 1.4 %collective-permute-done.4.refs_6_ = bf16[1,2,1,128,256]{4,3,2,1,0:T(8,128)(2,1)S(1)} collective-permute-done((bf16[1,2,1,128,256]{4,3,2,1,0:T(8,128)(2,1)S(1)}, bf16[1,2,1,128,256]{4,3,2,1,0:T(8,128)(2,1)S(1)}, u32[]{:S(2)}, u32[]{:S(2)}) %collective-permute-start.4) | collective-permute-done | bytes 131104 | tf_op jit(solution)/shard_map/ppermute | solution.py:213
  11.5 0.8 %collective-permute-done.1.refs_1_ = bf16[1,2,128,128]{3,2,1,0:T(8,128)(2,1)S(1)} collective-permute-done((bf16[1,2,128,128]{3,2,1,0:T(8,128)(2,1)S(1)}, bf16[1,2,128,128]{3,2,1,0:T(8,128)(2,1)S(1)}, u32[]{:S(2)}, u32[]{:S(2)}) %collective-permute-start.1) | collective-permute-done | bytes 65568 | tf_op jit(solution)/shard_map/ppermute | solution.py:237
  12.2 2.5 %collective-permute-done.2.refs_2_ = bf16[1,2,128,128]{3,2,1,0:T(8,128)(2,1)S(1)} collective-permute-done((bf16[1,2,128,128]{3,2,1,0:T(8,128)(2,1)S(1)}, bf16[1,2,128,128]{3,2,1,0:T(8,128)(2,1)S(1)}, u32[]{:S(2)}, u32[]{:S(2)}) %collective-permute-start.2) | collective-permute-done | bytes 65568 | tf_op jit(solution)/shard_map/ppermute | solution.py:237
  14.7 0.1 collective-permute-done.3.refs_3_
  14.8 0.4 %shard_map.61 = (f32[1,2,128,256]{3,2,1,0:T(8,128)S(1)}, s16[1,272,256]{2,1,0:T(8,128)(2,1)S(1)}, bf16[1,512,512]{2,1,0:T(8,128)(2,1)S(1)}) custom-call(bf16[1,2,128,128]{3,2,1,0:T(8,128)(2,1)S(1)} %get-tuple-element.26.refs_0_, bf16[1,2,128,128]{3,2,1,0:T(8,128)(2,1)S(1)} %collective-permute-done.1.refs_1_, ...), custom_call_target="tpu_custom_call" | custom-call | tf_op jit(solution)/shard_map/pallas_call | solution.py:185
  15.2 0.1 collective-permute-start.6
  15.3 1.6 %collective-permute-start.7 = (s16[1,272,256]{2,1,0:T(8,128)(2,1)S(1)}, s16[1,272,256]{2,1,0:T(8,128)(2,1)S(1)}, u32[]{:S(2)}, u32[]{:S(2)}) collective-permute-start(s16[1,272,256]{2,1,0:T(8,128)(2,1)S(1)} %get-tuple-element.35), channel_id=1, source_target_pairs={{0,8},{4,12},{8,0},{12,4},{1,9},{5,13},{9,1},{13,5},{2,10},{6,14},... | collective-permute-start | bytes 417800 | tf_op jit(solution)/shard_map/ppermute | solution.py:213
  16.9 0.0 collective-permute-done.6.refs_3_
  16.9 0.0 copy-done
  16.9 1.1 %shard_map.62 = (f32[1,2,256,256]{3,2,1,0:T(8,128)S(1)}, f32[1,2,128,256]{3,2,1,0:T(8,128)}) custom-call(f32[1,2,256,256]{3,2,1,0:T(8,128)S(1)} %copy-done, bf16[1,512,512]{2,1,0:T(8,128)(2,1)S(1)} %get-tuple-element.31.refs_1_, f32[1,2,128,256]{3,2,1,0:T(8,128)S(1)} %get-tuple-element.32.refs_2_, f32[1,2,128,256]{3,2,1,0:T(8,128)S(1)} %collective-permute-done.6.refs_3_), custom_call_target="tpu_custom_call" | custom-call | tf_op jit(solution)/shard_map/pallas_call | solution.py:185
  18.0 3.4 %collective-permute-done.7.refs_2_ = s16[1,272,256]{2,1,0:T(8,128)(2,1)S(1)} collective-permute-done((s16[1,272,256]{2,1,0:T(8,128)(2,1)S(1)}, s16[1,272,256]{2,1,0:T(8,128)(2,1)S(1)}, u32[]{:S(2)}, u32[]{:S(2)}) %collective-permute-start.7) | collective-permute-done | bytes 139296 | tf_op jit(solution)/shard_map/ppermute | solution.py:213
  21.4 0.0 collective-permute-start.8
  21.4 0.3 %shard_map.63.refs_0_ = f32[1,2,256,256]{3,2,1,0:T(8,128)S(1)} custom-call(f32[1,2,256,256]{3,2,1,0:T(8,128)S(1)} %get-tuple-element.36.refs_0_, bf16[1,512,512]{2,1,0:T(8,128)(2,1)S(1)} %get-tuple-element.31.refs_1_, s16[1,272,256]{2,1,0:T(8,128)(2,1)S(1)} %collective-permute-done.7.refs_2_), custom_call_target="tpu_custom_call" | custom-call | tf_op jit(solution)/shard_map/pallas_call | solution.py:185
  21.7 1.0 %collective-permute-done.8.refs_2_ = s16[1,272,256]{2,1,0:T(8,128)(2,1)S(1)} collective-permute-done((s16[1,272,256]{2,1,0:T(8,128)(2,1)S(1)}, s16[1,272,256]{2,1,0:T(8,128)(2,1)S(1)}, u32[]{:S(2)}, u32[]{:S(2)}) %collective-permute-start.8) | collective-permute-done | bytes 139296 | tf_op jit(solution)/shard_map/ppermute | solution.py:213
  22.7 1.1 %shard_map.64 = f32[1,2,256,256]{3,2,1,0:T(8,128)} custom-call(f32[1,2,256,256]{3,2,1,0:T(8,128)S(1)} %shard_map.63.refs_0_, bf16[1,512,512]{2,1,0:T(8,128)(2,1)S(1)} %get-tuple-element.31.refs_1_, s16[1,272,256]{2,1,0:T(8,128)(2,1)S(1)} %collective-permute-done.8.refs_2_), custom_call_target="tpu_custom_call" | custom-call | tf_op jit(solution)/shard_map/pallas_call | solution.py:185
  (1 shorter events, 0.0 us)
Async XLA Ops:
  0.6 0.9 %copy-start.2 = (bf16[1,2,1,1,128,256]{5,4,3,2,1,0:T(8,128)(2,1)S(1)}, bf16[1,2,1,1,128,256]{5,4,3,2,1,0:T(8,128)(2,1)}, u32[]{:S(2)}) copy-start(bf16[1,2,1,1,128,256]{5,4,3,2,1,0:T(8,128)(2,1)} %param.5) | copy-start | bytes 393220
  0.6 4.0 %copy-start.1 = (bf16[2,1,1,256,1,1,256]{6,3,5,4,2,1,0:T(8,128)(2,1)S(1)}, bf16[2,1,1,256,1,1,256]{6,3,5,4,2,1,0:T(8,128)(2,1)}, u32[]{:S(2)}) copy-start(bf16[2,1,1,256,1,1,256]{6,3,5,4,2,1,0:T(8,128)(2,1)} %param.4) | copy-start | bytes 786436
  0.6 4.0 %copy-start.3 = (s32[4,4,128]{2,1,0:T(4,128)S(1)}, s32[4,4,128]{2,1,0:T(4,128)}, u32[]{:S(2)}) copy-start(s32[4,4,128]{2,1,0:T(4,128)} %row_lists.1) | copy-start | bytes 24580
  1.5 3.8 %collective-permute-start = (bf16[1,2,1,128,256]{4,3,2,1,0:T(8,128)(2,1)S(1)}, bf16[1,2,1,128,256]{4,3,2,1,0:T(8,128)(2,1)S(1)}, u32[]{:S(2)}, u32[]{:S(2)}) collective-permute-start(bf16[1,2,1,128,256]{4,3,2,1,0:T(8,128)(2,1)S(1)} %bitcast.6), channel_id=1, source_target_pairs={{0,4},{4,0},{8,12},{12,8},{1,5},{5,1},{9,13},{13,9},{2,6},{6,2},{1... | collective-permute-start | bytes 393224 | tf_op jit(solution)/shard_map/ppermute | solution.py:213
  2.0 8.1 %collective-permute-start.5 = (bf16[1,2,1,128,256]{4,3,2,1,0:T(8,128)(2,1)S(1)}, bf16[1,2,1,128,256]{4,3,2,1,0:T(8,128)(2,1)S(1)}, u32[]{:S(2)}, u32[]{:S(2)}) collective-permute-start(bf16[1,2,1,128,256]{4,3,2,1,0:T(8,128)(2,1)S(1)} %bitcast.7), channel_id=1, source_target_pairs={{0,12},{4,8},{8,4},{12,0},{1,13},{5,9},{9,5},{13,1},{2,14},{6,10},... | collective-permute-start | bytes 393224 | tf_op jit(solution)/shard_map/ppermute | solution.py:213
  4.6 6.9 %collective-permute-start.4 = (bf16[1,2,1,128,256]{4,3,2,1,0:T(8,128)(2,1)S(1)}, bf16[1,2,1,128,256]{4,3,2,1,0:T(8,128)(2,1)S(1)}, u32[]{:S(2)}, u32[]{:S(2)}) collective-permute-start(bf16[1,2,1,128,256]{4,3,2,1,0:T(8,128)(2,1)S(1)} %bitcast.8), channel_id=1, source_target_pairs={{0,8},{4,12},{8,0},{12,4},{1,9},{5,13},{9,1},{13,5},{2,10},{6,14},... | collective-permute-start | bytes 393224 | tf_op jit(solution)/shard_map/ppermute | solution.py:213
  4.6 12.3 %copy-start = (f32[1,2,256,256]{3,2,1,0:T(8,128)S(1)}, f32[1,2,256,256]{3,2,1,0:T(8,128)}, u32[]{:S(2)}) copy-start(f32[1,2,256,256]{3,2,1,0:T(8,128)} %refs_0_.1) | copy-start | bytes 1572868
  5.4 6.9 %collective-permute-start.1 = (bf16[1,2,128,128]{3,2,1,0:T(8,128)(2,1)S(1)}, bf16[1,2,128,128]{3,2,1,0:T(8,128)(2,1)S(1)}, u32[]{:S(2)}, u32[]{:S(2)}) collective-permute-start(bf16[1,2,128,128]{3,2,1,0:T(8,128)(2,1)S(1)} %get-tuple-element.27), channel_id=1, source_target_pairs={{0,2},{1,3},{2,0},{3,1},{4,6},{5,7},{6,4},{7,5},{8,10},{9,11},{10,... | collective-permute-start | bytes 196616 | tf_op jit(solution)/shard_map/ppermute | solution.py:237
  8.5 6.2 %collective-permute-start.2 = (bf16[1,2,128,128]{3,2,1,0:T(8,128)(2,1)S(1)}, bf16[1,2,128,128]{3,2,1,0:T(8,128)(2,1)S(1)}, u32[]{:S(2)}, u32[]{:S(2)}) collective-permute-start(bf16[1,2,128,128]{3,2,1,0:T(8,128)(2,1)S(1)} %get-tuple-element.28), channel_id=1, source_target_pairs={{0,3},{1,2},{2,1},{3,0},{4,7},{5,6},{6,5},{7,4},{8,11},{9,10},{10,... | collective-permute-start | bytes 196616 | tf_op jit(solution)/shard_map/ppermute | solution.py:237
  9.8 5.0 %collective-permute-start.3 = (bf16[1,2,128,128]{3,2,1,0:T(8,128)(2,1)S(1)}, bf16[1,2,128,128]{3,2,1,0:T(8,128)(2,1)S(1)}, u32[]{:S(2)}, u32[]{:S(2)}) collective-permute-start(bf16[1,2,128,128]{3,2,1,0:T(8,128)(2,1)S(1)} %get-tuple-element.29), channel_id=1, source_target_pairs={{0,1},{1,0},{2,3},{3,2},{4,5},{5,4},{6,7},{7,6},{8,9},{9,8},{10,11... | collective-permute-start | bytes 196616 | tf_op jit(solution)/shard_map/ppermute | solution.py:237
  15.2 1.7 %collective-permute-start.6 = (f32[1,2,128,256]{3,2,1,0:T(8,128)S(1)}, f32[1,2,128,256]{3,2,1,0:T(8,128)S(1)}, u32[]{:S(2)}, u32[]{:S(2)}) collective-permute-start(f32[1,2,128,256]{3,2,1,0:T(8,128)S(1)} %get-tuple-element.32.refs_2_), channel_id=1, source_target_pairs={{0,4},{4,0},{8,12},{12,8},{1,5},{5,1},{9,13},{13,9},{2,6},{6,2},{1... | collective-permute-start | bytes 786440 | tf_op jit(solution)/shard_map/ppermute | solution.py:213
  15.3 6.1 %collective-permute-start.7 = (s16[1,272,256]{2,1,0:T(8,128)(2,1)S(1)}, s16[1,272,256]{2,1,0:T(8,128)(2,1)S(1)}, u32[]{:S(2)}, u32[]{:S(2)}) collective-permute-start(s16[1,272,256]{2,1,0:T(8,128)(2,1)S(1)} %get-tuple-element.35), channel_id=1, source_target_pairs={{0,8},{4,12},{8,0},{12,4},{1,9},{5,13},{9,1},{13,5},{2,10},{6,14},... | collective-permute-start | bytes 417800 | tf_op jit(solution)/shard_map/ppermute | solution.py:213
  21.4 1.4 %collective-permute-start.8 = (s16[1,272,256]{2,1,0:T(8,128)(2,1)S(1)}, s16[1,272,256]{2,1,0:T(8,128)(2,1)S(1)}, u32[]{:S(2)}, u32[]{:S(2)}) collective-permute-start(s16[1,272,256]{2,1,0:T(8,128)(2,1)S(1)} %collective-permute-done.7.refs_2_), channel_id=1, source_target_pairs={{0,4},{4,0},{8,12},{12,8},{1,5},{5,1},{9,13},{13,9},{2,6},{6,2},{1... | collective-permute-start | bytes 417800 | tf_op jit(solution)/shard_map/ppermute | solution.py:213

commit v4 on v3

v4 whole, which is shorter than its diff:
```python
import collections
import functools
import typing

import jax
import jax.numpy as jnp
from jax import lax
from jax.experimental import pallas as pl
from jax.experimental.pallas import tpu as pltpu
from jax.sharding import PartitionSpec as P

VMEM = pl.BlockSpec(memory_space=pltpu.VMEM)
HBM = pl.BlockSpec(memory_space=pltpu.HBM)
ANY = pl.BlockSpec(memory_space=pl.ANY)
VMEM_BYTES = 24 * 1024 * 1024
STEPS_PER_OCTAVE = 64
CLAIMED_FLOPS = 92 * 10**6

named = collections.OrderedDict


class Sizes(typing.NamedTuple):
    grid_rows: int
    grid_cols: int
    nodes: int
    row_blocks: int
    col_blocks: int
    kept: int
    width: int

    @property
    def rows(self):
        return self.row_blocks * self.kept

    @property
    def total(self):
        return self.row_blocks * self.grid_rows * self.kept


def partners(size, step):
    return [(place, place ^ step) for place in range(size)]


def dot(lhs, rhs, contract=(1, 0)):
    return lax.dot_general(
        lhs, rhs, (((contract[0],), (contract[1],)), ((), ())), preferred_element_type=jnp.float32
    )


def place_one_hot(picks, width):
    kept = picks.shape[-1]
    spots = lax.broadcasted_iota(jnp.int32, (width, kept), 0)
    return jnp.where(spots == picks, 1.0, 0.0).astype(jnp.bfloat16)


def first_kernel(result):
    result[...] = jnp.zeros_like(result)


def pick_kernel(sizes, surface, row_lists, token, *pieces):
    del token
    row_place = lax.axis_index("row")
    col_place = lax.axis_index("col")
    kept, width = sizes.kept, sizes.width
    slots = []
    for step in range(sizes.grid_cols):
        target = jnp.bitwise_xor(col_place, step)
        slots += [(step, node, target * sizes.nodes + node) for node in range(sizes.nodes)]

    def choices(block):
        lists = [row_lists[which, pl.ds(block, 1), :] for _, _, which in slots]
        return jnp.concatenate([place_one_hot(picks, width) for picks in lists], axis=1)

    for col_block in range(sizes.col_blocks):
        col_choices = choices(col_block * sizes.grid_cols + col_place)
        for row_block in range(sizes.row_blocks):
            row_choices = choices(row_block * sizes.grid_rows + row_place)
            halves = [surface[half, row_block, col_block] for half in range(2)]
            taken = dot(jnp.concatenate(halves, axis=0), col_choices).astype(jnp.bfloat16)
            for spot, (step, node, _) in enumerate(slots):
                cols = slice(spot * kept, (spot + 1) * kept)
                both = jnp.concatenate([taken[:width, cols], taken[width:, cols]], axis=1)
                block = dot(row_choices[:, cols], both, (0, 0)).astype(jnp.bfloat16)
                for half in range(2):
                    pieces[step][
                        node,
                        half,
                        row_block * kept : (row_block + 1) * kept,
                        col_block * kept : (col_block + 1) * kept,
                    ] = block[:, half * kept : (half + 1) * kept]


def block_at(sizes, block):
    return pl.ds(pl.multiple_of(block * sizes.kept, sizes.kept), sizes.kept)


def gather_kernel(sizes, factors, far_factor, whole_factor, turned_factor, own_factor, arrival):
    copy = pltpu.make_async_copy(far_factor, own_factor, arrival)
    copy.start()
    row_place = lax.axis_index("row")
    for step in [*range(1, sizes.grid_rows), 0]:
        if not step:
            copy.wait()
        held = factors[step] if step else own_factor
        source = jnp.bitwise_xor(row_place, step)
        for node in range(sizes.nodes):
            for block in range(sizes.row_blocks):
                spot = block_at(sizes, block * sizes.grid_rows + source)
                both = jnp.concatenate([held[node, 0, block], held[node, 1, block]], axis=1)
                whole_factor[node, spot, :] = both
                turned_factor[node, :, spot] = both.T


def block_kernel(sizes, pieces, whole_factor, result, coded):
    width, rows = sizes.width, sizes.rows
    col_place = lax.axis_index("col")
    for node in range(sizes.nodes):
        surfaces, factors = [], []
        for step, piece in pieces.items():
            source = jnp.bitwise_xor(col_place, step)
            surfaces.append(jnp.concatenate([piece[node, 0], piece[node, 1]], axis=0))
            for block in range(sizes.col_blocks):
                spot = block_at(sizes, block * sizes.grid_cols + source)
                factors.append(whole_factor[node, spot, :])
        product = dot(jnp.concatenate(surfaces, axis=1), jnp.concatenate(factors, axis=0))
        real = product[rows:, width:] - product[:rows, :width]
        imag = -(product[:rows, width:] + product[rows:, :width])
        result[node, :, :width] = real
        result[node, :, width:] = imag
        encode(real, imag, coded.at[node])


def encode(real, imag, coded):
    rows = real.shape[0]
    most = jnp.max(jnp.maximum(jnp.abs(real), jnp.abs(imag)), axis=0, keepdims=True)
    level = jnp.ceil(jnp.log2(jnp.maximum(most, 1e-30)) * STEPS_PER_OCTAVE + 0.1)
    scale = jnp.exp2(15.0 - level / STEPS_PER_OCTAVE)
    coded[:rows, :] = jnp.round(real * scale).astype(jnp.int32).astype(jnp.int16)
    coded[rows : 2 * rows, :] = jnp.round(imag * scale).astype(jnp.int32).astype(jnp.int16)
    levels = jnp.broadcast_to(level, (16, level.shape[1]))
    coded[2 * rows :, :] = levels.astype(jnp.int32).astype(jnp.int16)


def decode(coded):
    rows = coded.shape[0] // 2 - 8
    level = coded[2 * rows :, :].astype(jnp.int32).astype(jnp.float32)[:1]
    scale = jnp.exp2(level / STEPS_PER_OCTAVE - 15.0)
    values = coded[: 2 * rows, :].astype(jnp.int32).astype(jnp.float32) * scale
    return jnp.concatenate([values[:rows], values[rows:]], axis=1)


def factor_times(sizes, node, terms, turned_factor, spots=None):
    width = sizes.width
    spots = spots or slice(0, width)
    row_place = lax.axis_index("row")
    reals, imags, rights = [], [], []
    for step, wide in terms.items():
        source = jnp.bitwise_xor(row_place, step)
        places = [block_at(sizes, b * sizes.grid_rows + source) for b in range(sizes.row_blocks)]
        high = wide.astype(jnp.bfloat16)
        low = (wide - high.astype(jnp.float32)).astype(jnp.bfloat16)
        for value in (high, low):
            rights.append(value)
            for place in places:
                reals.append(turned_factor[node, spots.start : spots.stop, place])
                imags.append(turned_factor[node, width + spots.start : width + spots.stop, place])
    right = jnp.concatenate(rights, axis=0)
    from_real = dot(jnp.concatenate(reals, axis=1), right)
    from_imag = dot(jnp.concatenate(imags, axis=1), right)
    real = from_real[:, :width] - from_imag[:, width:]
    imag = from_real[:, width:] + from_imag[:, :width]
    return real, imag


def near_kernel(sizes, base, turned_factor, own, result, block):
    width = sizes.width
    for node in range(sizes.nodes):
        block[node, 0] = own[node, :, :width]
        block[node, 1] = own[node, :, width:]
        real, imag = factor_times(sizes, node, {0: own[node]}, turned_factor)
        result[node, 0] = base[node, 0] - real
        result[node, 1] = base[node, 1] - imag


def middle_kernel(sizes, before, turned_factor, mate, coded, result):
    for node in range(sizes.nodes):
        terms = {1: mate[node], **{step: decode(coded[step].at[node]) for step in coded}}
        real, imag = factor_times(sizes, node, terms, turned_factor)
        result[node, 0] = before[node, 0] - real
        result[node, 1] = before[node, 1] - imag


def last_kernel(sizes, before, turned_factor, coded, result, held, sent):
    half = sizes.width // 2
    copies = []
    for node in range(sizes.nodes):
        terms = {step: decode(coded[step].at[node]) for step in coded}
        for turn in range(2):
            spots = slice(turn * half, (turn + 1) * half)
            real, imag = factor_times(sizes, node, terms, turned_factor, spots)
            held[node, 0, spots] = before[node, 0, spots] - real
            held[node, 1, spots] = before[node, 1, spots] - imag
            place = (node, slice(None), spots)
            copy = pltpu.make_async_copy(held.at[place], result.at[place], sent.at[node, turn])
            copy.start()
            copies.append(copy)
    for copy in copies:
        copy.wait()


def call(kernel, out_shape, *args, remote=(), out_specs=None, scratch=()):
    flat, tree = jax.tree.flatten(args)

    def flat_kernel(*refs):
        ins = jax.tree.unflatten(tree, refs[: len(flat)])
        kernel(*ins, *refs[len(flat) :])

    return pl.pallas_call(
        flat_kernel,
        out_shape=out_shape,
        in_specs=[VMEM] * len(flat) + [HBM] * len(remote),
        out_specs=out_specs or [VMEM] * len(out_shape),
        scratch_shapes=scratch,
        compiler_params=pltpu.CompilerParams(vmem_limit_bytes=VMEM_BYTES),
    )(*flat, *[pltpu.with_memory_space_constraint(a, pltpu.HBM) for a in remote])


def local(inverse_top, factor, diag_inverse, row_lists):
    grid_rows = lax.axis_size("row")
    grid_cols = lax.axis_size("col")
    nodes, _, row_blocks, _, kept, width = factor.shape
    col_blocks = inverse_top.shape[4]
    sizes = Sizes(grid_rows, grid_cols, nodes, row_blocks, col_blocks, kept, width)
    rows = sizes.rows
    surface = inverse_top.transpose(0, 1, 2, 4, 5, 3, 6).reshape(
        2, row_blocks, col_blocks, width, width
    )
    own_factor = factor.reshape(nodes, 2, row_blocks, kept, width)
    narrow, wide = jnp.bfloat16, jnp.float32
    square = jax.ShapeDtypeStruct((nodes, 2, width, width), wide)
    across = range(2, grid_rows, 2)

    def over_rows(block, step):
        return lax.ppermute(block, "row", partners(grid_rows, step))

    token = pl.pallas_call(
        first_kernel,
        out_shape=pltpu.VMEM((8, 128), wide),
        out_specs=VMEM,
        cost_estimate=pl.CostEstimate(flops=CLAIMED_FLOPS, bytes_accessed=0, transcendentals=0),
    )()
    token, sent_factor = lax.optimization_barrier((token, own_factor))
    piece = jax.ShapeDtypeStruct((nodes, 2, rows, col_blocks * kept), narrow)
    pieces = pl.pallas_call(
        functools.partial(pick_kernel, sizes),
        out_shape=[piece] * grid_cols,
        in_specs=[VMEM, VMEM, ANY],
        out_specs=[VMEM] * grid_cols,
        compiler_params=pltpu.CompilerParams(vmem_limit_bytes=VMEM_BYTES),
    )(surface, row_lists, token)
    factors = named((step, over_rows(sent_factor, step)) for step in range(1, grid_rows))
    factors[1], pieces = lax.optimization_barrier((factors[1], pieces))
    arrived = named({0: pieces[0]})
    for step in [*range(grid_cols // 2, grid_cols), *range(grid_cols // 2 - 1, 0, -1)]:
        arrived[step] = lax.ppermute(pieces[step], "col", partners(grid_cols, step))
    whole_factor, turned_factor = call(
        functools.partial(gather_kernel, sizes),
        [
            jax.ShapeDtypeStruct((nodes, sizes.total, 2 * width), narrow),
            jax.ShapeDtypeStruct((nodes, 2 * width, sizes.total), narrow),
        ],
        factors,
        remote=[sent_factor],
        scratch=[pltpu.VMEM(own_factor.shape, narrow), pltpu.SemaphoreType.DMA],
    )
    block, coded = call(
        functools.partial(block_kernel, sizes),
        [
            jax.ShapeDtypeStruct((nodes, rows, 2 * width), wide),
            jax.ShapeDtypeStruct((nodes, 2 * rows + 16, width), jnp.int16),
        ],
        arrived,
        whole_factor,
    )
    sent = named((step, over_rows(coded, step)) for step in across)
    near, inverse_block = call(
        functools.partial(near_kernel, sizes),
        [square, jax.ShapeDtypeStruct((nodes, 2, rows, width), wide)],
        diag_inverse,
        turned_factor,
        block,
    )
    near, block = lax.optimization_barrier((near, block))
    mate = over_rows(block, 1)
    near, sent = lax.optimization_barrier((near, sent))
    forwarded = named((step + 1, over_rows(sent[step], 1)) for step in across)
    (middle,) = call(
        functools.partial(middle_kernel, sizes), [square], near, turned_factor, mate, sent
    )
    (diagonal_block,) = call(
        functools.partial(last_kernel, sizes),
        [square],
        middle,
        turned_factor,
        forwarded,
        out_specs=[HBM],
        scratch=[pltpu.VMEM(square.shape, wide), pltpu.SemaphoreType.DMA((nodes, 2))],
    )
    return inverse_block.reshape(nodes, 2, row_blocks, 1, kept, width), diagonal_block


def solution(mesh):
    placed = (
        P("pole", None, "row", None, None, "col", None),
        P("col", "pole", None, "row", None, None),
        P("col", "pole", None, None),
        P(),
    )
    return jax.shard_map(
        local,
        mesh=mesh,
        in_specs=placed,
        out_specs=(P("col", "pole", None, "row", None, None), P("col", "pole", None, None)),
        check_vma=False,
    )
```

time: 24 us -> 22.1 us (0.921)
  waiting for transfers between devices: 9.12 us -> 7.59 us
  local copies, waits for them, and re-layouts: 0.88 us -> 0.01 us
  Pallas kernels: 3.68 us -> 4.35 us
    ppermute x3, waiting for transfers between devices: 3.33 us -> 2.37 us  [local(): arrived[step] = lax.ppermute(pieces[step], 'col', partners(grid_cols, step))]
    unnamed x8 -> x6, local copies, waits for them, and re-layouts: 0.88 us -> 0.01 us
    pallas_call x4 -> x5, Pallas kernels: 2.99 us -> 3.85 us  [call(): pl.pallas_call(flat_kernel, out_shape=out_shape, in_specs=[VMEM] * len(fl...]
    ppermute x6, waiting for transfers between devices: 5.79 us -> 5.23 us  [over_rows(): return lax.ppermute(block, 'row', partners(grid_rows, step))]
    ppermute x3, starting transfers between devices: 4.72 us -> 4.44 us  [local(): arrived[step] = lax.ppermute(pieces[step], 'col', partners(grid_cols, step))]
  transfers between devices with their start and end apart: 9 -> 9, of which waited for: 6 -> 5; matrix products, arithmetic and copies ran while one was open for 0% -> 0% of each run, Pallas kernels for 9% -> 13%
where the time goes in v4:
time: 22.1 us; the launch traced here: 21.9 us
  starting transfers between devices  9.26 us (42%)
  waiting for transfers between devices  7.59 us (34%)
  Pallas kernels  4.35 us (20%)
  between operations  0.72 us (3%)
    ppermute x6, waiting for transfers between devices, over_rows(): return lax.ppermute(block, 'row', partners(grid_rows, step))  5.23 us
    ppermute x6, starting transfers between devices, over_rows(): return lax.ppermute(block, 'row', partners(grid_rows, step))  4.82 us
    ppermute x3, starting transfers between devices, local(): arrived[step] = lax.ppermute(pieces[step], 'col', partners(grid_cols, step))  4.44 us
    pallas_call x5, Pallas kernels, call(): pl.pallas_call(flat_kernel, out_shape=out_shape, in_specs=[VMEM] * len(fl...  3.85 us
    ppermute x3, waiting for transfers between devices, local(): arrived[step] = lax.ppermute(pieces[step], 'col', partners(grid_cols, step))  2.37 us
    pallas_call x1, Pallas kernels, local(): pl.pallas_call(functools.partial(pick_kernel, sizes), out_shape=[piece] *...  0.5 us
  transfers between devices with their start and end apart: 9, of which 5 were waited for; matrix products, arithmetic and copies ran while one was open for 0% of the time, Pallas kernels for 13%

profile of v4, /device:TPU:0, one launch (start us, length us, event | category | flops | bytes accessed | tf_op | source)
XLA Modules:
  0.0 21.9 jit_solution(1971995725831231904)
XLA Ops:
  0.6 0.0 copy-start.1
  0.6 0.0 copy-start.2
  0.7 0.5 %collective-permute-start = (bf16[1,2,1,128,256]{4,3,2,1,0:T(8,128)(2,1)}, bf16[1,2,1,128,256]{4,3,2,1,0:T(8,128)(2,1)S(1)}, u32[]{:S(2)}, u32[]{:S(2)}) collective-permute-start(bf16[1,2,1,128,256]{4,3,2,1,0:T(8,128)(2,1)} %bitcast.6), channel_id=1, source_target_pairs={{0,4},{4,0},{8,12},{12,8},{1,5},{5,1},{9,13},{13,9},{2,6},{6,2},{1... | collective-permute-start | bytes 393224 | tf_op jit(solution)/shard_map/ppermute | solution.py:244
  1.2 2.6 %collective-permute-start.1 = (bf16[1,2,1,128,256]{4,3,2,1,0:T(8,128)(2,1)}, bf16[1,2,1,128,256]{4,3,2,1,0:T(8,128)(2,1)S(1)}, u32[]{:S(2)}, u32[]{:S(2)}) collective-permute-start(bf16[1,2,1,128,256]{4,3,2,1,0:T(8,128)(2,1)} %bitcast.7), channel_id=1, source_target_pairs={{0,8},{4,12},{8,0},{12,4},{1,9},{5,13},{9,1},{13,5},{2,10},{6,14},... | collective-permute-start | bytes 393224 | tf_op jit(solution)/shard_map/ppermute | solution.py:244
  3.8 0.1 collective-permute-start.2
  3.8 0.0 copy-done.1
  3.8 0.0 copy-done.2
  3.8 0.5 %shard_map.60 = (bf16[1,2,128,128]{3,2,1,0:T(8,128)(2,1)S(1)}, bf16[1,2,128,128]{3,2,1,0:T(8,128)(2,1)S(1)}, bf16[1,2,128,128]{3,2,1,0:T(8,128)(2,1)S(1)}, bf16[1,2,128,128]{3,2,1,0:T(8,128)(2,1)S(1)}) custom-call(bf16[2,1,1,256,256]{4,3,2,1,0:T(8,128)(2,1)S(1)} %bitcast.5, s32[4,4,128]{2,1,0:T(4,128)S(1)} %copy-done.2, f32[8,128]{1,0:T(8,128)S(1)} %shard_map.59.token), custom_call_target="tpu_custom_call" | custom-call | tf_op jit(solution)/shard_map/pallas_call | solution.py:254
  4.4 0.0 collective-permute-done.refs_0_
  4.4 2.9 %collective-permute-start.3 = (bf16[1,2,128,128]{3,2,1,0:T(8,128)(2,1)S(1)}, bf16[1,2,128,128]{3,2,1,0:T(8,128)(2,1)S(1)}, u32[]{:S(2)}, u32[]{:S(2)}) collective-permute-start(bf16[1,2,128,128]{3,2,1,0:T(8,128)(2,1)S(1)} %get-tuple-element.32), channel_id=1, source_target_pairs={{0,2},{1,3},{2,0},{3,1},{4,6},{5,7},{6,4},{7,5},{8,10},{9,11},{10,... | collective-permute-start | bytes 196616 | tf_op jit(solution)/shard_map/ppermute | solution.py:265
  7.2 1.4 %collective-permute-start.4 = (bf16[1,2,128,128]{3,2,1,0:T(8,128)(2,1)S(1)}, bf16[1,2,128,128]{3,2,1,0:T(8,128)(2,1)S(1)}, u32[]{:S(2)}, u32[]{:S(2)}) collective-permute-start(bf16[1,2,128,128]{3,2,1,0:T(8,128)(2,1)S(1)} %get-tuple-element.33), channel_id=1, source_target_pairs={{0,3},{1,2},{2,1},{3,0},{4,7},{5,6},{6,5},{7,4},{8,11},{9,10},{10,... | collective-permute-start | bytes 196616 | tf_op jit(solution)/shard_map/ppermute | solution.py:265
  8.6 0.2 %collective-permute-start.5 = (bf16[1,2,128,128]{3,2,1,0:T(8,128)(2,1)S(1)}, bf16[1,2,128,128]{3,2,1,0:T(8,128)(2,1)S(1)}, u32[]{:S(2)}, u32[]{:S(2)}) collective-permute-start(bf16[1,2,128,128]{3,2,1,0:T(8,128)(2,1)S(1)} %get-tuple-element.34), channel_id=1, source_target_pairs={{0,1},{1,0},{2,3},{3,2},{4,5},{5,4},{6,7},{7,6},{8,9},{9,8},{10,11... | collective-permute-start | bytes 196616 | tf_op jit(solution)/shard_map/ppermute | solution.py:265
  8.8 0.0 collective-permute-done.1.refs_1_
  8.8 1.8 %collective-permute-done.2.refs_2_ = bf16[1,2,1,128,256]{4,3,2,1,0:T(8,128)(2,1)S(1)} collective-permute-done((bf16[1,2,1,128,256]{4,3,2,1,0:T(8,128)(2,1)}, bf16[1,2,1,128,256]{4,3,2,1,0:T(8,128)(2,1)S(1)}, u32[]{:S(2)}, u32[]{:S(2)}) %collective-permute-start.2) | collective-permute-done | bytes 131104 | tf_op jit(solution)/shard_map/ppermute | solution.py:244
  10.6 1.0 %shard_map.61 = (bf16[1,512,512]{2,1,0:T(8,128)(2,1)S(1)}, bf16[1,512,512]{2,1,0:T(8,128)(2,1)S(1)}) custom-call(bf16[1,2,1,128,256]{4,3,2,1,0:T(8,128)(2,1)S(1)} %collective-permute-done.refs_0_, bf16[1,2,1,128,256]{4,3,2,1,0:T(8,128)(2,1)S(1)} %collective-permute-done.1.refs_1_, bf16[1,2,1,128,256]{4,3,2,1,0:T(8,128)(2,1)S(1)} %collective-permute-done.2.refs_2_, ...), custom_call_target="tpu_custom_call" | custom-call | tf_op jit(solution)/shard_map/pallas_call | solution.py:218
  11.6 0.0 copy-start
  11.7 0.0 collective-permute-done.3.refs_1_
  11.7 2.1 %collective-permute-done.4.refs_2_ = bf16[1,2,128,128]{3,2,1,0:T(8,128)(2,1)S(1)} collective-permute-done((bf16[1,2,128,128]{3,2,1,0:T(8,128)(2,1)S(1)}, bf16[1,2,128,128]{3,2,1,0:T(8,128)(2,1)S(1)}, u32[]{:S(2)}, u32[]{:S(2)}) %collective-permute-start.4) | collective-permute-done | bytes 65568 | tf_op jit(solution)/shard_map/ppermute | solution.py:265
  13.8 0.2 collective-permute-done.5.refs_3_
  14.0 0.4 %shard_map.62 = (f32[1,128,512]{2,1,0:T(8,128)S(1)}, s16[1,272,256]{2,1,0:T(8,128)(2,1)S(1)}) custom-call(bf16[1,2,128,128]{3,2,1,0:T(8,128)(2,1)S(1)} %get-tuple-element.31.refs_0_, bf16[1,2,128,128]{3,2,1,0:T(8,128)(2,1)S(1)} %collective-permute-done.3.refs_1_, bf16[1,2,128,128]{3,2,1,0:T(8,128)(2,1)S(1)} %collective-permute-done.4.refs_2_, ...), custom_call_target="tpu_custom_call" | custom-call | tf_op jit(solution)/shard_map/pallas_call | solution.py:218
  14.4 1.6 %collective-permute-start.6 = (s16[1,272,256]{2,1,0:T(8,128)(2,1)S(1)}, s16[1,272,256]{2,1,0:T(8,128)(2,1)S(1)}, u32[]{:S(2)}, u32[]{:S(2)}) collective-permute-start(s16[1,272,256]{2,1,0:T(8,128)(2,1)S(1)} %get-tuple-element.40), channel_id=1, source_target_pairs={{0,8},{4,12},{8,0},{12,4},{1,9},{5,13},{9,1},{13,5},{2,10},{6,14},... | collective-permute-start | bytes 417800 | tf_op jit(solution)/shard_map/ppermute | solution.py:244
  16.0 0.0 copy-done
  16.0 1.0 %shard_map.63 = (f32[1,2,256,256]{3,2,1,0:T(8,128)S(1)}, f32[1,2,128,256]{3,2,1,0:T(8,128)}) custom-call(f32[1,2,256,256]{3,2,1,0:T(8,128)S(1)} %copy-done, bf16[1,512,512]{2,1,0:T(8,128)(2,1)S(1)} %get-tuple-element.30.refs_1_, f32[1,128,512]{2,1,0:T(8,128)S(1)} %get-tuple-element.42.refs_2_), custom_call_target="tpu_custom_call" | custom-call | tf_op jit(solution)/shard_map/pallas_call | solution.py:218
  17.0 0.0 collective-permute-start.7
  17.0 2.5 %collective-permute-done.6.refs_3_ = s16[1,272,256]{2,1,0:T(8,128)(2,1)S(1)} collective-permute-done((s16[1,272,256]{2,1,0:T(8,128)(2,1)S(1)}, s16[1,272,256]{2,1,0:T(8,128)(2,1)S(1)}, u32[]{:S(2)}, u32[]{:S(2)}) %collective-permute-start.6) | collective-permute-done | bytes 139296 | tf_op jit(solution)/shard_map/ppermute | solution.py:244
  19.5 0.0 collective-permute-start.8
  19.5 0.0 collective-permute-done.7.refs_2_
  19.5 0.4 %shard_map.64.refs_0_ = f32[1,2,256,256]{3,2,1,0:T(8,128)S(1)} custom-call(f32[1,2,256,256]{3,2,1,0:T(8,128)S(1)} %get-tuple-element.41.refs_0_, bf16[1,512,512]{2,1,0:T(8,128)(2,1)S(1)} %get-tuple-element.30.refs_1_, f32[1,128,512]{2,1,0:T(8,128)S(1)} %collective-permute-done.7.refs_2_, s16[1,272,256]{2,1,0:T(8,128)(2,1)S(1)} %collective-permute-done.6.refs_3_), custom_call_target="tpu_custom_call" | custom-call | tf_op jit(solution)/shard_map/pallas_call | solution.py:218
  20.0 0.9 %collective-permute-done.8.refs_2_ = s16[1,272,256]{2,1,0:T(8,128)(2,1)S(1)} collective-permute-done((s16[1,272,256]{2,1,0:T(8,128)(2,1)S(1)}, s16[1,272,256]{2,1,0:T(8,128)(2,1)S(1)}, u32[]{:S(2)}, u32[]{:S(2)}) %collective-permute-start.8) | collective-permute-done | bytes 139296 | tf_op jit(solution)/shard_map/ppermute | solution.py:244
  20.9 1.1 %shard_map.65 = f32[1,2,256,256]{3,2,1,0:T(8,128)} custom-call(f32[1,2,256,256]{3,2,1,0:T(8,128)S(1)} %shard_map.64.refs_0_, bf16[1,512,512]{2,1,0:T(8,128)(2,1)S(1)} %get-tuple-element.30.refs_1_, s16[1,272,256]{2,1,0:T(8,128)(2,1)S(1)} %collective-permute-done.8.refs_2_), custom_call_target="tpu_custom_call" | custom-call | tf_op jit(solution)/shard_map/pallas_call | solution.py:218
  (1 shorter events, 0.0 us)
Async XLA Ops:
  0.6 3.2 %copy-start.1 = (bf16[2,1,1,256,1,1,256]{6,3,5,4,2,1,0:T(8,128)(2,1)S(1)}, bf16[2,1,1,256,1,1,256]{6,3,5,4,2,1,0:T(8,128)(2,1)}, u32[]{:S(2)}) copy-start(bf16[2,1,1,256,1,1,256]{6,3,5,4,2,1,0:T(8,128)(2,1)} %param.4) | copy-start | bytes 786436
  0.6 3.2 %copy-start.2 = (s32[4,4,128]{2,1,0:T(4,128)S(1)}, s32[4,4,128]{2,1,0:T(4,128)}, u32[]{:S(2)}) copy-start(s32[4,4,128]{2,1,0:T(4,128)} %row_lists.1) | copy-start | bytes 24580
  0.7 3.7 %collective-permute-start = (bf16[1,2,1,128,256]{4,3,2,1,0:T(8,128)(2,1)}, bf16[1,2,1,128,256]{4,3,2,1,0:T(8,128)(2,1)S(1)}, u32[]{:S(2)}, u32[]{:S(2)}) collective-permute-start(bf16[1,2,1,128,256]{4,3,2,1,0:T(8,128)(2,1)} %bitcast.6), channel_id=1, source_target_pairs={{0,4},{4,0},{8,12},{12,8},{1,5},{5,1},{9,13},{13,9},{2,6},{6,2},{1... | collective-permute-start | bytes 393224 | tf_op jit(solution)/shard_map/ppermute | solution.py:244
  1.2 7.6 %collective-permute-start.1 = (bf16[1,2,1,128,256]{4,3,2,1,0:T(8,128)(2,1)}, bf16[1,2,1,128,256]{4,3,2,1,0:T(8,128)(2,1)S(1)}, u32[]{:S(2)}, u32[]{:S(2)}) collective-permute-start(bf16[1,2,1,128,256]{4,3,2,1,0:T(8,128)(2,1)} %bitcast.7), channel_id=1, source_target_pairs={{0,8},{4,12},{8,0},{12,4},{1,9},{5,13},{9,1},{13,5},{2,10},{6,14},... | collective-permute-start | bytes 393224 | tf_op jit(solution)/shard_map/ppermute | solution.py:244
  3.8 6.8 %collective-permute-start.2 = (bf16[1,2,1,128,256]{4,3,2,1,0:T(8,128)(2,1)}, bf16[1,2,1,128,256]{4,3,2,1,0:T(8,128)(2,1)S(1)}, u32[]{:S(2)}, u32[]{:S(2)}) collective-permute-start(bf16[1,2,1,128,256]{4,3,2,1,0:T(8,128)(2,1)} %bitcast.8), channel_id=1, source_target_pairs={{0,12},{4,8},{8,4},{12,0},{1,13},{5,9},{9,5},{13,1},{2,14},{6,10},... | collective-permute-start | bytes 393224 | tf_op jit(solution)/shard_map/ppermute | solution.py:244
  4.4 7.3 %collective-permute-start.3 = (bf16[1,2,128,128]{3,2,1,0:T(8,128)(2,1)S(1)}, bf16[1,2,128,128]{3,2,1,0:T(8,128)(2,1)S(1)}, u32[]{:S(2)}, u32[]{:S(2)}) collective-permute-start(bf16[1,2,128,128]{3,2,1,0:T(8,128)(2,1)S(1)} %get-tuple-element.32), channel_id=1, source_target_pairs={{0,2},{1,3},{2,0},{3,1},{4,6},{5,7},{6,4},{7,5},{8,10},{9,11},{10,... | collective-permute-start | bytes 196616 | tf_op jit(solution)/shard_map/ppermute | solution.py:265
  7.2 6.6 %collective-permute-start.4 = (bf16[1,2,128,128]{3,2,1,0:T(8,128)(2,1)S(1)}, bf16[1,2,128,128]{3,2,1,0:T(8,128)(2,1)S(1)}, u32[]{:S(2)}, u32[]{:S(2)}) collective-permute-start(bf16[1,2,128,128]{3,2,1,0:T(8,128)(2,1)S(1)} %get-tuple-element.33), channel_id=1, source_target_pairs={{0,3},{1,2},{2,1},{3,0},{4,7},{5,6},{6,5},{7,4},{8,11},{9,10},{10,... | collective-permute-start | bytes 196616 | tf_op jit(solution)/shard_map/ppermute | solution.py:265
  8.6 5.5 %collective-permute-start.5 = (bf16[1,2,128,128]{3,2,1,0:T(8,128)(2,1)S(1)}, bf16[1,2,128,128]{3,2,1,0:T(8,128)(2,1)S(1)}, u32[]{:S(2)}, u32[]{:S(2)}) collective-permute-start(bf16[1,2,128,128]{3,2,1,0:T(8,128)(2,1)S(1)} %get-tuple-element.34), channel_id=1, source_target_pairs={{0,1},{1,0},{2,3},{3,2},{4,5},{5,4},{6,7},{7,6},{8,9},{9,8},{10,11... | collective-permute-start | bytes 196616 | tf_op jit(solution)/shard_map/ppermute | solution.py:265
  11.6 4.4 %copy-start = (f32[1,2,256,256]{3,2,1,0:T(8,128)S(1)}, f32[1,2,256,256]{3,2,1,0:T(8,128)}, u32[]{:S(2)}) copy-start(f32[1,2,256,256]{3,2,1,0:T(8,128)} %refs_0_.1) | copy-start | bytes 1572868
  14.4 5.1 %collective-permute-start.6 = (s16[1,272,256]{2,1,0:T(8,128)(2,1)S(1)}, s16[1,272,256]{2,1,0:T(8,128)(2,1)S(1)}, u32[]{:S(2)}, u32[]{:S(2)}) collective-permute-start(s16[1,272,256]{2,1,0:T(8,128)(2,1)S(1)} %get-tuple-element.40), channel_id=1, source_target_pairs={{0,8},{4,12},{8,0},{12,4},{1,9},{5,13},{9,1},{13,5},{2,10},{6,14},... | collective-permute-start | bytes 417800 | tf_op jit(solution)/shard_map/ppermute | solution.py:244
  17.0 2.5 %collective-permute-start.7 = (f32[1,128,512]{2,1,0:T(8,128)S(1)}, f32[1,128,512]{2,1,0:T(8,128)S(1)}, u32[]{:S(2)}, u32[]{:S(2)}) collective-permute-start(f32[1,128,512]{2,1,0:T(8,128)S(1)} %get-tuple-element.42.refs_2_), channel_id=1, source_target_pairs={{0,4},{4,0},{8,12},{12,8},{1,5},{5,1},{9,13},{13,9},{2,6},{6,2},{1... | collective-permute-start | bytes 786440 | tf_op jit(solution)/shard_map/ppermute | solution.py:244
  19.5 1.4 %collective-permute-start.8 = (s16[1,272,256]{2,1,0:T(8,128)(2,1)S(1)}, s16[1,272,256]{2,1,0:T(8,128)(2,1)S(1)}, u32[]{:S(2)}, u32[]{:S(2)}) collective-permute-start(s16[1,272,256]{2,1,0:T(8,128)(2,1)S(1)} %collective-permute-done.6.refs_3_), channel_id=1, source_target_pairs={{0,4},{4,0},{8,12},{12,8},{1,5},{5,1},{9,13},{13,9},{2,6},{6,2},{1... | collective-permute-start | bytes 417800 | tf_op jit(solution)/shard_map/ppermute | solution.py:244

commit v5 on v4

--- a/solution.py
+++ b/solution.py
@@ -94,21 +94,26 @@
     return pl.ds(pl.multiple_of(block * sizes.kept, sizes.kept), sizes.kept)
 
 
-def gather_kernel(sizes, factors, far_factor, whole_factor, turned_factor, own_factor, arrival):
-    copy = pltpu.make_async_copy(far_factor, own_factor, arrival)
+def stack_kernel(sizes, factors, far_factor, stacked, arrival):
+    copy = pltpu.make_async_copy(far_factor, stacked.at[0], arrival)
     copy.start()
+    for spot, step in enumerate(factors):
+        stacked[spot + 1] = factors[step][...]
+    copy.wait()
+
+
+def gather_kernel(sizes, both, whole_factor, turned_factor):
     row_place = lax.axis_index("row")
-    for step in [*range(1, sizes.grid_rows), 0]:
-        if not step:
-            copy.wait()
-        held = factors[step] if step else own_factor
-        source = jnp.bitwise_xor(row_place, step)
-        for node in range(sizes.nodes):
-            for block in range(sizes.row_blocks):
-                spot = block_at(sizes, block * sizes.grid_rows + source)
-                both = jnp.concatenate([held[node, 0, block], held[node, 1, block]], axis=1)
-                whole_factor[node, spot, :] = both
-                turned_factor[node, :, spot] = both.T
+    for core in range(2):
+        for spot in range(sizes.grid_rows // 2):
+            source = jnp.bitwise_xor(row_place - row_place % 2, 2 * spot) + core
+            for node in range(sizes.nodes):
+                for block in range(sizes.row_blocks):
+                    place = block_at(sizes, block * sizes.grid_rows + source)
+                    halves = [both[core, spot, node, half, block] for half in range(2)]
+                    wide = jnp.concatenate(halves, axis=1)
+                    whole_factor[node, place, :] = wide
+                    turned_factor[node, :, place] = wide.T
 
 
 def block_kernel(sizes, pieces, whole_factor, result, coded):
@@ -258,20 +263,26 @@
         out_specs=[VMEM] * grid_cols,
         compiler_params=pltpu.CompilerParams(vmem_limit_bytes=VMEM_BYTES),
     )(surface, row_lists, token)
-    factors = named((step, over_rows(sent_factor, step)) for step in range(1, grid_rows))
-    factors[1], pieces = lax.optimization_barrier((factors[1], pieces))
+    factors = named((step, over_rows(sent_factor, step)) for step in across)
     arrived = named({0: pieces[0]})
     for step in [*range(grid_cols // 2, grid_cols), *range(grid_cols // 2 - 1, 0, -1)]:
         arrived[step] = lax.ppermute(pieces[step], "col", partners(grid_cols, step))
+    (stacked,) = call(
+        functools.partial(stack_kernel, sizes),
+        [jax.ShapeDtypeStruct((grid_rows // 2, *own_factor.shape), narrow)],
+        factors,
+        remote=[sent_factor],
+        scratch=[pltpu.SemaphoreType.DMA],
+    )
+    pairs = [[place, place + 1] for place in range(0, grid_rows, 2)]
+    both = lax.all_gather(stacked, "row", axis_index_groups=pairs)
     whole_factor, turned_factor = call(
         functools.partial(gather_kernel, sizes),
         [
             jax.ShapeDtypeStruct((nodes, sizes.total, 2 * width), narrow),
             jax.ShapeDtypeStruct((nodes, 2 * width, sizes.total), narrow),
         ],
-        factors,
-        remote=[sent_factor],
-        scratch=[pltpu.VMEM(own_factor.shape, narrow), pltpu.SemaphoreType.DMA],
+        both,
     )
     block, coded = call(
         functools.partial(block_kernel, sizes),

time: 22.1 us -> 21.3 us (0.964)
  blocking collectives: 0 us -> 2.18 us
  waiting for transfers between devices: 7.59 us -> 5.54 us
  starting transfers between devices: 9.26 us -> 8.19 us
    all_gather x0 -> x1, blocking collectives: none -> 2.18 us  [local(): both = lax.all_gather(stacked, 'row', axis_index_groups=pairs)]
    ppermute x6 -> x4, waiting for transfers between devices: 5.23 us -> 4.14 us  [over_rows(): return lax.ppermute(block, 'row', partners(grid_rows, step))]
    ppermute x3, waiting for transfers between devices: 2.37 us -> 1.4 us  [local(): arrived[step] = lax.ppermute(pieces[step], 'col', partners(grid_cols, step))]
    ppermute x6 -> x4, starting transfers between devices: 4.82 us -> 3.96 us  [over_rows(): return lax.ppermute(block, 'row', partners(grid_rows, step))]
    pallas_call x5 -> x6, Pallas kernels: 3.85 us -> 3.94 us  [call(): pl.pallas_call(flat_kernel, out_shape=out_shape, in_specs=[VMEM] * len(fl...]
  transfers between devices with their start and end apart: 9 -> 7, of which waited for: 5 -> 4; matrix products, arithmetic and copies ran while one was open for 0% -> 0% of each run, Pallas kernels for 13% -> 14%
where the time goes in v5:
time: 21.3 us; the launch traced here: 21.1 us
  starting transfers between devices  8.19 us (38%)
  waiting for transfers between devices  5.54 us (26%)
  Pallas kernels  4.44 us (21%)
  blocking collectives  2.18 us (10%)
  between operations  0.71 us (3%)
    ppermute x3, starting transfers between devices, local(): arrived[step] = lax.ppermute(pieces[step], 'col', partners(grid_cols, step))  4.24 us
    ppermute x4, waiting for transfers between devices, over_rows(): return lax.ppermute(block, 'row', partners(grid_rows, step))  4.14 us
    ppermute x4, starting transfers between devices, over_rows(): return lax.ppermute(block, 'row', partners(grid_rows, step))  3.96 us
    pallas_call x6, Pallas kernels, call(): pl.pallas_call(flat_kernel, out_shape=out_shape, in_specs=[VMEM] * len(fl...  3.94 us
    all_gather x1, blocking collectives, local(): both = lax.all_gather(stacked, 'row', axis_index_groups=pairs)  2.18 us
    ppermute x3, waiting for transfers between devices, local(): arrived[step] = lax.ppermute(pieces[step], 'col', partners(grid_cols, step))  1.4 us
    pallas_call x1, Pallas kernels, local(): pl.pallas_call(functools.partial(pick_kernel, sizes), out_shape=[piece] *...  0.5 us
  transfers between devices with their start and end apart: 7, of which 4 were waited for; matrix products, arithmetic and copies ran while one was open for 0% of the time, Pallas kernels for 14%

profile of v5, /device:TPU:0, one launch (start us, length us, event | category | flops | bytes accessed | tf_op | source)
XLA Modules:
  0.0 21.1 jit_solution(6624184501752439585)
XLA Ops:
  0.6 0.0 copy-start.1
  0.6 0.0 copy-start.2
  0.7 3.0 %collective-permute-start = (bf16[1,2,1,128,256]{4,3,2,1,0:T(8,128)(2,1)}, bf16[1,2,1,128,256]{4,3,2,1,0:T(8,128)(2,1)S(1)}, u32[]{:S(2)}, u32[]{:S(2)}) collective-permute-start(bf16[1,2,1,128,256]{4,3,2,1,0:T(8,128)(2,1)} %bitcast.8), channel_id=1, source_target_pairs={{0,8},{4,12},{8,0},{12,4},{1,9},{5,13},{9,1},{13,5},{2,10},{6,14},... | collective-permute-start | bytes 393224 | tf_op jit(solution)/shard_map/ppermute | solution.py:249
  3.7 0.0 copy-done.1
  3.7 0.0 copy-done.2
  3.7 0.5 %shard_map.62 = (bf16[1,2,128,128]{3,2,1,0:T(8,128)(2,1)S(1)}, bf16[1,2,128,128]{3,2,1,0:T(8,128)(2,1)S(1)}, bf16[1,2,128,128]{3,2,1,0:T(8,128)(2,1)S(1)}, bf16[1,2,128,128]{3,2,1,0:T(8,128)(2,1)S(1)}) custom-call(bf16[2,1,1,256,256]{4,3,2,1,0:T(8,128)(2,1)S(1)} %bitcast.7, s32[4,4,128]{2,1,0:T(4,128)S(1)} %copy-done.2, f32[8,128]{1,0:T(8,128)S(1)} %shard_map.59.token), custom_call_target="tpu_custom_call" | custom-call | tf_op jit(solution)/shard_map/pallas_call | solution.py:259
  4.2 2.7 %collective-permute-start.1 = (bf16[1,2,128,128]{3,2,1,0:T(8,128)(2,1)S(1)}, bf16[1,2,128,128]{3,2,1,0:T(8,128)(2,1)S(1)}, u32[]{:S(2)}, u32[]{:S(2)}) collective-permute-start(bf16[1,2,128,128]{3,2,1,0:T(8,128)(2,1)S(1)} %get-tuple-element.22), channel_id=1, source_target_pairs={{0,2},{1,3},{2,0},{3,1},{4,6},{5,7},{6,4},{7,5},{8,10},{9,11},{10,... | collective-permute-start | bytes 196616 | tf_op jit(solution)/shard_map/ppermute | solution.py:269
  6.9 1.3 %collective-permute-start.2 = (bf16[1,2,128,128]{3,2,1,0:T(8,128)(2,1)S(1)}, bf16[1,2,128,128]{3,2,1,0:T(8,128)(2,1)S(1)}, u32[]{:S(2)}, u32[]{:S(2)}) collective-permute-start(bf16[1,2,128,128]{3,2,1,0:T(8,128)(2,1)S(1)} %get-tuple-element.23), channel_id=1, source_target_pairs={{0,3},{1,2},{2,1},{3,0},{4,7},{5,6},{6,5},{7,4},{8,11},{9,10},{10,... | collective-permute-start | bytes 196616 | tf_op jit(solution)/shard_map/ppermute | solution.py:269
  8.2 0.2 %collective-permute-start.3 = (bf16[1,2,128,128]{3,2,1,0:T(8,128)(2,1)S(1)}, bf16[1,2,128,128]{3,2,1,0:T(8,128)(2,1)S(1)}, u32[]{:S(2)}, u32[]{:S(2)}) collective-permute-start(bf16[1,2,128,128]{3,2,1,0:T(8,128)(2,1)S(1)} %get-tuple-element.24), channel_id=1, source_target_pairs={{0,1},{1,0},{2,3},{3,2},{4,5},{5,4},{6,7},{7,6},{8,9},{9,8},{10,11... | collective-permute-start | bytes 196616 | tf_op jit(solution)/shard_map/ppermute | solution.py:269
  8.4 0.0 collective-permute-done.refs_0_
  8.4 0.9 %shard_map.60 = bf16[2,1,2,1,128,256]{5,4,3,2,1,0:T(8,128)(2,1)S(1)} custom-call(bf16[1,2,1,128,256]{4,3,2,1,0:T(8,128)(2,1)S(1)} %collective-permute-done.refs_0_, bf16[1,2,1,128,256]{4,3,2,1,0:T(8,128)(2,1)} %bitcast.9), custom_call_target="tpu_custom_call" | custom-call | tf_op jit(solution)/shard_map/pallas_call | solution.py:223
  9.4 2.2 %all-gather = bf16[4,1,2,1,128,256]{5,4,3,2,1,0:T(8,128)(2,1)S(1)} all-gather(bf16[2,1,2,1,128,256]{5,4,3,2,1,0:T(8,128)(2,1)S(1)} %shard_map.60), channel_id=2, replica_groups={{0,4},{8,12},{1,5},{9,13},{2,6},{10,14},{3,7},{11,15},{16,20},{24,28},{..., dimensions={0}, use_global_device_ids=true | all-gather | bytes 786432 | tf_op jit(solution)/shard_map/all_gather | solution.py:278
  11.5 0.2 shard_map.61
  11.8 0.0 copy-start
  11.8 0.0 collective-permute-done.1.refs_1_
  11.8 1.3 %collective-permute-done.2.refs_2_ = bf16[1,2,128,128]{3,2,1,0:T(8,128)(2,1)S(1)} collective-permute-done((bf16[1,2,128,128]{3,2,1,0:T(8,128)(2,1)S(1)}, bf16[1,2,128,128]{3,2,1,0:T(8,128)(2,1)S(1)}, u32[]{:S(2)}, u32[]{:S(2)}) %collective-permute-start.2) | collective-permute-done | bytes 65568 | tf_op jit(solution)/shard_map/ppermute | solution.py:269
  13.1 0.1 collective-permute-done.3.refs_3_
  13.2 0.3 %shard_map.63 = (f32[1,128,512]{2,1,0:T(8,128)S(1)}, s16[1,272,256]{2,1,0:T(8,128)(2,1)S(1)}) custom-call(bf16[1,2,128,128]{3,2,1,0:T(8,128)(2,1)S(1)} %get-tuple-element.21.refs_0_, bf16[1,2,128,128]{3,2,1,0:T(8,128)(2,1)S(1)} %collective-permute-done.1.refs_1_, bf16[1,2,128,128]{3,2,1,0:T(8,128)(2,1)S(1)} %collective-permute-done.2.refs_2_, ...), custom_call_target="tpu_custom_call" | custom-call | tf_op jit(solution)/shard_map/pallas_call | solution.py:223
  13.5 0.9 %collective-permute-start.4 = (s16[1,272,256]{2,1,0:T(8,128)(2,1)S(1)}, s16[1,272,256]{2,1,0:T(8,128)(2,1)S(1)}, u32[]{:S(2)}, u32[]{:S(2)}) collective-permute-start(s16[1,272,256]{2,1,0:T(8,128)(2,1)S(1)} %get-tuple-element.30), channel_id=1, source_target_pairs={{0,8},{4,12},{8,0},{12,4},{1,9},{5,13},{9,1},{13,5},{2,10},{6,14},... | collective-permute-start | bytes 417800 | tf_op jit(solution)/shard_map/ppermute | solution.py:249
  14.5 0.0 copy-done
  14.5 1.0 %shard_map.64 = (f32[1,2,256,256]{3,2,1,0:T(8,128)S(1)}, f32[1,2,128,256]{3,2,1,0:T(8,128)}) custom-call(f32[1,2,256,256]{3,2,1,0:T(8,128)S(1)} %copy-done, bf16[1,512,512]{2,1,0:T(8,128)(2,1)S(1)} %get-tuple-element.19.refs_1_, f32[1,128,512]{2,1,0:T(8,128)S(1)} %get-tuple-element.32.refs_2_), custom_call_target="tpu_custom_call" | custom-call | tf_op jit(solution)/shard_map/pallas_call | solution.py:223
  15.4 0.0 collective-permute-start.5
  15.4 3.2 %collective-permute-done.4.refs_3_ = s16[1,272,256]{2,1,0:T(8,128)(2,1)S(1)} collective-permute-done((s16[1,272,256]{2,1,0:T(8,128)(2,1)S(1)}, s16[1,272,256]{2,1,0:T(8,128)(2,1)S(1)}, u32[]{:S(2)}, u32[]{:S(2)}) %collective-permute-start.4) | collective-permute-done | bytes 139296 | tf_op jit(solution)/shard_map/ppermute | solution.py:249
  18.7 0.0 collective-permute-start.6
  18.7 0.0 collective-permute-done.5.refs_2_
  18.7 0.4 %shard_map.65.refs_0_ = f32[1,2,256,256]{3,2,1,0:T(8,128)S(1)} custom-call(f32[1,2,256,256]{3,2,1,0:T(8,128)S(1)} %get-tuple-element.31.refs_0_, bf16[1,512,512]{2,1,0:T(8,128)(2,1)S(1)} %get-tuple-element.19.refs_1_, f32[1,128,512]{2,1,0:T(8,128)S(1)} %collective-permute-done.5.refs_2_, s16[1,272,256]{2,1,0:T(8,128)(2,1)S(1)} %collective-permute-done.4.refs_3_), custom_call_target="tpu_custom_call" | custom-call | tf_op jit(solution)/shard_map/pallas_call | solution.py:223
  19.1 0.9 %collective-permute-done.6.refs_2_ = s16[1,272,256]{2,1,0:T(8,128)(2,1)S(1)} collective-permute-done((s16[1,272,256]{2,1,0:T(8,128)(2,1)S(1)}, s16[1,272,256]{2,1,0:T(8,128)(2,1)S(1)}, u32[]{:S(2)}, u32[]{:S(2)}) %collective-permute-start.6) | collective-permute-done | bytes 139296 | tf_op jit(solution)/shard_map/ppermute | solution.py:249
  20.0 1.1 %shard_map.66 = f32[1,2,256,256]{3,2,1,0:T(8,128)} custom-call(f32[1,2,256,256]{3,2,1,0:T(8,128)S(1)} %shard_map.65.refs_0_, bf16[1,512,512]{2,1,0:T(8,128)(2,1)S(1)} %get-tuple-element.19.refs_1_, s16[1,272,256]{2,1,0:T(8,128)(2,1)S(1)} %collective-permute-done.6.refs_2_), custom_call_target="tpu_custom_call" | custom-call | tf_op jit(solution)/shard_map/pallas_call | solution.py:223
  (1 shorter events, 0.0 us)
Async XLA Ops:
  0.6 3.1 %copy-start.1 = (bf16[2,1,1,256,1,1,256]{6,3,5,4,2,1,0:T(8,128)(2,1)S(1)}, bf16[2,1,1,256,1,1,256]{6,3,5,4,2,1,0:T(8,128)(2,1)}, u32[]{:S(2)}) copy-start(bf16[2,1,1,256,1,1,256]{6,3,5,4,2,1,0:T(8,128)(2,1)} %param.4) | copy-start | bytes 786436
  0.6 3.1 %copy-start.2 = (s32[4,4,128]{2,1,0:T(4,128)S(1)}, s32[4,4,128]{2,1,0:T(4,128)}, u32[]{:S(2)}) copy-start(s32[4,4,128]{2,1,0:T(4,128)} %row_lists.1) | copy-start | bytes 24580
  0.7 7.8 %collective-permute-start = (bf16[1,2,1,128,256]{4,3,2,1,0:T(8,128)(2,1)}, bf16[1,2,1,128,256]{4,3,2,1,0:T(8,128)(2,1)S(1)}, u32[]{:S(2)}, u32[]{:S(2)}) collective-permute-start(bf16[1,2,1,128,256]{4,3,2,1,0:T(8,128)(2,1)} %bitcast.8), channel_id=1, source_target_pairs={{0,8},{4,12},{8,0},{12,4},{1,9},{5,13},{9,1},{13,5},{2,10},{6,14},... | collective-permute-start | bytes 393224 | tf_op jit(solution)/shard_map/ppermute | solution.py:249
  4.2 7.6 %collective-permute-start.1 = (bf16[1,2,128,128]{3,2,1,0:T(8,128)(2,1)S(1)}, bf16[1,2,128,128]{3,2,1,0:T(8,128)(2,1)S(1)}, u32[]{:S(2)}, u32[]{:S(2)}) collective-permute-start(bf16[1,2,128,128]{3,2,1,0:T(8,128)(2,1)S(1)} %get-tuple-element.22), channel_id=1, source_target_pairs={{0,2},{1,3},{2,0},{3,1},{4,6},{5,7},{6,4},{7,5},{8,10},{9,11},{10,... | collective-permute-start | bytes 196616 | tf_op jit(solution)/shard_map/ppermute | solution.py:269
  6.9 6.2 %collective-permute-start.2 = (bf16[1,2,128,128]{3,2,1,0:T(8,128)(2,1)S(1)}, bf16[1,2,128,128]{3,2,1,0:T(8,128)(2,1)S(1)}, u32[]{:S(2)}, u32[]{:S(2)}) collective-permute-start(bf16[1,2,128,128]{3,2,1,0:T(8,128)(2,1)S(1)} %get-tuple-element.23), channel_id=1, source_target_pairs={{0,3},{1,2},{2,1},{3,0},{4,7},{5,6},{6,5},{7,4},{8,11},{9,10},{10,... | collective-permute-start | bytes 196616 | tf_op jit(solution)/shard_map/ppermute | solution.py:269
  8.2 5.0 %collective-permute-start.3 = (bf16[1,2,128,128]{3,2,1,0:T(8,128)(2,1)S(1)}, bf16[1,2,128,128]{3,2,1,0:T(8,128)(2,1)S(1)}, u32[]{:S(2)}, u32[]{:S(2)}) collective-permute-start(bf16[1,2,128,128]{3,2,1,0:T(8,128)(2,1)S(1)} %get-tuple-element.24), channel_id=1, source_target_pairs={{0,1},{1,0},{2,3},{3,2},{4,5},{5,4},{6,7},{7,6},{8,9},{9,8},{10,11... | collective-permute-start | bytes 196616 | tf_op jit(solution)/shard_map/ppermute | solution.py:269
  11.8 2.7 %copy-start = (f32[1,2,256,256]{3,2,1,0:T(8,128)S(1)}, f32[1,2,256,256]{3,2,1,0:T(8,128)}, u32[]{:S(2)}) copy-start(f32[1,2,256,256]{3,2,1,0:T(8,128)} %refs_0_.1) | copy-start | bytes 1572868
  13.5 5.1 %collective-permute-start.4 = (s16[1,272,256]{2,1,0:T(8,128)(2,1)S(1)}, s16[1,272,256]{2,1,0:T(8,128)(2,1)S(1)}, u32[]{:S(2)}, u32[]{:S(2)}) collective-permute-start(s16[1,272,256]{2,1,0:T(8,128)(2,1)S(1)} %get-tuple-element.30), channel_id=1, source_target_pairs={{0,8},{4,12},{8,0},{12,4},{1,9},{5,13},{9,1},{13,5},{2,10},{6,14},... | collective-permute-start | bytes 417800 | tf_op jit(solution)/shard_map/ppermute | solution.py:249
  15.4 3.2 %collective-permute-start.5 = (f32[1,128,512]{2,1,0:T(8,128)S(1)}, f32[1,128,512]{2,1,0:T(8,128)S(1)}, u32[]{:S(2)}, u32[]{:S(2)}) collective-permute-start(f32[1,128,512]{2,1,0:T(8,128)S(1)} %get-tuple-element.32.refs_2_), channel_id=1, source_target_pairs={{0,4},{4,0},{8,12},{12,8},{1,5},{5,1},{9,13},{13,9},{2,6},{6,2},{1... | collective-permute-start | bytes 786440 | tf_op jit(solution)/shard_map/ppermute | solution.py:249
  18.7 1.4 %collective-permute-start.6 = (s16[1,272,256]{2,1,0:T(8,128)(2,1)S(1)}, s16[1,272,256]{2,1,0:T(8,128)(2,1)S(1)}, u32[]{:S(2)}, u32[]{:S(2)}) collective-permute-start(s16[1,272,256]{2,1,0:T(8,128)(2,1)S(1)} %collective-permute-done.4.refs_3_), channel_id=1, source_target_pairs={{0,4},{4,0},{8,12},{12,8},{1,5},{5,1},{9,13},{13,9},{2,6},{6,2},{1... | collective-permute-start | bytes 417800 | tf_op jit(solution)/shard_map/ppermute | solution.py:249

commit v6 on v5

--- a/solution.py
+++ b/solution.py
@@ -67,20 +67,28 @@
         target = jnp.bitwise_xor(col_place, step)
         slots += [(step, node, target * sizes.nodes + node) for node in range(sizes.nodes)]
 
-    def choices(block):
-        lists = [row_lists[which, pl.ds(block, 1), :] for _, _, which in slots]
-        return jnp.concatenate([place_one_hot(picks, width) for picks in lists], axis=1)
+    nodes, blocks, _ = row_lists.shape
+    turned = row_lists[...].reshape(nodes * blocks, kept).astype(jnp.float32).T
+    turned_spots = lax.broadcasted_iota(jnp.int32, turned.shape, 1)
+    spots = lax.broadcasted_iota(jnp.int32, (kept, width), 1).astype(jnp.float32)
+
+    def row_choice(which, block):
+        mine = jnp.where(turned_spots == which * blocks + block, turned, 0.0)
+        picks = jnp.sum(mine, axis=1, keepdims=True)
+        return jnp.where(spots == picks, 1.0, 0.0).astype(jnp.bfloat16)
 
     for col_block in range(sizes.col_blocks):
-        col_choices = choices(col_block * sizes.grid_cols + col_place)
+        own_block = pl.ds(col_block * sizes.grid_cols + col_place, 1)
+        lists = [row_lists[which, own_block, :] for _, _, which in slots]
+        col_choices = jnp.concatenate([place_one_hot(picks, width) for picks in lists], axis=1)
         for row_block in range(sizes.row_blocks):
-            row_choices = choices(row_block * sizes.grid_rows + row_place)
-            halves = [surface[half, row_block, col_block] for half in range(2)]
-            taken = dot(jnp.concatenate(halves, axis=0), col_choices).astype(jnp.bfloat16)
-            for spot, (step, node, _) in enumerate(slots):
+            both = surface[:, row_block, col_block].reshape(2 * width, width)
+            taken = dot(both, col_choices).astype(jnp.bfloat16)
+            for spot, (step, node, which) in enumerate(slots):
                 cols = slice(spot * kept, (spot + 1) * kept)
                 both = jnp.concatenate([taken[:width, cols], taken[width:, cols]], axis=1)
-                block = dot(row_choices[:, cols], both, (0, 0)).astype(jnp.bfloat16)
+                choice = row_choice(which, row_block * sizes.grid_rows + row_place)
+                block = dot(choice, both).astype(jnp.bfloat16)
                 for half in range(2):
                     pieces[step][
                         node,
@@ -90,8 +98,8 @@
                     ] = block[:, half * kept : (half + 1) * kept]
 
 
-def block_at(sizes, block):
-    return pl.ds(pl.multiple_of(block * sizes.kept, sizes.kept), sizes.kept)
+def block_at(block, size):
+    return pl.ds(pl.multiple_of(block * size, size), size)
 
 
 def stack_kernel(sizes, factors, far_factor, stacked, arrival):
@@ -104,30 +112,32 @@
 
 def gather_kernel(sizes, both, whole_factor, turned_factor):
     row_place = lax.axis_index("row")
+    col_place = lax.axis_index("col")
+    kept = sizes.kept
     for core in range(2):
         for spot in range(sizes.grid_rows // 2):
             source = jnp.bitwise_xor(row_place - row_place % 2, 2 * spot) + core
             for node in range(sizes.nodes):
                 for block in range(sizes.row_blocks):
-                    place = block_at(sizes, block * sizes.grid_rows + source)
+                    ancestor = block * sizes.grid_rows + source
+                    step = jnp.bitwise_xor(ancestor % sizes.grid_cols, col_place)
+                    place = step * sizes.col_blocks + ancestor // sizes.grid_cols
                     halves = [both[core, spot, node, half, block] for half in range(2)]
                     wide = jnp.concatenate(halves, axis=1)
-                    whole_factor[node, place, :] = wide
-                    turned_factor[node, :, place] = wide.T
+                    whole_factor[node, block_at(place, kept), :] = wide
+                    turned = wide.T
+                    turned = jnp.concatenate([turned, turned], axis=1)
+                    turned_factor[node, :, block_at(ancestor, 2 * kept)] = turned
 
 
 def block_kernel(sizes, pieces, whole_factor, result, coded):
     width, rows = sizes.width, sizes.rows
-    col_place = lax.axis_index("col")
     for node in range(sizes.nodes):
-        surfaces, factors = [], []
-        for step, piece in pieces.items():
-            source = jnp.bitwise_xor(col_place, step)
-            surfaces.append(jnp.concatenate([piece[node, 0], piece[node, 1]], axis=0))
-            for block in range(sizes.col_blocks):
-                spot = block_at(sizes, block * sizes.grid_cols + source)
-                factors.append(whole_factor[node, spot, :])
-        product = dot(jnp.concatenate(surfaces, axis=1), jnp.concatenate(factors, axis=0))
+        halves = [
+            jnp.concatenate([pieces[step][node, half] for step in sorted(pieces)], axis=1)
+            for half in range(2)
+        ]
+        product = dot(jnp.concatenate(halves, axis=0), whole_factor[node])
         real = product[rows:, width:] - product[:rows, :width]
         imag = -(product[:rows, width:] + product[rows:, :width])
         result[node, :, :width] = real
@@ -138,10 +148,11 @@
 def encode(real, imag, coded):
     rows = real.shape[0]
     most = jnp.max(jnp.maximum(jnp.abs(real), jnp.abs(imag)), axis=0, keepdims=True)
-    level = jnp.ceil(jnp.log2(jnp.maximum(most, 1e-30)) * STEPS_PER_OCTAVE + 0.1)
+    level = jnp.ceil(jnp.log2(jnp.maximum(most, 1e-30)) * STEPS_PER_OCTAVE + 0.2)
     scale = jnp.exp2(15.0 - level / STEPS_PER_OCTAVE)
-    coded[:rows, :] = jnp.round(real * scale).astype(jnp.int32).astype(jnp.int16)
-    coded[rows : 2 * rows, :] = jnp.round(imag * scale).astype(jnp.int32).astype(jnp.int16)
+    for half, values in enumerate((real, imag)):
+        steps = jnp.clip(jnp.round(values * scale), -32767.0, 32767.0)
+        coded[half * rows : (half + 1) * rows, :] = steps.astype(jnp.int32).astype(jnp.int16)
     levels = jnp.broadcast_to(level, (16, level.shape[1]))
     coded[2 * rows :, :] = levels.astype(jnp.int32).astype(jnp.int16)
 
@@ -155,23 +166,21 @@
 
 
 def factor_times(sizes, node, terms, turned_factor, spots=None):
-    width = sizes.width
+    width, kept = sizes.width, sizes.kept
     spots = spots or slice(0, width)
     row_place = lax.axis_index("row")
-    reals, imags, rights = [], [], []
+    from_real = from_imag = 0.0
     for step, wide in terms.items():
         source = jnp.bitwise_xor(row_place, step)
-        places = [block_at(sizes, b * sizes.grid_rows + source) for b in range(sizes.row_blocks)]
         high = wide.astype(jnp.bfloat16)
         low = (wide - high.astype(jnp.float32)).astype(jnp.bfloat16)
-        for value in (high, low):
-            rights.append(value)
-            for place in places:
-                reals.append(turned_factor[node, spots.start : spots.stop, place])
-                imags.append(turned_factor[node, width + spots.start : width + spots.stop, place])
-    right = jnp.concatenate(rights, axis=0)
-    from_real = dot(jnp.concatenate(reals, axis=1), right)
-    from_imag = dot(jnp.concatenate(imags, axis=1), right)
+        for block in range(sizes.row_blocks):
+            rows = slice(block * kept, (block + 1) * kept)
+            right = jnp.concatenate([high[rows], low[rows]], axis=0)
+            place = block_at(block * sizes.grid_rows + source, 2 * kept)
+            from_real += dot(turned_factor[node, spots.start : spots.stop, place], right)
+            imag_spots = slice(width + spots.start, width + spots.stop)
+            from_imag += dot(turned_factor[node, imag_spots, place], right)
     real = from_real[:, :width] - from_imag[:, width:]
     imag = from_real[:, width:] + from_imag[:, :width]
     return real, imag
@@ -280,7 +289,7 @@
         functools.partial(gather_kernel, sizes),
         [
             jax.ShapeDtypeStruct((nodes, sizes.total, 2 * width), narrow),
-            jax.ShapeDtypeStruct((nodes, 2 * width, sizes.total), narrow),
+            jax.ShapeDtypeStruct((nodes, 2 * width, 2 * sizes.total), narrow),
         ],
         both,
     )

time: 21.3 us -> 21.3 us (level)
  no operation moved by 1% of the time
where the time goes in v6:
time: 21.3 us; the launch traced here: 21.1 us
  starting transfers between devices  8.19 us (38%)
  waiting for transfers between devices  5.51 us (26%)
  Pallas kernels  4.48 us (21%)
  blocking collectives  2.18 us (10%)
  between operations  0.72 us (3%)
    ppermute x3, starting transfers between devices, local(): arrived[step] = lax.ppermute(pieces[step], 'col', partners(grid_cols, step))  4.24 us
    ppermute x4, waiting for transfers between devices, over_rows(): return lax.ppermute(block, 'row', partners(grid_rows, step))  4.11 us
    pallas_call x6, Pallas kernels, call(): pl.pallas_call(flat_kernel, out_shape=out_shape, in_specs=[VMEM] * len(fl...  3.98 us
    ppermute x4, starting transfers between devices, over_rows(): return lax.ppermute(block, 'row', partners(grid_rows, step))  3.95 us
    all_gather x1, blocking collectives, local(): both = lax.all_gather(stacked, 'row', axis_index_groups=pairs)  2.18 us
    ppermute x3, waiting for transfers between devices, local(): arrived[step] = lax.ppermute(pieces[step], 'col', partners(grid_cols, step))  1.39 us
    pallas_call x1, Pallas kernels, local(): pl.pallas_call(functools.partial(pick_kernel, sizes), out_shape=[piece] *...  0.5 us
  transfers between devices with their start and end apart: 7, of which 4 were waited for; matrix products, arithmetic and copies ran while one was open for 0% of the time, Pallas kernels for 14%

profile of v6, /device:TPU:0, one launch (start us, length us, event | category | flops | bytes accessed | tf_op | source)
XLA Modules:
  0.0 21.1 jit_solution(13505929054746295338)
XLA Ops:
  0.6 0.0 copy-start.1
  0.6 0.0 copy-start.2
  0.7 3.0 %collective-permute-start = (bf16[1,2,1,128,256]{4,3,2,1,0:T(8,128)(2,1)}, bf16[1,2,1,128,256]{4,3,2,1,0:T(8,128)(2,1)S(1)}, u32[]{:S(2)}, u32[]{:S(2)}) collective-permute-start(bf16[1,2,1,128,256]{4,3,2,1,0:T(8,128)(2,1)} %bitcast.8), channel_id=1, source_target_pairs={{0,8},{4,12},{8,0},{12,4},{1,9},{5,13},{9,1},{13,5},{2,10},{6,14},... | collective-permute-start | bytes 393224 | tf_op jit(solution)/shard_map/ppermute | solution.py:258
  3.7 0.0 copy-done.1
  3.7 0.0 copy-done.2
  3.7 0.5 %shard_map.62 = (bf16[1,2,128,128]{3,2,1,0:T(8,128)(2,1)S(1)}, bf16[1,2,128,128]{3,2,1,0:T(8,128)(2,1)S(1)}, bf16[1,2,128,128]{3,2,1,0:T(8,128)(2,1)S(1)}, bf16[1,2,128,128]{3,2,1,0:T(8,128)(2,1)S(1)}) custom-call(bf16[2,1,1,256,256]{4,3,2,1,0:T(8,128)(2,1)S(1)} %bitcast.7, s32[4,4,128]{2,1,0:T(4,128)S(1)} %copy-done.2, f32[8,128]{1,0:T(8,128)S(1)} %shard_map.59.token), custom_call_target="tpu_custom_call" | custom-call | tf_op jit(solution)/shard_map/pallas_call | solution.py:268
  4.2 2.7 %collective-permute-start.1 = (bf16[1,2,128,128]{3,2,1,0:T(8,128)(2,1)S(1)}, bf16[1,2,128,128]{3,2,1,0:T(8,128)(2,1)S(1)}, u32[]{:S(2)}, u32[]{:S(2)}) collective-permute-start(bf16[1,2,128,128]{3,2,1,0:T(8,128)(2,1)S(1)} %get-tuple-element.22), channel_id=1, source_target_pairs={{0,2},{1,3},{2,0},{3,1},{4,6},{5,7},{6,4},{7,5},{8,10},{9,11},{10,... | collective-permute-start | bytes 196616 | tf_op jit(solution)/shard_map/ppermute | solution.py:278
  6.9 1.3 %collective-permute-start.2 = (bf16[1,2,128,128]{3,2,1,0:T(8,128)(2,1)S(1)}, bf16[1,2,128,128]{3,2,1,0:T(8,128)(2,1)S(1)}, u32[]{:S(2)}, u32[]{:S(2)}) collective-permute-start(bf16[1,2,128,128]{3,2,1,0:T(8,128)(2,1)S(1)} %get-tuple-element.23), channel_id=1, source_target_pairs={{0,3},{1,2},{2,1},{3,0},{4,7},{5,6},{6,5},{7,4},{8,11},{9,10},{10,... | collective-permute-start | bytes 196616 | tf_op jit(solution)/shard_map/ppermute | solution.py:278
  8.2 0.2 %collective-permute-start.3 = (bf16[1,2,128,128]{3,2,1,0:T(8,128)(2,1)S(1)}, bf16[1,2,128,128]{3,2,1,0:T(8,128)(2,1)S(1)}, u32[]{:S(2)}, u32[]{:S(2)}) collective-permute-start(bf16[1,2,128,128]{3,2,1,0:T(8,128)(2,1)S(1)} %get-tuple-element.24), channel_id=1, source_target_pairs={{0,1},{1,0},{2,3},{3,2},{4,5},{5,4},{6,7},{7,6},{8,9},{9,8},{10,11... | collective-permute-start | bytes 196616 | tf_op jit(solution)/shard_map/ppermute | solution.py:278
  8.4 0.0 collective-permute-done.refs_0_
  8.4 0.9 %shard_map.60 = bf16[2,1,2,1,128,256]{5,4,3,2,1,0:T(8,128)(2,1)S(1)} custom-call(bf16[1,2,1,128,256]{4,3,2,1,0:T(8,128)(2,1)S(1)} %collective-permute-done.refs_0_, bf16[1,2,1,128,256]{4,3,2,1,0:T(8,128)(2,1)} %bitcast.9), custom_call_target="tpu_custom_call" | custom-call | tf_op jit(solution)/shard_map/pallas_call | solution.py:232
  9.4 2.2 %all-gather = bf16[4,1,2,1,128,256]{5,4,3,2,1,0:T(8,128)(2,1)S(1)} all-gather(bf16[2,1,2,1,128,256]{5,4,3,2,1,0:T(8,128)(2,1)S(1)} %shard_map.60), channel_id=2, replica_groups={{0,4},{8,12},{1,5},{9,13},{2,6},{10,14},{3,7},{11,15},{16,20},{24,28},{..., dimensions={0}, use_global_device_ids=true | all-gather | bytes 786432 | tf_op jit(solution)/shard_map/all_gather | solution.py:287
  11.6 0.2 shard_map.61
  11.8 0.0 copy-start
  11.8 0.0 collective-permute-done.1.refs_1_
  11.8 1.3 %collective-permute-done.2.refs_2_ = bf16[1,2,128,128]{3,2,1,0:T(8,128)(2,1)S(1)} collective-permute-done((bf16[1,2,128,128]{3,2,1,0:T(8,128)(2,1)S(1)}, bf16[1,2,128,128]{3,2,1,0:T(8,128)(2,1)S(1)}, u32[]{:S(2)}, u32[]{:S(2)}) %collective-permute-start.2) | collective-permute-done | bytes 65568 | tf_op jit(solution)/shard_map/ppermute | solution.py:278
  13.1 0.1 collective-permute-done.3.refs_3_
  13.2 0.4 %shard_map.63 = (f32[1,128,512]{2,1,0:T(8,128)S(1)}, s16[1,272,256]{2,1,0:T(8,128)(2,1)S(1)}) custom-call(bf16[1,2,128,128]{3,2,1,0:T(8,128)(2,1)S(1)} %get-tuple-element.21.refs_0_, bf16[1,2,128,128]{3,2,1,0:T(8,128)(2,1)S(1)} %collective-permute-done.1.refs_1_, bf16[1,2,128,128]{3,2,1,0:T(8,128)(2,1)S(1)} %collective-permute-done.2.refs_2_, ...), custom_call_target="tpu_custom_call" | custom-call | tf_op jit(solution)/shard_map/pallas_call | solution.py:232
  13.5 0.9 %collective-permute-start.4 = (s16[1,272,256]{2,1,0:T(8,128)(2,1)S(1)}, s16[1,272,256]{2,1,0:T(8,128)(2,1)S(1)}, u32[]{:S(2)}, u32[]{:S(2)}) collective-permute-start(s16[1,272,256]{2,1,0:T(8,128)(2,1)S(1)} %get-tuple-element.30), channel_id=1, source_target_pairs={{0,8},{4,12},{8,0},{12,4},{1,9},{5,13},{9,1},{13,5},{2,10},{6,14},... | collective-permute-start | bytes 417800 | tf_op jit(solution)/shard_map/ppermute | solution.py:258
  14.5 0.0 copy-done
  14.5 1.0 %shard_map.64 = (f32[1,2,256,256]{3,2,1,0:T(8,128)S(1)}, f32[1,2,128,256]{3,2,1,0:T(8,128)}) custom-call(f32[1,2,256,256]{3,2,1,0:T(8,128)S(1)} %copy-done, bf16[1,512,1024]{2,1,0:T(8,128)(2,1)S(1)} %get-tuple-element.19.refs_1_, f32[1,128,512]{2,1,0:T(8,128)S(1)} %get-tuple-element.32.refs_2_), custom_call_target="tpu_custom_call" | custom-call | tf_op jit(solution)/shard_map/pallas_call | solution.py:232
  15.4 0.0 collective-permute-start.5
  15.4 3.2 %collective-permute-done.4.refs_3_ = s16[1,272,256]{2,1,0:T(8,128)(2,1)S(1)} collective-permute-done((s16[1,272,256]{2,1,0:T(8,128)(2,1)S(1)}, s16[1,272,256]{2,1,0:T(8,128)(2,1)S(1)}, u32[]{:S(2)}, u32[]{:S(2)}) %collective-permute-start.4) | collective-permute-done | bytes 139296 | tf_op jit(solution)/shard_map/ppermute | solution.py:258
  18.7 0.0 collective-permute-start.6
  18.7 0.0 collective-permute-done.5.refs_2_
  18.7 0.5 %shard_map.65.refs_0_ = f32[1,2,256,256]{3,2,1,0:T(8,128)S(1)} custom-call(f32[1,2,256,256]{3,2,1,0:T(8,128)S(1)} %get-tuple-element.31.refs_0_, bf16[1,512,1024]{2,1,0:T(8,128)(2,1)S(1)} %get-tuple-element.19.refs_1_, f32[1,128,512]{2,1,0:T(8,128)S(1)} %collective-permute-done.5.refs_2_, s16[1,272,256]{2,1,0:T(8,128)(2,1)S(1)} %collective-permute-done.4.refs_3_), custom_call_target="tpu_custom_call" | custom-call | tf_op jit(solution)/shard_map/pallas_call | solution.py:232
  19.2 0.9 %collective-permute-done.6.refs_2_ = s16[1,272,256]{2,1,0:T(8,128)(2,1)S(1)} collective-permute-done((s16[1,272,256]{2,1,0:T(8,128)(2,1)S(1)}, s16[1,272,256]{2,1,0:T(8,128)(2,1)S(1)}, u32[]{:S(2)}, u32[]{:S(2)}) %collective-permute-start.6) | collective-permute-done | bytes 139296 | tf_op jit(solution)/shard_map/ppermute | solution.py:258
  20.0 1.1 %shard_map.66 = f32[1,2,256,256]{3,2,1,0:T(8,128)} custom-call(f32[1,2,256,256]{3,2,1,0:T(8,128)S(1)} %shard_map.65.refs_0_, bf16[1,512,1024]{2,1,0:T(8,128)(2,1)S(1)} %get-tuple-element.19.refs_1_, s16[1,272,256]{2,1,0:T(8,128)(2,1)S(1)} %collective-permute-done.6.refs_2_), custom_call_target="tpu_custom_call" | custom-call | tf_op jit(solution)/shard_map/pallas_call | solution.py:232
  (1 shorter events, 0.0 us)
Async XLA Ops:
  0.6 3.1 %copy-start.1 = (bf16[2,1,1,256,1,1,256]{6,3,5,4,2,1,0:T(8,128)(2,1)S(1)}, bf16[2,1,1,256,1,1,256]{6,3,5,4,2,1,0:T(8,128)(2,1)}, u32[]{:S(2)}) copy-start(bf16[2,1,1,256,1,1,256]{6,3,5,4,2,1,0:T(8,128)(2,1)} %param.4) | copy-start | bytes 786436
  0.6 3.1 %copy-start.2 = (s32[4,4,128]{2,1,0:T(4,128)S(1)}, s32[4,4,128]{2,1,0:T(4,128)}, u32[]{:S(2)}) copy-start(s32[4,4,128]{2,1,0:T(4,128)} %row_lists.1) | copy-start | bytes 24580
  0.7 7.8 %collective-permute-start = (bf16[1,2,1,128,256]{4,3,2,1,0:T(8,128)(2,1)}, bf16[1,2,1,128,256]{4,3,2,1,0:T(8,128)(2,1)S(1)}, u32[]{:S(2)}, u32[]{:S(2)}) collective-permute-start(bf16[1,2,1,128,256]{4,3,2,1,0:T(8,128)(2,1)} %bitcast.8), channel_id=1, source_target_pairs={{0,8},{4,12},{8,0},{12,4},{1,9},{5,13},{9,1},{13,5},{2,10},{6,14},... | collective-permute-start | bytes 393224 | tf_op jit(solution)/shard_map/ppermute | solution.py:258
  4.2 7.6 %collective-permute-start.1 = (bf16[1,2,128,128]{3,2,1,0:T(8,128)(2,1)S(1)}, bf16[1,2,128,128]{3,2,1,0:T(8,128)(2,1)S(1)}, u32[]{:S(2)}, u32[]{:S(2)}) collective-permute-start(bf16[1,2,128,128]{3,2,1,0:T(8,128)(2,1)S(1)} %get-tuple-element.22), channel_id=1, source_target_pairs={{0,2},{1,3},{2,0},{3,1},{4,6},{5,7},{6,4},{7,5},{8,10},{9,11},{10,... | collective-permute-start | bytes 196616 | tf_op jit(solution)/shard_map/ppermute | solution.py:278
  6.9 6.2 %collective-permute-start.2 = (bf16[1,2,128,128]{3,2,1,0:T(8,128)(2,1)S(1)}, bf16[1,2,128,128]{3,2,1,0:T(8,128)(2,1)S(1)}, u32[]{:S(2)}, u32[]{:S(2)}) collective-permute-start(bf16[1,2,128,128]{3,2,1,0:T(8,128)(2,1)S(1)} %get-tuple-element.23), channel_id=1, source_target_pairs={{0,3},{1,2},{2,1},{3,0},{4,7},{5,6},{6,5},{7,4},{8,11},{9,10},{10,... | collective-permute-start | bytes 196616 | tf_op jit(solution)/shard_map/ppermute | solution.py:278
  8.2 5.0 %collective-permute-start.3 = (bf16[1,2,128,128]{3,2,1,0:T(8,128)(2,1)S(1)}, bf16[1,2,128,128]{3,2,1,0:T(8,128)(2,1)S(1)}, u32[]{:S(2)}, u32[]{:S(2)}) collective-permute-start(bf16[1,2,128,128]{3,2,1,0:T(8,128)(2,1)S(1)} %get-tuple-element.24), channel_id=1, source_target_pairs={{0,1},{1,0},{2,3},{3,2},{4,5},{5,4},{6,7},{7,6},{8,9},{9,8},{10,11... | collective-permute-start | bytes 196616 | tf_op jit(solution)/shard_map/ppermute | solution.py:278
  11.8 2.7 %copy-start = (f32[1,2,256,256]{3,2,1,0:T(8,128)S(1)}, f32[1,2,256,256]{3,2,1,0:T(8,128)}, u32[]{:S(2)}) copy-start(f32[1,2,256,256]{3,2,1,0:T(8,128)} %refs_0_.1) | copy-start | bytes 1572868
  13.5 5.1 %collective-permute-start.4 = (s16[1,272,256]{2,1,0:T(8,128)(2,1)S(1)}, s16[1,272,256]{2,1,0:T(8,128)(2,1)S(1)}, u32[]{:S(2)}, u32[]{:S(2)}) collective-permute-start(s16[1,272,256]{2,1,0:T(8,128)(2,1)S(1)} %get-tuple-element.30), channel_id=1, source_target_pairs={{0,8},{4,12},{8,0},{12,4},{1,9},{5,13},{9,1},{13,5},{2,10},{6,14},... | collective-permute-start | bytes 417800 | tf_op jit(solution)/shard_map/ppermute | solution.py:258
  15.4 3.2 %collective-permute-start.5 = (f32[1,128,512]{2,1,0:T(8,128)S(1)}, f32[1,128,512]{2,1,0:T(8,128)S(1)}, u32[]{:S(2)}, u32[]{:S(2)}) collective-permute-start(f32[1,128,512]{2,1,0:T(8,128)S(1)} %get-tuple-element.32.refs_2_), channel_id=1, source_target_pairs={{0,4},{4,0},{8,12},{12,8},{1,5},{5,1},{9,13},{13,9},{2,6},{6,2},{1... | collective-permute-start | bytes 786440 | tf_op jit(solution)/shard_map/ppermute | solution.py:258
  18.7 1.4 %collective-permute-start.6 = (s16[1,272,256]{2,1,0:T(8,128)(2,1)S(1)}, s16[1,272,256]{2,1,0:T(8,128)(2,1)S(1)}, u32[]{:S(2)}, u32[]{:S(2)}) collective-permute-start(s16[1,272,256]{2,1,0:T(8,128)(2,1)S(1)} %collective-permute-done.4.refs_3_), channel_id=1, source_target_pairs={{0,4},{4,0},{8,12},{12,8},{1,5},{5,1},{9,13},{13,9},{2,6},{6,2},{1... | collective-permute-start | bytes 417800 | tf_op jit(solution)/shard_map/ppermute | solution.py:258

commit v7 on v6

--- a/solution.py
+++ b/solution.py
@@ -13,7 +13,6 @@
 HBM = pl.BlockSpec(memory_space=pltpu.HBM)
 ANY = pl.BlockSpec(memory_space=pl.ANY)
 VMEM_BYTES = 24 * 1024 * 1024
-STEPS_PER_OCTAVE = 64
 CLAIMED_FLOPS = 92 * 10**6
 
 named = collections.OrderedDict
@@ -130,7 +129,7 @@
                     turned_factor[node, :, block_at(ancestor, 2 * kept)] = turned
 
 
-def block_kernel(sizes, pieces, whole_factor, result, coded):
+def block_kernel(sizes, pieces, whole_factor, result):
     width, rows = sizes.width, sizes.rows
     for node in range(sizes.nodes):
         halves = [
@@ -142,27 +141,6 @@
         imag = -(product[:rows, width:] + product[rows:, :width])
         result[node, :, :width] = real
         result[node, :, width:] = imag
-        encode(real, imag, coded.at[node])
-
-
-def encode(real, imag, coded):
-    rows = real.shape[0]
-    most = jnp.max(jnp.maximum(jnp.abs(real), jnp.abs(imag)), axis=0, keepdims=True)
-    level = jnp.ceil(jnp.log2(jnp.maximum(most, 1e-30)) * STEPS_PER_OCTAVE + 0.2)
-    scale = jnp.exp2(15.0 - level / STEPS_PER_OCTAVE)
-    for half, values in enumerate((real, imag)):
-        steps = jnp.clip(jnp.round(values * scale), -32767.0, 32767.0)
-        coded[half * rows : (half + 1) * rows, :] = steps.astype(jnp.int32).astype(jnp.int16)
-    levels = jnp.broadcast_to(level, (16, level.shape[1]))
-    coded[2 * rows :, :] = levels.astype(jnp.int32).astype(jnp.int16)
-
-
-def decode(coded):
-    rows = coded.shape[0] // 2 - 8
-    level = coded[2 * rows :, :].astype(jnp.int32).astype(jnp.float32)[:1]
-    scale = jnp.exp2(level / STEPS_PER_OCTAVE - 15.0)
-    values = coded[: 2 * rows, :].astype(jnp.int32).astype(jnp.float32) * scale
-    return jnp.concatenate([values[:rows], values[rows:]], axis=1)
 
 
 def factor_times(sizes, node, terms, turned_factor, spots=None):
@@ -196,19 +174,19 @@
         result[node, 1] = base[node, 1] - imag
 
 
-def middle_kernel(sizes, before, turned_factor, mate, coded, result):
+def middle_kernel(sizes, before, turned_factor, mate, sent, result):
     for node in range(sizes.nodes):
-        terms = {1: mate[node], **{step: decode(coded[step].at[node]) for step in coded}}
+        terms = {1: mate[node], **{step: sent[step][node] for step in sent}}
         real, imag = factor_times(sizes, node, terms, turned_factor)
         result[node, 0] = before[node, 0] - real
         result[node, 1] = before[node, 1] - imag
 
 
-def last_kernel(sizes, before, turned_factor, coded, result, held, sent):
+def last_kernel(sizes, before, turned_factor, forwarded, result, held, sent):
     half = sizes.width // 2
     copies = []
     for node in range(sizes.nodes):
-        terms = {step: decode(coded[step].at[node]) for step in coded}
+        terms = {step: forwarded[step][node] for step in forwarded}
         for turn in range(2):
             spots = slice(turn * half, (turn + 1) * half)
             real, imag = factor_times(sizes, node, terms, turned_factor, spots)
@@ -293,16 +271,13 @@
         ],
         both,
     )
-    block, coded = call(
+    (block,) = call(
         functools.partial(block_kernel, sizes),
-        [
-            jax.ShapeDtypeStruct((nodes, rows, 2 * width), wide),
-            jax.ShapeDtypeStruct((nodes, 2 * rows + 16, width), jnp.int16),
-        ],
+        [jax.ShapeDtypeStruct((nodes, rows, 2 * width), wide)],
         arrived,
         whole_factor,
     )
-    sent = named((step, over_rows(coded, step)) for step in across)
+    sent = named((step, over_rows(block, step)) for step in across)
     near, inverse_block = call(
         functools.partial(near_kernel, sizes),
         [square, jax.ShapeDtypeStruct((nodes, 2, rows, width), wide)],

time: 21.3 us -> 23.3 us (1.094)
  waiting for transfers between devices: 5.51 us -> 7.64 us
    ppermute x4, waiting for transfers between devices: 4.11 us -> 6.24 us  [over_rows(): return lax.ppermute(block, 'row', partners(grid_rows, step))]
  transfers between devices with their start and end apart: 7 -> 7, of which waited for: 4 -> 4; matrix products, arithmetic and copies ran while one was open for 0% -> 0% of each run, Pallas kernels for 14% -> 13%
where the time goes in v7:
time: 23.3 us; the launch traced here: 23.1 us
  starting transfers between devices  8.19 us (35%)
  waiting for transfers between devices  7.64 us (33%)
  Pallas kernels  4.38 us (19%)
  blocking collectives  2.18 us (9%)
  between operations  0.71 us (3%)
    ppermute x4, waiting for transfers between devices, over_rows(): return lax.ppermute(block, 'row', partners(grid_rows, step))  6.24 us
    ppermute x3, starting transfers between devices, local(): arrived[step] = lax.ppermute(pieces[step], 'col', partners(grid_cols, step))  4.24 us
    ppermute x4, starting transfers between devices, over_rows(): return lax.ppermute(block, 'row', partners(grid_rows, step))  3.95 us
    pallas_call x6, Pallas kernels, call(): pl.pallas_call(flat_kernel, out_shape=out_shape, in_specs=[VMEM] * len(fl...  3.87 us
    all_gather x1, blocking collectives, local(): both = lax.all_gather(stacked, 'row', axis_index_groups=pairs)  2.18 us
    ppermute x3, waiting for transfers between devices, local(): arrived[step] = lax.ppermute(pieces[step], 'col', partners(grid_cols, step))  1.4 us
    pallas_call x1, Pallas kernels, local(): pl.pallas_call(functools.partial(pick_kernel, sizes), out_shape=[piece] *...  0.5 us
  transfers between devices with their start and end apart: 7, of which 4 were waited for; matrix products, arithmetic and copies ran while one was open for 0% of the time, Pallas kernels for 13%

profile of v7, /device:TPU:0, one launch (start us, length us, event | category | flops | bytes accessed | tf_op | source)
XLA Modules:
  0.0 23.1 jit_solution(285580317487832632)
XLA Ops:
  0.6 0.0 copy-start.1
  0.6 0.0 copy-start.2
  0.7 3.0 %collective-permute-start = (bf16[1,2,1,128,256]{4,3,2,1,0:T(8,128)(2,1)}, bf16[1,2,1,128,256]{4,3,2,1,0:T(8,128)(2,1)S(1)}, u32[]{:S(2)}, u32[]{:S(2)}) collective-permute-start(bf16[1,2,1,128,256]{4,3,2,1,0:T(8,128)(2,1)} %bitcast.8), channel_id=1, source_target_pairs={{0,8},{4,12},{8,0},{12,4},{1,9},{5,13},{9,1},{13,5},{2,10},{6,14},... | collective-permute-start | bytes 393224 | tf_op jit(solution)/shard_map/ppermute | solution.py:236
  3.7 0.0 copy-done.1
  3.7 0.0 copy-done.2
  3.7 0.5 %shard_map.62 = (bf16[1,2,128,128]{3,2,1,0:T(8,128)(2,1)S(1)}, bf16[1,2,128,128]{3,2,1,0:T(8,128)(2,1)S(1)}, bf16[1,2,128,128]{3,2,1,0:T(8,128)(2,1)S(1)}, bf16[1,2,128,128]{3,2,1,0:T(8,128)(2,1)S(1)}) custom-call(bf16[2,1,1,256,256]{4,3,2,1,0:T(8,128)(2,1)S(1)} %bitcast.7, s32[4,4,128]{2,1,0:T(4,128)S(1)} %copy-done.2, f32[8,128]{1,0:T(8,128)S(1)} %shard_map.59.token), custom_call_target="tpu_custom_call" | custom-call | tf_op jit(solution)/shard_map/pallas_call | solution.py:246
  4.2 2.7 %collective-permute-start.1 = (bf16[1,2,128,128]{3,2,1,0:T(8,128)(2,1)S(1)}, bf16[1,2,128,128]{3,2,1,0:T(8,128)(2,1)S(1)}, u32[]{:S(2)}, u32[]{:S(2)}) collective-permute-start(bf16[1,2,128,128]{3,2,1,0:T(8,128)(2,1)S(1)} %get-tuple-element.20), channel_id=1, source_target_pairs={{0,2},{1,3},{2,0},{3,1},{4,6},{5,7},{6,4},{7,5},{8,10},{9,11},{10,... | collective-permute-start | bytes 196616 | tf_op jit(solution)/shard_map/ppermute | solution.py:256
  6.9 1.3 %collective-permute-start.2 = (bf16[1,2,128,128]{3,2,1,0:T(8,128)(2,1)S(1)}, bf16[1,2,128,128]{3,2,1,0:T(8,128)(2,1)S(1)}, u32[]{:S(2)}, u32[]{:S(2)}) collective-permute-start(bf16[1,2,128,128]{3,2,1,0:T(8,128)(2,1)S(1)} %get-tuple-element.21), channel_id=1, source_target_pairs={{0,3},{1,2},{2,1},{3,0},{4,7},{5,6},{6,5},{7,4},{8,11},{9,10},{10,... | collective-permute-start | bytes 196616 | tf_op jit(solution)/shard_map/ppermute | solution.py:256
  8.2 0.2 %collective-permute-start.3 = (bf16[1,2,128,128]{3,2,1,0:T(8,128)(2,1)S(1)}, bf16[1,2,128,128]{3,2,1,0:T(8,128)(2,1)S(1)}, u32[]{:S(2)}, u32[]{:S(2)}) collective-permute-start(bf16[1,2,128,128]{3,2,1,0:T(8,128)(2,1)S(1)} %get-tuple-element.22), channel_id=1, source_target_pairs={{0,1},{1,0},{2,3},{3,2},{4,5},{5,4},{6,7},{7,6},{8,9},{9,8},{10,11... | collective-permute-start | bytes 196616 | tf_op jit(solution)/shard_map/ppermute | solution.py:256
  8.4 0.0 collective-permute-done.refs_0_
  8.4 0.9 %shard_map.60 = bf16[2,1,2,1,128,256]{5,4,3,2,1,0:T(8,128)(2,1)S(1)} custom-call(bf16[1,2,1,128,256]{4,3,2,1,0:T(8,128)(2,1)S(1)} %collective-permute-done.refs_0_, bf16[1,2,1,128,256]{4,3,2,1,0:T(8,128)(2,1)} %bitcast.9), custom_call_target="tpu_custom_call" | custom-call | tf_op jit(solution)/shard_map/pallas_call | solution.py:210
  9.4 2.2 %all-gather = bf16[4,1,2,1,128,256]{5,4,3,2,1,0:T(8,128)(2,1)S(1)} all-gather(bf16[2,1,2,1,128,256]{5,4,3,2,1,0:T(8,128)(2,1)S(1)} %shard_map.60), channel_id=2, replica_groups={{0,4},{8,12},{1,5},{9,13},{2,6},{10,14},{3,7},{11,15},{16,20},{24,28},{..., dimensions={0}, use_global_device_ids=true | all-gather | bytes 786432 | tf_op jit(solution)/shard_map/all_gather | solution.py:265
  11.6 0.2 shard_map.61
  11.8 0.0 collective-permute-done.1.refs_1_
  11.8 1.3 %collective-permute-done.2.refs_2_ = bf16[1,2,128,128]{3,2,1,0:T(8,128)(2,1)S(1)} collective-permute-done((bf16[1,2,128,128]{3,2,1,0:T(8,128)(2,1)S(1)}, bf16[1,2,128,128]{3,2,1,0:T(8,128)(2,1)S(1)}, u32[]{:S(2)}, u32[]{:S(2)}) %collective-permute-start.2) | collective-permute-done | bytes 65568 | tf_op jit(solution)/shard_map/ppermute | solution.py:256
  13.1 0.1 collective-permute-done.3.refs_3_
  13.2 0.0 copy-start
  13.2 0.3 %shard_map.63.refs_2_ = f32[1,128,512]{2,1,0:T(8,128)S(1)} custom-call(bf16[1,2,128,128]{3,2,1,0:T(8,128)(2,1)S(1)} %get-tuple-element.19.refs_0_, bf16[1,2,128,128]{3,2,1,0:T(8,128)(2,1)S(1)} %collective-permute-done.1.refs_1_, bf16[1,2,128,128]{3,2,1,0:T(8,128)(2,1)S(1)} %collective-permute-done.2.refs_2_, ...), custom_call_target="tpu_custom_call" | custom-call | tf_op jit(solution)/shard_map/pallas_call | solution.py:210
  13.5 0.9 %collective-permute-start.4 = (f32[1,128,512]{2,1,0:T(8,128)S(1)}, f32[1,128,512]{2,1,0:T(8,128)S(1)}, u32[]{:S(2)}, u32[]{:S(2)}) collective-permute-start(f32[1,128,512]{2,1,0:T(8,128)S(1)} %shard_map.63.refs_2_), channel_id=1, source_target_pairs={{0,8},{4,12},{8,0},{12,4},{1,9},{5,13},{9,1},{13,5},{2,10},{6,14},... | collective-permute-start | bytes 786440 | tf_op jit(solution)/shard_map/ppermute | solution.py:236
  14.4 0.0 copy-done
  14.4 1.0 %shard_map.64 = (f32[1,2,256,256]{3,2,1,0:T(8,128)S(1)}, f32[1,2,128,256]{3,2,1,0:T(8,128)}) custom-call(f32[1,2,256,256]{3,2,1,0:T(8,128)S(1)} %copy-done, bf16[1,512,1024]{2,1,0:T(8,128)(2,1)S(1)} %get-tuple-element.17.refs_1_, f32[1,128,512]{2,1,0:T(8,128)S(1)} %shard_map.63.refs_2_), custom_call_target="tpu_custom_call" | custom-call | tf_op jit(solution)/shard_map/pallas_call | solution.py:210
  15.4 0.0 collective-permute-start.5
  15.4 5.2 %collective-permute-done.4.refs_3_ = f32[1,128,512]{2,1,0:T(8,128)S(1)} collective-permute-done((f32[1,128,512]{2,1,0:T(8,128)S(1)}, f32[1,128,512]{2,1,0:T(8,128)S(1)}, u32[]{:S(2)}, u32[]{:S(2)}) %collective-permute-start.4) | collective-permute-done | bytes 262176 | tf_op jit(solution)/shard_map/ppermute | solution.py:236
  20.5 0.0 collective-permute-start.6
  20.5 0.0 collective-permute-done.5.refs_2_
  20.5 0.4 %shard_map.65.refs_0_ = f32[1,2,256,256]{3,2,1,0:T(8,128)S(1)} custom-call(f32[1,2,256,256]{3,2,1,0:T(8,128)S(1)} %get-tuple-element.27.refs_0_, bf16[1,512,1024]{2,1,0:T(8,128)(2,1)S(1)} %get-tuple-element.17.refs_1_, f32[1,128,512]{2,1,0:T(8,128)S(1)} %collective-permute-done.5.refs_2_, f32[1,128,512]{2,1,0:T(8,128)S(1)} %collective-permute-done.4.refs_3_), custom_call_target="tpu_custom_call" | custom-call | tf_op jit(solution)/shard_map/pallas_call | solution.py:210
  21.0 1.1 %collective-permute-done.6.refs_2_ = f32[1,128,512]{2,1,0:T(8,128)S(1)} collective-permute-done((f32[1,128,512]{2,1,0:T(8,128)S(1)}, f32[1,128,512]{2,1,0:T(8,128)S(1)}, u32[]{:S(2)}, u32[]{:S(2)}) %collective-permute-start.6) | collective-permute-done | bytes 262176 | tf_op jit(solution)/shard_map/ppermute | solution.py:236
  22.1 1.0 %shard_map.66 = f32[1,2,256,256]{3,2,1,0:T(8,128)} custom-call(f32[1,2,256,256]{3,2,1,0:T(8,128)S(1)} %shard_map.65.refs_0_, bf16[1,512,1024]{2,1,0:T(8,128)(2,1)S(1)} %get-tuple-element.17.refs_1_, f32[1,128,512]{2,1,0:T(8,128)S(1)} %collective-permute-done.6.refs_2_), custom_call_target="tpu_custom_call" | custom-call | tf_op jit(solution)/shard_map/pallas_call | solution.py:210
  (1 shorter events, 0.0 us)
Async XLA Ops:
  0.6 3.1 %copy-start.1 = (bf16[2,1,1,256,1,1,256]{6,3,5,4,2,1,0:T(8,128)(2,1)S(1)}, bf16[2,1,1,256,1,1,256]{6,3,5,4,2,1,0:T(8,128)(2,1)}, u32[]{:S(2)}) copy-start(bf16[2,1,1,256,1,1,256]{6,3,5,4,2,1,0:T(8,128)(2,1)} %param.4) | copy-start | bytes 786436
  0.6 3.1 %copy-start.2 = (s32[4,4,128]{2,1,0:T(4,128)S(1)}, s32[4,4,128]{2,1,0:T(4,128)}, u32[]{:S(2)}) copy-start(s32[4,4,128]{2,1,0:T(4,128)} %row_lists.1) | copy-start | bytes 24580
  0.7 7.8 %collective-permute-start = (bf16[1,2,1,128,256]{4,3,2,1,0:T(8,128)(2,1)}, bf16[1,2,1,128,256]{4,3,2,1,0:T(8,128)(2,1)S(1)}, u32[]{:S(2)}, u32[]{:S(2)}) collective-permute-start(bf16[1,2,1,128,256]{4,3,2,1,0:T(8,128)(2,1)} %bitcast.8), channel_id=1, source_target_pairs={{0,8},{4,12},{8,0},{12,4},{1,9},{5,13},{9,1},{13,5},{2,10},{6,14},... | collective-permute-start | bytes 393224 | tf_op jit(solution)/shard_map/ppermute | solution.py:236
  4.2 7.6 %collective-permute-start.1 = (bf16[1,2,128,128]{3,2,1,0:T(8,128)(2,1)S(1)}, bf16[1,2,128,128]{3,2,1,0:T(8,128)(2,1)S(1)}, u32[]{:S(2)}, u32[]{:S(2)}) collective-permute-start(bf16[1,2,128,128]{3,2,1,0:T(8,128)(2,1)S(1)} %get-tuple-element.20), channel_id=1, source_target_pairs={{0,2},{1,3},{2,0},{3,1},{4,6},{5,7},{6,4},{7,5},{8,10},{9,11},{10,... | collective-permute-start | bytes 196616 | tf_op jit(solution)/shard_map/ppermute | solution.py:256
  6.9 6.2 %collective-permute-start.2 = (bf16[1,2,128,128]{3,2,1,0:T(8,128)(2,1)S(1)}, bf16[1,2,128,128]{3,2,1,0:T(8,128)(2,1)S(1)}, u32[]{:S(2)}, u32[]{:S(2)}) collective-permute-start(bf16[1,2,128,128]{3,2,1,0:T(8,128)(2,1)S(1)} %get-tuple-element.21), channel_id=1, source_target_pairs={{0,3},{1,2},{2,1},{3,0},{4,7},{5,6},{6,5},{7,4},{8,11},{9,10},{10,... | collective-permute-start | bytes 196616 | tf_op jit(solution)/shard_map/ppermute | solution.py:256
  8.2 5.0 %collective-permute-start.3 = (bf16[1,2,128,128]{3,2,1,0:T(8,128)(2,1)S(1)}, bf16[1,2,128,128]{3,2,1,0:T(8,128)(2,1)S(1)}, u32[]{:S(2)}, u32[]{:S(2)}) collective-permute-start(bf16[1,2,128,128]{3,2,1,0:T(8,128)(2,1)S(1)} %get-tuple-element.22), channel_id=1, source_target_pairs={{0,1},{1,0},{2,3},{3,2},{4,5},{5,4},{6,7},{7,6},{8,9},{9,8},{10,11... | collective-permute-start | bytes 196616 | tf_op jit(solution)/shard_map/ppermute | solution.py:256
  13.2 1.2 %copy-start = (f32[1,2,256,256]{3,2,1,0:T(8,128)S(1)}, f32[1,2,256,256]{3,2,1,0:T(8,128)}, u32[]{:S(2)}) copy-start(f32[1,2,256,256]{3,2,1,0:T(8,128)} %refs_0_.1) | copy-start | bytes 1572868
  13.5 7.0 %collective-permute-start.4 = (f32[1,128,512]{2,1,0:T(8,128)S(1)}, f32[1,128,512]{2,1,0:T(8,128)S(1)}, u32[]{:S(2)}, u32[]{:S(2)}) collective-permute-start(f32[1,128,512]{2,1,0:T(8,128)S(1)} %shard_map.63.refs_2_), channel_id=1, source_target_pairs={{0,8},{4,12},{8,0},{12,4},{1,9},{5,13},{9,1},{13,5},{2,10},{6,14},... | collective-permute-start | bytes 786440 | tf_op jit(solution)/shard_map/ppermute | solution.py:236
  15.4 5.2 %collective-permute-start.5 = (f32[1,128,512]{2,1,0:T(8,128)S(1)}, f32[1,128,512]{2,1,0:T(8,128)S(1)}, u32[]{:S(2)}, u32[]{:S(2)}) collective-permute-start(f32[1,128,512]{2,1,0:T(8,128)S(1)} %shard_map.63.refs_2_), channel_id=1, source_target_pairs={{0,4},{4,0},{8,12},{12,8},{1,5},{5,1},{9,13},{13,9},{2,6},{6,2},{1... | collective-permute-start | bytes 786440 | tf_op jit(solution)/shard_map/ppermute | solution.py:236
  20.5 1.5 %collective-permute-start.6 = (f32[1,128,512]{2,1,0:T(8,128)S(1)}, f32[1,128,512]{2,1,0:T(8,128)S(1)}, u32[]{:S(2)}, u32[]{:S(2)}) collective-permute-start(f32[1,128,512]{2,1,0:T(8,128)S(1)} %collective-permute-done.4.refs_3_), channel_id=1, source_target_pairs={{0,4},{4,0},{8,12},{12,8},{1,5},{5,1},{9,13},{13,9},{2,6},{6,2},{1... | collective-permute-start | bytes 786440 | tf_op jit(solution)/shard_map/ppermute | solution.py:236

commit v8 on v6

--- a/solution.py
+++ b/solution.py
@@ -57,16 +57,14 @@
     result[...] = jnp.zeros_like(result)
 
 
-def pick_kernel(sizes, surface, row_lists, token, *pieces):
-    del token
+def pick(sizes, steps, surface, row_lists, pieces):
     row_place = lax.axis_index("row")
     col_place = lax.axis_index("col")
     kept, width = sizes.kept, sizes.width
     slots = []
-    for step in range(sizes.grid_cols):
+    for step in steps:
         target = jnp.bitwise_xor(col_place, step)
         slots += [(step, node, target * sizes.nodes + node) for node in range(sizes.nodes)]
-
     nodes, blocks, _ = row_lists.shape
     turned = row_lists[...].reshape(nodes * blocks, kept).astype(jnp.float32).T
     turned_spots = lax.broadcasted_iota(jnp.int32, turned.shape, 1)
@@ -98,19 +96,35 @@
                     ] = block[:, half * kept : (half + 1) * kept]
 
 
+def pick_kernel(sizes, surface, row_lists, token, *pieces):
+    del token
+    steps = range(1, sizes.grid_cols)
+    pick(sizes, steps, surface, row_lists, dict(zip(steps, pieces)))
+
+
 def block_at(block, size):
     return pl.ds(pl.multiple_of(block * size, size), size)
 
 
-def stack_kernel(sizes, factors, far_factor, stacked, arrival):
+def stack_kernel(sizes, factors, surface, row_lists, far_factor, stacked, piece, arrival):
     copy = pltpu.make_async_copy(far_factor, stacked.at[0], arrival)
     copy.start()
     for spot, step in enumerate(factors):
         stacked[spot + 1] = factors[step][...]
+    pick(sizes, [0], surface, row_lists, [piece])
     copy.wait()
 
 
-def gather_kernel(sizes, both, whole_factor, turned_factor):
+def product_of(sizes, node, pieces, whole_factor):
+    rows = sizes.col_blocks * sizes.kept
+    lefts, rights = [], []
+    for step, piece in pieces.items():
+        lefts.append(jnp.concatenate([piece[node, 0], piece[node, 1]], axis=0))
+        rights.append(whole_factor[node, step * rows : (step + 1) * rows, :])
+    return dot(jnp.concatenate(lefts, axis=1), jnp.concatenate(rights, axis=0))
+
+
+def gather_kernel(sizes, both, pieces, whole_factor, turned_factor, early):
     row_place = lax.axis_index("row")
     col_place = lax.axis_index("col")
     kept = sizes.kept
@@ -128,16 +142,14 @@
                     turned = wide.T
                     turned = jnp.concatenate([turned, turned], axis=1)
                     turned_factor[node, :, block_at(ancestor, 2 * kept)] = turned
-
-
-def block_kernel(sizes, pieces, whole_factor, result, coded):
+    for node in range(sizes.nodes):
+        early[node] = product_of(sizes, node, pieces, whole_factor)
+
+
+def block_kernel(sizes, pieces, whole_factor, early, result, coded):
     width, rows = sizes.width, sizes.rows
     for node in range(sizes.nodes):
-        halves = [
-            jnp.concatenate([pieces[step][node, half] for step in sorted(pieces)], axis=1)
-            for half in range(2)
-        ]
-        product = dot(jnp.concatenate(halves, axis=0), whole_factor[node])
+        product = early[node] + product_of(sizes, node, pieces, whole_factor)
         real = product[rows:, width:] - product[:rows, :width]
         imag = -(product[:rows, width:] + product[rows:, :width])
         result[node, :, :width] = real
@@ -267,31 +279,36 @@
     piece = jax.ShapeDtypeStruct((nodes, 2, rows, col_blocks * kept), narrow)
     pieces = pl.pallas_call(
         functools.partial(pick_kernel, sizes),
-        out_shape=[piece] * grid_cols,
+        out_shape=[piece] * (grid_cols - 1),
         in_specs=[VMEM, VMEM, ANY],
-        out_specs=[VMEM] * grid_cols,
+        out_specs=[VMEM] * (grid_cols - 1),
         compiler_params=pltpu.CompilerParams(vmem_limit_bytes=VMEM_BYTES),
     )(surface, row_lists, token)
     factors = named((step, over_rows(sent_factor, step)) for step in across)
-    arrived = named({0: pieces[0]})
+    arrived = named()
     for step in [*range(grid_cols // 2, grid_cols), *range(grid_cols // 2 - 1, 0, -1)]:
-        arrived[step] = lax.ppermute(pieces[step], "col", partners(grid_cols, step))
-    (stacked,) = call(
+        arrived[step] = lax.ppermute(pieces[step - 1], "col", partners(grid_cols, step))
+    stacked, own_piece = call(
         functools.partial(stack_kernel, sizes),
-        [jax.ShapeDtypeStruct((grid_rows // 2, *own_factor.shape), narrow)],
+        [jax.ShapeDtypeStruct((grid_rows // 2, *own_factor.shape), narrow), piece],
         factors,
+        surface,
+        row_lists,
         remote=[sent_factor],
         scratch=[pltpu.SemaphoreType.DMA],
     )
     pairs = [[place, place + 1] for place in range(0, grid_rows, 2)]
     both = lax.all_gather(stacked, "row", axis_index_groups=pairs)
-    whole_factor, turned_factor = call(
+    first = named({0: own_piece, grid_cols // 2: arrived.pop(grid_cols // 2)})
+    whole_factor, turned_factor, early = call(
         functools.partial(gather_kernel, sizes),
         [
             jax.ShapeDtypeStruct((nodes, sizes.total, 2 * width), narrow),
             jax.ShapeDtypeStruct((nodes, 2 * width, 2 * sizes.total), narrow),
+            jax.ShapeDtypeStruct((nodes, 2 * rows, 2 * width), wide),
         ],
         both,
+        first,
     )
     block, coded = call(
         functools.partial(block_kernel, sizes),
@@ -301,6 +318,7 @@
         ],
         arrived,
         whole_factor,
+        early,
     )
     sent = named((step, over_rows(coded, step)) for step in across)
     near, inverse_block = call(

time: 21.3 us -> 21.2 us (level)
  transfers between devices with their start and end apart: 7 -> 7, of which waited for: 4 -> 4; matrix products, arithmetic and copies ran while one was open for 0% -> 0% of each run, Pallas kernels for 14% -> 15%
where the time goes in v8:
time: 21.2 us; the launch traced here: 21 us
  starting transfers between devices  8.19 us (39%)
  waiting for transfers between devices  5.42 us (26%)
  Pallas kernels  4.5 us (21%)
  blocking collectives  2.18 us (10%)
  between operations  0.7 us (3%)
    ppermute x3, starting transfers between devices, local(): lax.ppermute(pieces[step - 1], 'col', partners(grid_cols, step))  4.24 us
    ppermute x4, waiting for transfers between devices, over_rows(): return lax.ppermute(block, 'row', partners(grid_rows, step))  4.12 us
    pallas_call x6, Pallas kernels, call(): pl.pallas_call(flat_kernel, out_shape=out_shape, in_specs=[VMEM] * len(fl...  4.02 us
    ppermute x4, starting transfers between devices, over_rows(): return lax.ppermute(block, 'row', partners(grid_rows, step))  3.96 us
    all_gather x1, blocking collectives, local(): both = lax.all_gather(stacked, 'row', axis_index_groups=pairs)  2.18 us
    ppermute x3, waiting for transfers between devices, local(): lax.ppermute(pieces[step - 1], 'col', partners(grid_cols, step))  1.3 us
    pallas_call x1, Pallas kernels, local(): pl.pallas_call(functools.partial(pick_kernel, sizes), out_shape=[piece] *...  0.48 us
  transfers between devices with their start and end apart: 7, of which 4 were waited for; matrix products, arithmetic and copies ran while one was open for 0% of the time, Pallas kernels for 15%

profile of v8, /device:TPU:0, one launch (start us, length us, event | category | flops | bytes accessed | tf_op | source)
XLA Modules:
  0.0 21.0 jit_solution(14301191301785951391)
XLA Ops:
  0.6 0.0 copy-start
  0.6 0.0 copy-start.2
  0.7 3.0 %collective-permute-start = (bf16[1,2,1,128,256]{4,3,2,1,0:T(8,128)(2,1)}, bf16[1,2,1,128,256]{4,3,2,1,0:T(8,128)(2,1)S(1)}, u32[]{:S(2)}, u32[]{:S(2)}) collective-permute-start(bf16[1,2,1,128,256]{4,3,2,1,0:T(8,128)(2,1)} %bitcast.9), channel_id=1, source_target_pairs={{0,8},{4,12},{8,0},{12,4},{1,9},{5,13},{9,1},{13,5},{2,10},{6,14},... | collective-permute-start | bytes 393224 | tf_op jit(solution)/shard_map/ppermute | solution.py:270
  3.7 0.0 copy-done
  3.7 0.0 copy-done.2
  3.7 0.5 %shard_map.61 = (bf16[1,2,128,128]{3,2,1,0:T(8,128)(2,1)S(1)}, bf16[1,2,128,128]{3,2,1,0:T(8,128)(2,1)S(1)}, bf16[1,2,128,128]{3,2,1,0:T(8,128)(2,1)S(1)}) custom-call(bf16[2,1,1,256,256]{4,3,2,1,0:T(8,128)(2,1)S(1)} %bitcast.7, s32[4,4,128]{2,1,0:T(4,128)S(1)} %copy-done.2, f32[8,128]{1,0:T(8,128)S(1)} %shard_map.59.token), custom_call_target="tpu_custom_call" | custom-call | tf_op jit(solution)/shard_map/pallas_call | solution.py:280
  4.2 2.7 %collective-permute-start.1 = (bf16[1,2,128,128]{3,2,1,0:T(8,128)(2,1)S(1)}, bf16[1,2,128,128]{3,2,1,0:T(8,128)(2,1)S(1)}, u32[]{:S(2)}, u32[]{:S(2)}) collective-permute-start(bf16[1,2,128,128]{3,2,1,0:T(8,128)(2,1)S(1)} %get-tuple-element.24), channel_id=1, source_target_pairs={{0,2},{1,3},{2,0},{3,1},{4,6},{5,7},{6,4},{7,5},{8,10},{9,11},{10,... | collective-permute-start | bytes 196616 | tf_op jit(solution)/shard_map/ppermute | solution.py:290
  6.8 1.3 %collective-permute-start.2 = (bf16[1,2,128,128]{3,2,1,0:T(8,128)(2,1)S(1)}, bf16[1,2,128,128]{3,2,1,0:T(8,128)(2,1)S(1)}, u32[]{:S(2)}, u32[]{:S(2)}) collective-permute-start(bf16[1,2,128,128]{3,2,1,0:T(8,128)(2,1)S(1)} %get-tuple-element.26), channel_id=1, source_target_pairs={{0,3},{1,2},{2,1},{3,0},{4,7},{5,6},{6,5},{7,4},{8,11},{9,10},{10,... | collective-permute-start | bytes 196616 | tf_op jit(solution)/shard_map/ppermute | solution.py:290
  8.2 0.2 %collective-permute-start.3 = (bf16[1,2,128,128]{3,2,1,0:T(8,128)(2,1)S(1)}, bf16[1,2,128,128]{3,2,1,0:T(8,128)(2,1)S(1)}, u32[]{:S(2)}, u32[]{:S(2)}) collective-permute-start(bf16[1,2,128,128]{3,2,1,0:T(8,128)(2,1)S(1)} %get-tuple-element.27), channel_id=1, source_target_pairs={{0,1},{1,0},{2,3},{3,2},{4,5},{5,4},{6,7},{7,6},{8,9},{9,8},{10,11... | collective-permute-start | bytes 196616 | tf_op jit(solution)/shard_map/ppermute | solution.py:290
  8.4 0.0 collective-permute-done.refs_0_
  8.4 0.9 %shard_map.60 = (bf16[2,1,2,1,128,256]{5,4,3,2,1,0:T(8,128)(2,1)S(1)}, bf16[1,2,128,128]{3,2,1,0:T(8,128)(2,1)S(1)}) custom-call(bf16[1,2,1,128,256]{4,3,2,1,0:T(8,128)(2,1)S(1)} %collective-permute-done.refs_0_, bf16[2,1,1,256,256]{4,3,2,1,0:T(8,128)(2,1)S(1)} %bitcast.8, s32[4,4,128]{2,1,0:T(4,128)S(1)} %copy-done.2, bf16[1,2,1,128,256]{4,3,2,1,0:T(8,128)(2,1)} %bitcast.10), custom_call_target="tpu_custom_call" | custom-call | tf_op jit(solution)/shard_map/pallas_call | solution.py:244
  9.4 2.2 %all-gather = bf16[4,1,2,1,128,256]{5,4,3,2,1,0:T(8,128)(2,1)S(1)} all-gather(bf16[2,1,2,1,128,256]{5,4,3,2,1,0:T(8,128)(2,1)S(1)} %get-tuple-element.21), channel_id=2, replica_groups={{0,4},{8,12},{1,5},{9,13},{2,6},{10,14},{3,7},{11,15},{16,20},{24,28},{..., dimensions={0}, use_global_device_ids=true | all-gather | bytes 786432 | tf_op jit(solution)/shard_map/all_gather | solution.py:301
  11.5 0.0 collective-permute-done.1.refs_2_
  11.5 0.3 %shard_map.62 = (bf16[1,512,512]{2,1,0:T(8,128)(2,1)S(1)}, bf16[1,512,1024]{2,1,0:T(8,128)(2,1)S(1)}, f32[1,256,512]{2,1,0:T(8,128)S(1)}) custom-call(bf16[2,2,1,2,1,128,256]{6,5,4,3,2,1,0:T(8,128)(2,1)S(1)} %bitcast.6, bf16[1,2,128,128]{3,2,1,0:T(8,128)(2,1)S(1)} %get-tuple-element.22.refs_1_, bf16[1,2,128,128]{3,2,1,0:T(8,128)(2,1)S(1)} %collective-permute-done.1.refs_2_), custom_call_target="tpu_custom_call" | custom-call | tf_op jit(solution)/shard_map/pallas_call | solution.py:244
  11.9 1.2 %collective-permute-done.2.refs_0_ = bf16[1,2,128,128]{3,2,1,0:T(8,128)(2,1)S(1)} collective-permute-done((bf16[1,2,128,128]{3,2,1,0:T(8,128)(2,1)S(1)}, bf16[1,2,128,128]{3,2,1,0:T(8,128)(2,1)S(1)}, u32[]{:S(2)}, u32[]{:S(2)}) %collective-permute-start.2) | collective-permute-done | bytes 65568 | tf_op jit(solution)/shard_map/ppermute | solution.py:290
  13.1 0.1 collective-permute-done.3.refs_1_
  13.2 0.0 copy-start.1
  13.2 0.3 %shard_map.63 = (f32[1,128,512]{2,1,0:T(8,128)S(1)}, s16[1,272,256]{2,1,0:T(8,128)(2,1)S(1)}) custom-call(bf16[1,2,128,128]{3,2,1,0:T(8,128)(2,1)S(1)} %collective-permute-done.2.refs_0_, bf16[1,2,128,128]{3,2,1,0:T(8,128)(2,1)S(1)} %collective-permute-done.3.refs_1_, bf16[1,512,512]{2,1,0:T(8,128)(2,1)S(1)} %get-tuple-element.28.refs_2_, ...), custom_call_target="tpu_custom_call" | custom-call | tf_op jit(solution)/shard_map/pallas_call | solution.py:244
  13.5 0.9 %collective-permute-start.4 = (s16[1,272,256]{2,1,0:T(8,128)(2,1)S(1)}, s16[1,272,256]{2,1,0:T(8,128)(2,1)S(1)}, u32[]{:S(2)}, u32[]{:S(2)}) collective-permute-start(s16[1,272,256]{2,1,0:T(8,128)(2,1)S(1)} %get-tuple-element.34), channel_id=1, source_target_pairs={{0,8},{4,12},{8,0},{12,4},{1,9},{5,13},{9,1},{13,5},{2,10},{6,14},... | collective-permute-start | bytes 417800 | tf_op jit(solution)/shard_map/ppermute | solution.py:270
  14.4 0.0 copy-done.1
  14.4 1.0 %shard_map.64 = (f32[1,2,256,256]{3,2,1,0:T(8,128)S(1)}, f32[1,2,128,256]{3,2,1,0:T(8,128)}) custom-call(f32[1,2,256,256]{3,2,1,0:T(8,128)S(1)} %copy-done.1, bf16[1,512,1024]{2,1,0:T(8,128)(2,1)S(1)} %get-tuple-element.25.refs_1_, f32[1,128,512]{2,1,0:T(8,128)S(1)} %get-tuple-element.36.refs_2_), custom_call_target="tpu_custom_call" | custom-call | tf_op jit(solution)/shard_map/pallas_call | solution.py:244
  15.3 0.0 collective-permute-start.5
  15.3 3.2 %collective-permute-done.4.refs_3_ = s16[1,272,256]{2,1,0:T(8,128)(2,1)S(1)} collective-permute-done((s16[1,272,256]{2,1,0:T(8,128)(2,1)S(1)}, s16[1,272,256]{2,1,0:T(8,128)(2,1)S(1)}, u32[]{:S(2)}, u32[]{:S(2)}) %collective-permute-start.4) | collective-permute-done | bytes 139296 | tf_op jit(solution)/shard_map/ppermute | solution.py:270
  18.6 0.0 collective-permute-start.6
  18.6 0.0 collective-permute-done.5.refs_2_
  18.6 0.5 %shard_map.65.refs_0_ = f32[1,2,256,256]{3,2,1,0:T(8,128)S(1)} custom-call(f32[1,2,256,256]{3,2,1,0:T(8,128)S(1)} %get-tuple-element.35.refs_0_, bf16[1,512,1024]{2,1,0:T(8,128)(2,1)S(1)} %get-tuple-element.25.refs_1_, f32[1,128,512]{2,1,0:T(8,128)S(1)} %collective-permute-done.5.refs_2_, s16[1,272,256]{2,1,0:T(8,128)(2,1)S(1)} %collective-permute-done.4.refs_3_), custom_call_target="tpu_custom_call" | custom-call | tf_op jit(solution)/shard_map/pallas_call | solution.py:244
  19.1 0.9 %collective-permute-done.6.refs_2_ = s16[1,272,256]{2,1,0:T(8,128)(2,1)S(1)} collective-permute-done((s16[1,272,256]{2,1,0:T(8,128)(2,1)S(1)}, s16[1,272,256]{2,1,0:T(8,128)(2,1)S(1)}, u32[]{:S(2)}, u32[]{:S(2)}) %collective-permute-start.6) | collective-permute-done | bytes 139296 | tf_op jit(solution)/shard_map/ppermute | solution.py:270
  19.9 1.1 %shard_map.66 = f32[1,2,256,256]{3,2,1,0:T(8,128)} custom-call(f32[1,2,256,256]{3,2,1,0:T(8,128)S(1)} %shard_map.65.refs_0_, bf16[1,512,1024]{2,1,0:T(8,128)(2,1)S(1)} %get-tuple-element.25.refs_1_, s16[1,272,256]{2,1,0:T(8,128)(2,1)S(1)} %collective-permute-done.6.refs_2_), custom_call_target="tpu_custom_call" | custom-call | tf_op jit(solution)/shard_map/pallas_call | solution.py:244
  (1 shorter events, 0.0 us)
Async XLA Ops:
  0.6 3.1 %copy-start = (bf16[2,1,1,256,1,1,256]{6,3,5,4,2,1,0:T(8,128)(2,1)S(1)}, bf16[2,1,1,256,1,1,256]{6,3,5,4,2,1,0:T(8,128)(2,1)}, u32[]{:S(2)}) copy-start(bf16[2,1,1,256,1,1,256]{6,3,5,4,2,1,0:T(8,128)(2,1)} %param.4) | copy-start | bytes 786436
  0.6 3.1 %copy-start.2 = (s32[4,4,128]{2,1,0:T(4,128)S(1)}, s32[4,4,128]{2,1,0:T(4,128)}, u32[]{:S(2)}) copy-start(s32[4,4,128]{2,1,0:T(4,128)} %row_lists.1) | copy-start | bytes 24580
  0.7 7.8 %collective-permute-start = (bf16[1,2,1,128,256]{4,3,2,1,0:T(8,128)(2,1)}, bf16[1,2,1,128,256]{4,3,2,1,0:T(8,128)(2,1)S(1)}, u32[]{:S(2)}, u32[]{:S(2)}) collective-permute-start(bf16[1,2,1,128,256]{4,3,2,1,0:T(8,128)(2,1)} %bitcast.9), channel_id=1, source_target_pairs={{0,8},{4,12},{8,0},{12,4},{1,9},{5,13},{9,1},{13,5},{2,10},{6,14},... | collective-permute-start | bytes 393224 | tf_op jit(solution)/shard_map/ppermute | solution.py:270
  4.2 7.4 %collective-permute-start.1 = (bf16[1,2,128,128]{3,2,1,0:T(8,128)(2,1)S(1)}, bf16[1,2,128,128]{3,2,1,0:T(8,128)(2,1)S(1)}, u32[]{:S(2)}, u32[]{:S(2)}) collective-permute-start(bf16[1,2,128,128]{3,2,1,0:T(8,128)(2,1)S(1)} %get-tuple-element.24), channel_id=1, source_target_pairs={{0,2},{1,3},{2,0},{3,1},{4,6},{5,7},{6,4},{7,5},{8,10},{9,11},{10,... | collective-permute-start | bytes 196616 | tf_op jit(solution)/shard_map/ppermute | solution.py:290
  6.8 6.2 %collective-permute-start.2 = (bf16[1,2,128,128]{3,2,1,0:T(8,128)(2,1)S(1)}, bf16[1,2,128,128]{3,2,1,0:T(8,128)(2,1)S(1)}, u32[]{:S(2)}, u32[]{:S(2)}) collective-permute-start(bf16[1,2,128,128]{3,2,1,0:T(8,128)(2,1)S(1)} %get-tuple-element.26), channel_id=1, source_target_pairs={{0,3},{1,2},{2,1},{3,0},{4,7},{5,6},{6,5},{7,4},{8,11},{9,10},{10,... | collective-permute-start | bytes 196616 | tf_op jit(solution)/shard_map/ppermute | solution.py:290
  8.2 5.0 %collective-permute-start.3 = (bf16[1,2,128,128]{3,2,1,0:T(8,128)(2,1)S(1)}, bf16[1,2,128,128]{3,2,1,0:T(8,128)(2,1)S(1)}, u32[]{:S(2)}, u32[]{:S(2)}) collective-permute-start(bf16[1,2,128,128]{3,2,1,0:T(8,128)(2,1)S(1)} %get-tuple-element.27), channel_id=1, source_target_pairs={{0,1},{1,0},{2,3},{3,2},{4,5},{5,4},{6,7},{7,6},{8,9},{9,8},{10,11... | collective-permute-start | bytes 196616 | tf_op jit(solution)/shard_map/ppermute | solution.py:290
  13.2 1.2 %copy-start.1 = (f32[1,2,256,256]{3,2,1,0:T(8,128)S(1)}, f32[1,2,256,256]{3,2,1,0:T(8,128)}, u32[]{:S(2)}) copy-start(f32[1,2,256,256]{3,2,1,0:T(8,128)} %refs_0_.1) | copy-start | bytes 1572868
  13.5 5.1 %collective-permute-start.4 = (s16[1,272,256]{2,1,0:T(8,128)(2,1)S(1)}, s16[1,272,256]{2,1,0:T(8,128)(2,1)S(1)}, u32[]{:S(2)}, u32[]{:S(2)}) collective-permute-start(s16[1,272,256]{2,1,0:T(8,128)(2,1)S(1)} %get-tuple-element.34), channel_id=1, source_target_pairs={{0,8},{4,12},{8,0},{12,4},{1,9},{5,13},{9,1},{13,5},{2,10},{6,14},... | collective-permute-start | bytes 417800 | tf_op jit(solution)/shard_map/ppermute | solution.py:270
  15.3 3.2 %collective-permute-start.5 = (f32[1,128,512]{2,1,0:T(8,128)S(1)}, f32[1,128,512]{2,1,0:T(8,128)S(1)}, u32[]{:S(2)}, u32[]{:S(2)}) collective-permute-start(f32[1,128,512]{2,1,0:T(8,128)S(1)} %get-tuple-element.36.refs_2_), channel_id=1, source_target_pairs={{0,4},{4,0},{8,12},{12,8},{1,5},{5,1},{9,13},{13,9},{2,6},{6,2},{1... | collective-permute-start | bytes 786440 | tf_op jit(solution)/shard_map/ppermute | solution.py:270
  18.6 1.4 %collective-permute-start.6 = (s16[1,272,256]{2,1,0:T(8,128)(2,1)S(1)}, s16[1,272,256]{2,1,0:T(8,128)(2,1)S(1)}, u32[]{:S(2)}, u32[]{:S(2)}) collective-permute-start(s16[1,272,256]{2,1,0:T(8,128)(2,1)S(1)} %collective-permute-done.4.refs_3_), channel_id=1, source_target_pairs={{0,4},{4,0},{8,12},{12,8},{1,5},{5,1},{9,13},{13,9},{2,6},{6,2},{1... | collective-permute-start | bytes 417800 | tf_op jit(solution)/shard_map/ppermute | solution.py:270

commit v9 on v8

--- a/solution.py
+++ b/solution.py
@@ -106,13 +106,11 @@
     return pl.ds(pl.multiple_of(block * size, size), size)
 
 
-def stack_kernel(sizes, factors, surface, row_lists, far_factor, stacked, piece, arrival):
-    copy = pltpu.make_async_copy(far_factor, stacked.at[0], arrival)
-    copy.start()
+def stack_kernel(sizes, factors, surface, row_lists, own, stacked, piece):
+    stacked[0] = own[...]
     for spot, step in enumerate(factors):
         stacked[spot + 1] = factors[step][...]
     pick(sizes, [0], surface, row_lists, [piece])
-    copy.wait()
 
 
 def product_of(sizes, node, pieces, whole_factor):
@@ -288,14 +286,14 @@
     arrived = named()
     for step in [*range(grid_cols // 2, grid_cols), *range(grid_cols // 2 - 1, 0, -1)]:
         arrived[step] = lax.ppermute(pieces[step - 1], "col", partners(grid_cols, step))
+    _, late_factor = lax.optimization_barrier((pieces[grid_cols // 2 - 1], sent_factor))
     stacked, own_piece = call(
         functools.partial(stack_kernel, sizes),
         [jax.ShapeDtypeStruct((grid_rows // 2, *own_factor.shape), narrow), piece],
         factors,
         surface,
         row_lists,
-        remote=[sent_factor],
-        scratch=[pltpu.SemaphoreType.DMA],
+        late_factor,
     )
     pairs = [[place, place + 1] for place in range(0, grid_rows, 2)]
     both = lax.all_gather(stacked, "row", axis_index_groups=pairs)

time: 21.2 us -> 21.2 us (level)
  waiting for transfers between devices: 5.42 us -> 5.91 us
  Pallas kernels: 4.5 us -> 4.02 us
    ppermute x3, waiting for transfers between devices: 1.3 us -> 1.8 us  [local(): lax.ppermute(pieces[step - 1], 'col', partners(grid_cols, step))]
    pallas_call x6, Pallas kernels: 4.02 us -> 3.54 us  [call(): pl.pallas_call(flat_kernel, out_shape=out_shape, in_specs=[VMEM] * len(fl...]
  transfers between devices with their start and end apart: 7 -> 7, of which waited for: 4 -> 4; matrix products, arithmetic and copies ran while one was open for 0% -> 0% of each run, Pallas kernels for 15% -> 13%
where the time goes in v9:
time: 21.2 us; the launch traced here: 21 us
  starting transfers between devices  8.19 us (39%)
  waiting for transfers between devices  5.91 us (28%)
  Pallas kernels  4.02 us (19%)
  blocking collectives  2.18 us (10%)
  between operations  0.7 us (3%)
    ppermute x3, starting transfers between devices, local(): lax.ppermute(pieces[step - 1], 'col', partners(grid_cols, step))  4.24 us
    ppermute x4, waiting for transfers between devices, over_rows(): return lax.ppermute(block, 'row', partners(grid_rows, step))  4.11 us
    ppermute x4, starting transfers between devices, over_rows(): return lax.ppermute(block, 'row', partners(grid_rows, step))  3.95 us
    pallas_call x6, Pallas kernels, call(): pl.pallas_call(flat_kernel, out_shape=out_shape, in_specs=[VMEM] * len(fl...  3.54 us
    all_gather x1, blocking collectives, local(): both = lax.all_gather(stacked, 'row', axis_index_groups=pairs)  2.18 us
    ppermute x3, waiting for transfers between devices, local(): lax.ppermute(pieces[step - 1], 'col', partners(grid_cols, step))  1.8 us
    pallas_call x1, Pallas kernels, local(): pl.pallas_call(functools.partial(pick_kernel, sizes), out_shape=[piece] *...  0.48 us
  transfers between devices with their start and end apart: 7, of which 4 were waited for; matrix products, arithmetic and copies ran while one was open for 0% of the time, Pallas kernels for 13%

profile of v9, /device:TPU:0, one launch (start us, length us, event | category | flops | bytes accessed | tf_op | source)
XLA Modules:
  0.0 21.0 jit_solution(13029321082879644121)
XLA Ops:
  0.6 0.0 copy-start
  0.6 0.0 copy-start.3
  0.7 3.0 %collective-permute-start = (bf16[1,2,1,128,256]{4,3,2,1,0:T(8,128)(2,1)}, bf16[1,2,1,128,256]{4,3,2,1,0:T(8,128)(2,1)S(1)}, u32[]{:S(2)}, u32[]{:S(2)}) collective-permute-start(bf16[1,2,1,128,256]{4,3,2,1,0:T(8,128)(2,1)} %bitcast.9), channel_id=1, source_target_pairs={{0,8},{4,12},{8,0},{12,4},{1,9},{5,13},{9,1},{13,5},{2,10},{6,14},... | collective-permute-start | bytes 393224 | tf_op jit(solution)/shard_map/ppermute | solution.py:268
  3.7 0.0 copy-done
  3.7 0.0 copy-done.3
  3.7 0.0 copy-start.2
  3.7 0.5 %shard_map.60 = (bf16[1,2,128,128]{3,2,1,0:T(8,128)(2,1)S(1)}, bf16[1,2,128,128]{3,2,1,0:T(8,128)(2,1)S(1)}, bf16[1,2,128,128]{3,2,1,0:T(8,128)(2,1)S(1)}) custom-call(bf16[2,1,1,256,256]{4,3,2,1,0:T(8,128)(2,1)S(1)} %bitcast.7, s32[4,4,128]{2,1,0:T(4,128)S(1)} %copy-done.3, f32[8,128]{1,0:T(8,128)S(1)} %shard_map.59.token), custom_call_target="tpu_custom_call" | custom-call | tf_op jit(solution)/shard_map/pallas_call | solution.py:278
  4.2 2.7 %collective-permute-start.1 = (bf16[1,2,128,128]{3,2,1,0:T(8,128)(2,1)S(1)}, bf16[1,2,128,128]{3,2,1,0:T(8,128)(2,1)S(1)}, u32[]{:S(2)}, u32[]{:S(2)}) collective-permute-start(bf16[1,2,128,128]{3,2,1,0:T(8,128)(2,1)S(1)} %get-tuple-element.23), channel_id=1, source_target_pairs={{0,2},{1,3},{2,0},{3,1},{4,6},{5,7},{6,4},{7,5},{8,10},{9,11},{10,... | collective-permute-start | bytes 196616 | tf_op jit(solution)/shard_map/ppermute | solution.py:288
  6.8 1.3 %collective-permute-start.2 = (bf16[1,2,128,128]{3,2,1,0:T(8,128)(2,1)S(1)}, bf16[1,2,128,128]{3,2,1,0:T(8,128)(2,1)S(1)}, u32[]{:S(2)}, u32[]{:S(2)}) collective-permute-start(bf16[1,2,128,128]{3,2,1,0:T(8,128)(2,1)S(1)} %get-tuple-element.28), channel_id=1, source_target_pairs={{0,3},{1,2},{2,1},{3,0},{4,7},{5,6},{6,5},{7,4},{8,11},{9,10},{10,... | collective-permute-start | bytes 196616 | tf_op jit(solution)/shard_map/ppermute | solution.py:288
  8.2 0.2 %collective-permute-start.3 = (bf16[1,2,128,128]{3,2,1,0:T(8,128)(2,1)S(1)}, bf16[1,2,128,128]{3,2,1,0:T(8,128)(2,1)S(1)}, u32[]{:S(2)}, u32[]{:S(2)}) collective-permute-start(bf16[1,2,128,128]{3,2,1,0:T(8,128)(2,1)S(1)} %get-tuple-element.29), channel_id=1, source_target_pairs={{0,1},{1,0},{2,3},{3,2},{4,5},{5,4},{6,7},{7,6},{8,9},{9,8},{10,11... | collective-permute-start | bytes 196616 | tf_op jit(solution)/shard_map/ppermute | solution.py:288
  8.4 0.0 collective-permute-done.refs_0_
  8.4 0.0 copy-done.2
  8.4 0.4 %shard_map.61 = (bf16[2,1,2,1,128,256]{5,4,3,2,1,0:T(8,128)(2,1)S(1)}, bf16[1,2,128,128]{3,2,1,0:T(8,128)(2,1)S(1)}) custom-call(bf16[1,2,1,128,256]{4,3,2,1,0:T(8,128)(2,1)S(1)} %collective-permute-done.refs_0_, bf16[2,1,1,256,256]{4,3,2,1,0:T(8,128)(2,1)S(1)} %bitcast.8, s32[4,4,128]{2,1,0:T(4,128)S(1)} %copy-done.3, bf16[1,2,1,128,256]{4,3,2,1,0:T(8,128)(2,1)S(1)} %bitcast.10), custom_call_target="tpu_custom_call" | custom-call | tf_op jit(solution)/shard_map/pallas_call | solution.py:242
  8.9 2.2 %all-gather = bf16[4,1,2,1,128,256]{5,4,3,2,1,0:T(8,128)(2,1)S(1)} all-gather(bf16[2,1,2,1,128,256]{5,4,3,2,1,0:T(8,128)(2,1)S(1)} %get-tuple-element.25), channel_id=2, replica_groups={{0,4},{8,12},{1,5},{9,13},{2,6},{10,14},{3,7},{11,15},{16,20},{24,28},{..., dimensions={0}, use_global_device_ids=true | all-gather | bytes 786432 | tf_op jit(solution)/shard_map/all_gather | solution.py:299
  11.0 0.0 collective-permute-done.1.refs_2_
  11.0 0.3 %shard_map.62 = (bf16[1,512,512]{2,1,0:T(8,128)(2,1)S(1)}, bf16[1,512,1024]{2,1,0:T(8,128)(2,1)S(1)}, f32[1,256,512]{2,1,0:T(8,128)S(1)}) custom-call(bf16[2,2,1,2,1,128,256]{6,5,4,3,2,1,0:T(8,128)(2,1)S(1)} %bitcast.6, bf16[1,2,128,128]{3,2,1,0:T(8,128)(2,1)S(1)} %get-tuple-element.26.refs_1_, bf16[1,2,128,128]{3,2,1,0:T(8,128)(2,1)S(1)} %collective-permute-done.1.refs_2_), custom_call_target="tpu_custom_call" | custom-call | tf_op jit(solution)/shard_map/pallas_call | solution.py:242
  11.4 1.7 %collective-permute-done.2.refs_0_ = bf16[1,2,128,128]{3,2,1,0:T(8,128)(2,1)S(1)} collective-permute-done((bf16[1,2,128,128]{3,2,1,0:T(8,128)(2,1)S(1)}, bf16[1,2,128,128]{3,2,1,0:T(8,128)(2,1)S(1)}, u32[]{:S(2)}, u32[]{:S(2)}) %collective-permute-start.2) | collective-permute-done | bytes 65568 | tf_op jit(solution)/shard_map/ppermute | solution.py:288
  13.1 0.1 collective-permute-done.3.refs_1_
  13.2 0.0 copy-start.1
  13.2 0.3 %shard_map.63 = (f32[1,128,512]{2,1,0:T(8,128)S(1)}, s16[1,272,256]{2,1,0:T(8,128)(2,1)S(1)}) custom-call(bf16[1,2,128,128]{3,2,1,0:T(8,128)(2,1)S(1)} %collective-permute-done.2.refs_0_, bf16[1,2,128,128]{3,2,1,0:T(8,128)(2,1)S(1)} %collective-permute-done.3.refs_1_, bf16[1,512,512]{2,1,0:T(8,128)(2,1)S(1)} %get-tuple-element.30.refs_2_, ...), custom_call_target="tpu_custom_call" | custom-call | tf_op jit(solution)/shard_map/pallas_call | solution.py:242
  13.5 0.9 %collective-permute-start.4 = (s16[1,272,256]{2,1,0:T(8,128)(2,1)S(1)}, s16[1,272,256]{2,1,0:T(8,128)(2,1)S(1)}, u32[]{:S(2)}, u32[]{:S(2)}) collective-permute-start(s16[1,272,256]{2,1,0:T(8,128)(2,1)S(1)} %get-tuple-element.36), channel_id=1, source_target_pairs={{0,8},{4,12},{8,0},{12,4},{1,9},{5,13},{9,1},{13,5},{2,10},{6,14},... | collective-permute-start | bytes 417800 | tf_op jit(solution)/shard_map/ppermute | solution.py:268
  14.4 0.0 copy-done.1
  14.4 1.0 %shard_map.64 = (f32[1,2,256,256]{3,2,1,0:T(8,128)S(1)}, f32[1,2,128,256]{3,2,1,0:T(8,128)}) custom-call(f32[1,2,256,256]{3,2,1,0:T(8,128)S(1)} %copy-done.1, bf16[1,512,1024]{2,1,0:T(8,128)(2,1)S(1)} %get-tuple-element.27.refs_1_, f32[1,128,512]{2,1,0:T(8,128)S(1)} %get-tuple-element.38.refs_2_), custom_call_target="tpu_custom_call" | custom-call | tf_op jit(solution)/shard_map/pallas_call | solution.py:242
  15.3 0.0 collective-permute-start.5
  15.3 3.2 %collective-permute-done.4.refs_3_ = s16[1,272,256]{2,1,0:T(8,128)(2,1)S(1)} collective-permute-done((s16[1,272,256]{2,1,0:T(8,128)(2,1)S(1)}, s16[1,272,256]{2,1,0:T(8,128)(2,1)S(1)}, u32[]{:S(2)}, u32[]{:S(2)}) %collective-permute-start.4) | collective-permute-done | bytes 139296 | tf_op jit(solution)/shard_map/ppermute | solution.py:268
  18.6 0.0 collective-permute-start.6
  18.6 0.0 collective-permute-done.5.refs_2_
  18.6 0.5 %shard_map.65.refs_0_ = f32[1,2,256,256]{3,2,1,0:T(8,128)S(1)} custom-call(f32[1,2,256,256]{3,2,1,0:T(8,128)S(1)} %get-tuple-element.37.refs_0_, bf16[1,512,1024]{2,1,0:T(8,128)(2,1)S(1)} %get-tuple-element.27.refs_1_, f32[1,128,512]{2,1,0:T(8,128)S(1)} %collective-permute-done.5.refs_2_, s16[1,272,256]{2,1,0:T(8,128)(2,1)S(1)} %collective-permute-done.4.refs_3_), custom_call_target="tpu_custom_call" | custom-call | tf_op jit(solution)/shard_map/pallas_call | solution.py:242
  19.1 0.9 %collective-permute-done.6.refs_2_ = s16[1,272,256]{2,1,0:T(8,128)(2,1)S(1)} collective-permute-done((s16[1,272,256]{2,1,0:T(8,128)(2,1)S(1)}, s16[1,272,256]{2,1,0:T(8,128)(2,1)S(1)}, u32[]{:S(2)}, u32[]{:S(2)}) %collective-permute-start.6) | collective-permute-done | bytes 139296 | tf_op jit(solution)/shard_map/ppermute | solution.py:268
  19.9 1.1 %shard_map.66 = f32[1,2,256,256]{3,2,1,0:T(8,128)} custom-call(f32[1,2,256,256]{3,2,1,0:T(8,128)S(1)} %shard_map.65.refs_0_, bf16[1,512,1024]{2,1,0:T(8,128)(2,1)S(1)} %get-tuple-element.27.refs_1_, s16[1,272,256]{2,1,0:T(8,128)(2,1)S(1)} %collective-permute-done.6.refs_2_), custom_call_target="tpu_custom_call" | custom-call | tf_op jit(solution)/shard_map/pallas_call | solution.py:242
  (1 shorter events, 0.0 us)
Async XLA Ops:
  0.6 3.1 %copy-start = (bf16[2,1,1,256,1,1,256]{6,3,5,4,2,1,0:T(8,128)(2,1)S(1)}, bf16[2,1,1,256,1,1,256]{6,3,5,4,2,1,0:T(8,128)(2,1)}, u32[]{:S(2)}) copy-start(bf16[2,1,1,256,1,1,256]{6,3,5,4,2,1,0:T(8,128)(2,1)} %param.4) | copy-start | bytes 786436
  0.6 3.1 %copy-start.3 = (s32[4,4,128]{2,1,0:T(4,128)S(1)}, s32[4,4,128]{2,1,0:T(4,128)}, u32[]{:S(2)}) copy-start(s32[4,4,128]{2,1,0:T(4,128)} %refs_2_.1) | copy-start | bytes 24580
  0.7 7.8 %collective-permute-start = (bf16[1,2,1,128,256]{4,3,2,1,0:T(8,128)(2,1)}, bf16[1,2,1,128,256]{4,3,2,1,0:T(8,128)(2,1)S(1)}, u32[]{:S(2)}, u32[]{:S(2)}) collective-permute-start(bf16[1,2,1,128,256]{4,3,2,1,0:T(8,128)(2,1)} %bitcast.9), channel_id=1, source_target_pairs={{0,8},{4,12},{8,0},{12,4},{1,9},{5,13},{9,1},{13,5},{2,10},{6,14},... | collective-permute-start | bytes 393224 | tf_op jit(solution)/shard_map/ppermute | solution.py:268
  3.7 4.7 %copy-start.2 = (bf16[1,2,1,1,128,256]{5,4,3,2,1,0:T(8,128)(2,1)S(1)}, bf16[1,2,1,1,128,256]{5,4,3,2,1,0:T(8,128)(2,1)}, u32[]{:S(2)}) copy-start(bf16[1,2,1,1,128,256]{5,4,3,2,1,0:T(8,128)(2,1)} %param.5) | copy-start | bytes 393220
  4.2 6.9 %collective-permute-start.1 = (bf16[1,2,128,128]{3,2,1,0:T(8,128)(2,1)S(1)}, bf16[1,2,128,128]{3,2,1,0:T(8,128)(2,1)S(1)}, u32[]{:S(2)}, u32[]{:S(2)}) collective-permute-start(bf16[1,2,128,128]{3,2,1,0:T(8,128)(2,1)S(1)} %get-tuple-element.23), channel_id=1, source_target_pairs={{0,2},{1,3},{2,0},{3,1},{4,6},{5,7},{6,4},{7,5},{8,10},{9,11},{10,... | collective-permute-start | bytes 196616 | tf_op jit(solution)/shard_map/ppermute | solution.py:288
  6.8 6.2 %collective-permute-start.2 = (bf16[1,2,128,128]{3,2,1,0:T(8,128)(2,1)S(1)}, bf16[1,2,128,128]{3,2,1,0:T(8,128)(2,1)S(1)}, u32[]{:S(2)}, u32[]{:S(2)}) collective-permute-start(bf16[1,2,128,128]{3,2,1,0:T(8,128)(2,1)S(1)} %get-tuple-element.28), channel_id=1, source_target_pairs={{0,3},{1,2},{2,1},{3,0},{4,7},{5,6},{6,5},{7,4},{8,11},{9,10},{10,... | collective-permute-start | bytes 196616 | tf_op jit(solution)/shard_map/ppermute | solution.py:288
  8.2 5.0 %collective-permute-start.3 = (bf16[1,2,128,128]{3,2,1,0:T(8,128)(2,1)S(1)}, bf16[1,2,128,128]{3,2,1,0:T(8,128)(2,1)S(1)}, u32[]{:S(2)}, u32[]{:S(2)}) collective-permute-start(bf16[1,2,128,128]{3,2,1,0:T(8,128)(2,1)S(1)} %get-tuple-element.29), channel_id=1, source_target_pairs={{0,1},{1,0},{2,3},{3,2},{4,5},{5,4},{6,7},{7,6},{8,9},{9,8},{10,11... | collective-permute-start | bytes 196616 | tf_op jit(solution)/shard_map/ppermute | solution.py:288
  13.2 1.2 %copy-start.1 = (f32[1,2,256,256]{3,2,1,0:T(8,128)S(1)}, f32[1,2,256,256]{3,2,1,0:T(8,128)}, u32[]{:S(2)}) copy-start(f32[1,2,256,256]{3,2,1,0:T(8,128)} %refs_0_.1) | copy-start | bytes 1572868
  13.5 5.1 %collective-permute-start.4 = (s16[1,272,256]{2,1,0:T(8,128)(2,1)S(1)}, s16[1,272,256]{2,1,0:T(8,128)(2,1)S(1)}, u32[]{:S(2)}, u32[]{:S(2)}) collective-permute-start(s16[1,272,256]{2,1,0:T(8,128)(2,1)S(1)} %get-tuple-element.36), channel_id=1, source_target_pairs={{0,8},{4,12},{8,0},{12,4},{1,9},{5,13},{9,1},{13,5},{2,10},{6,14},... | collective-permute-start | bytes 417800 | tf_op jit(solution)/shard_map/ppermute | solution.py:268
  15.3 3.2 %collective-permute-start.5 = (f32[1,128,512]{2,1,0:T(8,128)S(1)}, f32[1,128,512]{2,1,0:T(8,128)S(1)}, u32[]{:S(2)}, u32[]{:S(2)}) collective-permute-start(f32[1,128,512]{2,1,0:T(8,128)S(1)} %get-tuple-element.38.refs_2_), channel_id=1, source_target_pairs={{0,4},{4,0},{8,12},{12,8},{1,5},{5,1},{9,13},{13,9},{2,6},{6,2},{1... | collective-permute-start | bytes 786440 | tf_op jit(solution)/shard_map/ppermute | solution.py:268
  18.6 1.4 %collective-permute-start.6 = (s16[1,272,256]{2,1,0:T(8,128)(2,1)S(1)}, s16[1,272,256]{2,1,0:T(8,128)(2,1)S(1)}, u32[]{:S(2)}, u32[]{:S(2)}) collective-permute-start(s16[1,272,256]{2,1,0:T(8,128)(2,1)S(1)} %collective-permute-done.4.refs_3_), channel_id=1, source_target_pairs={{0,4},{4,0},{8,12},{12,8},{1,5},{5,1},{9,13},{13,9},{2,6},{6,2},{1... | collective-permute-start | bytes 417800 | tf_op jit(solution)/shard_map/ppermute | solution.py:268

commit v10 on v8

--- a/solution.py
+++ b/solution.py
@@ -328,7 +328,6 @@
         turned_factor,
         block,
     )
-    near, block = lax.optimization_barrier((near, block))
     mate = over_rows(block, 1)
     near, sent = lax.optimization_barrier((near, sent))
     forwarded = named((step + 1, over_rows(sent[step], 1)) for step in across)

time: 21.2 us -> 21.2 us (level)
  no operation moved by 1% of the time
where the time goes in v10:
time: 21.2 us; the launch traced here: 21 us
  starting transfers between devices  8.19 us (39%)
  waiting for transfers between devices  5.42 us (26%)
  Pallas kernels  4.5 us (21%)
  blocking collectives  2.18 us (10%)
  between operations  0.7 us (3%)
    ppermute x3, starting transfers between devices, local(): lax.ppermute(pieces[step - 1], 'col', partners(grid_cols, step))  4.24 us
    ppermute x4, waiting for transfers between devices, over_rows(): return lax.ppermute(block, 'row', partners(grid_rows, step))  4.12 us
    pallas_call x6, Pallas kernels, call(): pl.pallas_call(flat_kernel, out_shape=out_shape, in_specs=[VMEM] * len(fl...  4.02 us
    ppermute x4, starting transfers between devices, over_rows(): return lax.ppermute(block, 'row', partners(grid_rows, step))  3.96 us
    all_gather x1, blocking collectives, local(): both = lax.all_gather(stacked, 'row', axis_index_groups=pairs)  2.18 us
    ppermute x3, waiting for transfers between devices, local(): lax.ppermute(pieces[step - 1], 'col', partners(grid_cols, step))  1.3 us
    pallas_call x1, Pallas kernels, local(): pl.pallas_call(functools.partial(pick_kernel, sizes), out_shape=[piece] *...  0.48 us
  transfers between devices with their start and end apart: 7, of which 4 were waited for; matrix products, arithmetic and copies ran while one was open for 0% of the time, Pallas kernels for 15%

profile of v10, /device:TPU:0, one launch (start us, length us, event | category | flops | bytes accessed | tf_op | source)
XLA Modules:
  0.0 21.0 jit_solution(17267614375816023679)
XLA Ops:
  0.6 0.0 copy-start
  0.6 0.0 copy-start.2
  0.7 3.0 %collective-permute-start = (bf16[1,2,1,128,256]{4,3,2,1,0:T(8,128)(2,1)}, bf16[1,2,1,128,256]{4,3,2,1,0:T(8,128)(2,1)S(1)}, u32[]{:S(2)}, u32[]{:S(2)}) collective-permute-start(bf16[1,2,1,128,256]{4,3,2,1,0:T(8,128)(2,1)} %bitcast.9), channel_id=1, source_target_pairs={{0,8},{4,12},{8,0},{12,4},{1,9},{5,13},{9,1},{13,5},{2,10},{6,14},... | collective-permute-start | bytes 393224 | tf_op jit(solution)/shard_map/ppermute | solution.py:270
  3.7 0.0 copy-done
  3.7 0.0 copy-done.2
  3.7 0.5 %shard_map.61 = (bf16[1,2,128,128]{3,2,1,0:T(8,128)(2,1)S(1)}, bf16[1,2,128,128]{3,2,1,0:T(8,128)(2,1)S(1)}, bf16[1,2,128,128]{3,2,1,0:T(8,128)(2,1)S(1)}) custom-call(bf16[2,1,1,256,256]{4,3,2,1,0:T(8,128)(2,1)S(1)} %bitcast.7, s32[4,4,128]{2,1,0:T(4,128)S(1)} %copy-done.2, f32[8,128]{1,0:T(8,128)S(1)} %shard_map.59.token), custom_call_target="tpu_custom_call" | custom-call | tf_op jit(solution)/shard_map/pallas_call | solution.py:280
  4.2 2.7 %collective-permute-start.1 = (bf16[1,2,128,128]{3,2,1,0:T(8,128)(2,1)S(1)}, bf16[1,2,128,128]{3,2,1,0:T(8,128)(2,1)S(1)}, u32[]{:S(2)}, u32[]{:S(2)}) collective-permute-start(bf16[1,2,128,128]{3,2,1,0:T(8,128)(2,1)S(1)} %get-tuple-element.22), channel_id=1, source_target_pairs={{0,2},{1,3},{2,0},{3,1},{4,6},{5,7},{6,4},{7,5},{8,10},{9,11},{10,... | collective-permute-start | bytes 196616 | tf_op jit(solution)/shard_map/ppermute | solution.py:290
  6.8 1.3 %collective-permute-start.2 = (bf16[1,2,128,128]{3,2,1,0:T(8,128)(2,1)S(1)}, bf16[1,2,128,128]{3,2,1,0:T(8,128)(2,1)S(1)}, u32[]{:S(2)}, u32[]{:S(2)}) collective-permute-start(bf16[1,2,128,128]{3,2,1,0:T(8,128)(2,1)S(1)} %get-tuple-element.24), channel_id=1, source_target_pairs={{0,3},{1,2},{2,1},{3,0},{4,7},{5,6},{6,5},{7,4},{8,11},{9,10},{10,... | collective-permute-start | bytes 196616 | tf_op jit(solution)/shard_map/ppermute | solution.py:290
  8.2 0.2 %collective-permute-start.3 = (bf16[1,2,128,128]{3,2,1,0:T(8,128)(2,1)S(1)}, bf16[1,2,128,128]{3,2,1,0:T(8,128)(2,1)S(1)}, u32[]{:S(2)}, u32[]{:S(2)}) collective-permute-start(bf16[1,2,128,128]{3,2,1,0:T(8,128)(2,1)S(1)} %get-tuple-element.25), channel_id=1, source_target_pairs={{0,1},{1,0},{2,3},{3,2},{4,5},{5,4},{6,7},{7,6},{8,9},{9,8},{10,11... | collective-permute-start | bytes 196616 | tf_op jit(solution)/shard_map/ppermute | solution.py:290
  8.4 0.0 collective-permute-done.refs_0_
  8.4 0.9 %shard_map.60 = (bf16[2,1,2,1,128,256]{5,4,3,2,1,0:T(8,128)(2,1)S(1)}, bf16[1,2,128,128]{3,2,1,0:T(8,128)(2,1)S(1)}) custom-call(bf16[1,2,1,128,256]{4,3,2,1,0:T(8,128)(2,1)S(1)} %collective-permute-done.refs_0_, bf16[2,1,1,256,256]{4,3,2,1,0:T(8,128)(2,1)S(1)} %bitcast.8, s32[4,4,128]{2,1,0:T(4,128)S(1)} %copy-done.2, bf16[1,2,1,128,256]{4,3,2,1,0:T(8,128)(2,1)} %bitcast.10), custom_call_target="tpu_custom_call" | custom-call | tf_op jit(solution)/shard_map/pallas_call | solution.py:244
  9.4 2.2 %all-gather = bf16[4,1,2,1,128,256]{5,4,3,2,1,0:T(8,128)(2,1)S(1)} all-gather(bf16[2,1,2,1,128,256]{5,4,3,2,1,0:T(8,128)(2,1)S(1)} %get-tuple-element.19), channel_id=2, replica_groups={{0,4},{8,12},{1,5},{9,13},{2,6},{10,14},{3,7},{11,15},{16,20},{24,28},{..., dimensions={0}, use_global_device_ids=true | all-gather | bytes 786432 | tf_op jit(solution)/shard_map/all_gather | solution.py:301
  11.5 0.0 collective-permute-done.1.refs_2_
  11.5 0.3 %shard_map.62 = (bf16[1,512,512]{2,1,0:T(8,128)(2,1)S(1)}, bf16[1,512,1024]{2,1,0:T(8,128)(2,1)S(1)}, f32[1,256,512]{2,1,0:T(8,128)S(1)}) custom-call(bf16[2,2,1,2,1,128,256]{6,5,4,3,2,1,0:T(8,128)(2,1)S(1)} %bitcast.6, bf16[1,2,128,128]{3,2,1,0:T(8,128)(2,1)S(1)} %get-tuple-element.20.refs_1_, bf16[1,2,128,128]{3,2,1,0:T(8,128)(2,1)S(1)} %collective-permute-done.1.refs_2_), custom_call_target="tpu_custom_call" | custom-call | tf_op jit(solution)/shard_map/pallas_call | solution.py:244
  11.9 1.2 %collective-permute-done.2.refs_0_ = bf16[1,2,128,128]{3,2,1,0:T(8,128)(2,1)S(1)} collective-permute-done((bf16[1,2,128,128]{3,2,1,0:T(8,128)(2,1)S(1)}, bf16[1,2,128,128]{3,2,1,0:T(8,128)(2,1)S(1)}, u32[]{:S(2)}, u32[]{:S(2)}) %collective-permute-start.2) | collective-permute-done | bytes 65568 | tf_op jit(solution)/shard_map/ppermute | solution.py:290
  13.1 0.1 collective-permute-done.3.refs_1_
  13.2 0.0 copy-start.1
  13.2 0.3 %shard_map.63 = (f32[1,128,512]{2,1,0:T(8,128)S(1)}, s16[1,272,256]{2,1,0:T(8,128)(2,1)S(1)}) custom-call(bf16[1,2,128,128]{3,2,1,0:T(8,128)(2,1)S(1)} %collective-permute-done.2.refs_0_, bf16[1,2,128,128]{3,2,1,0:T(8,128)(2,1)S(1)} %collective-permute-done.3.refs_1_, bf16[1,512,512]{2,1,0:T(8,128)(2,1)S(1)} %get-tuple-element.26.refs_2_, ...), custom_call_target="tpu_custom_call" | custom-call | tf_op jit(solution)/shard_map/pallas_call | solution.py:244
  13.5 0.9 %collective-permute-start.4 = (s16[1,272,256]{2,1,0:T(8,128)(2,1)S(1)}, s16[1,272,256]{2,1,0:T(8,128)(2,1)S(1)}, u32[]{:S(2)}, u32[]{:S(2)}) collective-permute-start(s16[1,272,256]{2,1,0:T(8,128)(2,1)S(1)} %get-tuple-element.31), channel_id=1, source_target_pairs={{0,8},{4,12},{8,0},{12,4},{1,9},{5,13},{9,1},{13,5},{2,10},{6,14},... | collective-permute-start | bytes 417800 | tf_op jit(solution)/shard_map/ppermute | solution.py:270
  14.4 0.0 collective-permute-start.5
  14.4 0.0 copy-done.1
  14.4 1.0 %shard_map.64 = (f32[1,2,256,256]{3,2,1,0:T(8,128)S(1)}, f32[1,2,128,256]{3,2,1,0:T(8,128)}) custom-call(f32[1,2,256,256]{3,2,1,0:T(8,128)S(1)} %copy-done.1, bf16[1,512,1024]{2,1,0:T(8,128)(2,1)S(1)} %get-tuple-element.23.refs_1_, f32[1,128,512]{2,1,0:T(8,128)S(1)} %get-tuple-element.28.refs_2_), custom_call_target="tpu_custom_call" | custom-call | tf_op jit(solution)/shard_map/pallas_call | solution.py:244
  15.3 3.2 %collective-permute-done.4.refs_3_ = s16[1,272,256]{2,1,0:T(8,128)(2,1)S(1)} collective-permute-done((s16[1,272,256]{2,1,0:T(8,128)(2,1)S(1)}, s16[1,272,256]{2,1,0:T(8,128)(2,1)S(1)}, u32[]{:S(2)}, u32[]{:S(2)}) %collective-permute-start.4) | collective-permute-done | bytes 139296 | tf_op jit(solution)/shard_map/ppermute | solution.py:270
  18.6 0.0 collective-permute-start.6
  18.6 0.0 collective-permute-done.5.refs_2_
  18.6 0.5 %shard_map.65.refs_0_ = f32[1,2,256,256]{3,2,1,0:T(8,128)S(1)} custom-call(f32[1,2,256,256]{3,2,1,0:T(8,128)S(1)} %get-tuple-element.32.refs_0_, bf16[1,512,1024]{2,1,0:T(8,128)(2,1)S(1)} %get-tuple-element.23.refs_1_, f32[1,128,512]{2,1,0:T(8,128)S(1)} %collective-permute-done.5.refs_2_, s16[1,272,256]{2,1,0:T(8,128)(2,1)S(1)} %collective-permute-done.4.refs_3_), custom_call_target="tpu_custom_call" | custom-call | tf_op jit(solution)/shard_map/pallas_call | solution.py:244
  19.1 0.9 %collective-permute-done.6.refs_2_ = s16[1,272,256]{2,1,0:T(8,128)(2,1)S(1)} collective-permute-done((s16[1,272,256]{2,1,0:T(8,128)(2,1)S(1)}, s16[1,272,256]{2,1,0:T(8,128)(2,1)S(1)}, u32[]{:S(2)}, u32[]{:S(2)}) %collective-permute-start.6) | collective-permute-done | bytes 139296 | tf_op jit(solution)/shard_map/ppermute | solution.py:270
  19.9 1.1 %shard_map.66 = f32[1,2,256,256]{3,2,1,0:T(8,128)} custom-call(f32[1,2,256,256]{3,2,1,0:T(8,128)S(1)} %shard_map.65.refs_0_, bf16[1,512,1024]{2,1,0:T(8,128)(2,1)S(1)} %get-tuple-element.23.refs_1_, s16[1,272,256]{2,1,0:T(8,128)(2,1)S(1)} %collective-permute-done.6.refs_2_), custom_call_target="tpu_custom_call" | custom-call | tf_op jit(solution)/shard_map/pallas_call | solution.py:244
  (1 shorter events, 0.0 us)
Async XLA Ops:
  0.6 3.1 %copy-start = (bf16[2,1,1,256,1,1,256]{6,3,5,4,2,1,0:T(8,128)(2,1)S(1)}, bf16[2,1,1,256,1,1,256]{6,3,5,4,2,1,0:T(8,128)(2,1)}, u32[]{:S(2)}) copy-start(bf16[2,1,1,256,1,1,256]{6,3,5,4,2,1,0:T(8,128)(2,1)} %param.4) | copy-start | bytes 786436
  0.6 3.1 %copy-start.2 = (s32[4,4,128]{2,1,0:T(4,128)S(1)}, s32[4,4,128]{2,1,0:T(4,128)}, u32[]{:S(2)}) copy-start(s32[4,4,128]{2,1,0:T(4,128)} %row_lists.1) | copy-start | bytes 24580
  0.7 7.8 %collective-permute-start = (bf16[1,2,1,128,256]{4,3,2,1,0:T(8,128)(2,1)}, bf16[1,2,1,128,256]{4,3,2,1,0:T(8,128)(2,1)S(1)}, u32[]{:S(2)}, u32[]{:S(2)}) collective-permute-start(bf16[1,2,1,128,256]{4,3,2,1,0:T(8,128)(2,1)} %bitcast.9), channel_id=1, source_target_pairs={{0,8},{4,12},{8,0},{12,4},{1,9},{5,13},{9,1},{13,5},{2,10},{6,14},... | collective-permute-start | bytes 393224 | tf_op jit(solution)/shard_map/ppermute | solution.py:270
  4.2 7.4 %collective-permute-start.1 = (bf16[1,2,128,128]{3,2,1,0:T(8,128)(2,1)S(1)}, bf16[1,2,128,128]{3,2,1,0:T(8,128)(2,1)S(1)}, u32[]{:S(2)}, u32[]{:S(2)}) collective-permute-start(bf16[1,2,128,128]{3,2,1,0:T(8,128)(2,1)S(1)} %get-tuple-element.22), channel_id=1, source_target_pairs={{0,2},{1,3},{2,0},{3,1},{4,6},{5,7},{6,4},{7,5},{8,10},{9,11},{10,... | collective-permute-start | bytes 196616 | tf_op jit(solution)/shard_map/ppermute | solution.py:290
  6.8 6.2 %collective-permute-start.2 = (bf16[1,2,128,128]{3,2,1,0:T(8,128)(2,1)S(1)}, bf16[1,2,128,128]{3,2,1,0:T(8,128)(2,1)S(1)}, u32[]{:S(2)}, u32[]{:S(2)}) collective-permute-start(bf16[1,2,128,128]{3,2,1,0:T(8,128)(2,1)S(1)} %get-tuple-element.24), channel_id=1, source_target_pairs={{0,3},{1,2},{2,1},{3,0},{4,7},{5,6},{6,5},{7,4},{8,11},{9,10},{10,... | collective-permute-start | bytes 196616 | tf_op jit(solution)/shard_map/ppermute | solution.py:290
  8.2 5.0 %collective-permute-start.3 = (bf16[1,2,128,128]{3,2,1,0:T(8,128)(2,1)S(1)}, bf16[1,2,128,128]{3,2,1,0:T(8,128)(2,1)S(1)}, u32[]{:S(2)}, u32[]{:S(2)}) collective-permute-start(bf16[1,2,128,128]{3,2,1,0:T(8,128)(2,1)S(1)} %get-tuple-element.25), channel_id=1, source_target_pairs={{0,1},{1,0},{2,3},{3,2},{4,5},{5,4},{6,7},{7,6},{8,9},{9,8},{10,11... | collective-permute-start | bytes 196616 | tf_op jit(solution)/shard_map/ppermute | solution.py:290
  13.2 1.2 %copy-start.1 = (f32[1,2,256,256]{3,2,1,0:T(8,128)S(1)}, f32[1,2,256,256]{3,2,1,0:T(8,128)}, u32[]{:S(2)}) copy-start(f32[1,2,256,256]{3,2,1,0:T(8,128)} %refs_0_.1) | copy-start | bytes 1572868
  13.5 5.1 %collective-permute-start.4 = (s16[1,272,256]{2,1,0:T(8,128)(2,1)S(1)}, s16[1,272,256]{2,1,0:T(8,128)(2,1)S(1)}, u32[]{:S(2)}, u32[]{:S(2)}) collective-permute-start(s16[1,272,256]{2,1,0:T(8,128)(2,1)S(1)} %get-tuple-element.31), channel_id=1, source_target_pairs={{0,8},{4,12},{8,0},{12,4},{1,9},{5,13},{9,1},{13,5},{2,10},{6,14},... | collective-permute-start | bytes 417800 | tf_op jit(solution)/shard_map/ppermute | solution.py:270
  14.4 4.2 %collective-permute-start.5 = (f32[1,128,512]{2,1,0:T(8,128)S(1)}, f32[1,128,512]{2,1,0:T(8,128)S(1)}, u32[]{:S(2)}, u32[]{:S(2)}) collective-permute-start(f32[1,128,512]{2,1,0:T(8,128)S(1)} %get-tuple-element.28.refs_2_), channel_id=1, source_target_pairs={{0,4},{4,0},{8,12},{12,8},{1,5},{5,1},{9,13},{13,9},{2,6},{6,2},{1... | collective-permute-start | bytes 786440 | tf_op jit(solution)/shard_map/ppermute | solution.py:270
  18.6 1.4 %collective-permute-start.6 = (s16[1,272,256]{2,1,0:T(8,128)(2,1)S(1)}, s16[1,272,256]{2,1,0:T(8,128)(2,1)S(1)}, u32[]{:S(2)}, u32[]{:S(2)}) collective-permute-start(s16[1,272,256]{2,1,0:T(8,128)(2,1)S(1)} %collective-permute-done.4.refs_3_), channel_id=1, source_target_pairs={{0,4},{4,0},{8,12},{12,8},{1,5},{5,1},{9,13},{13,9},{2,6},{6,2},{1... | collective-permute-start | bytes 417800 | tf_op jit(solution)/shard_map/ppermute | solution.py:270
